TPU v7x, 32 devices: a whole 2x2x4 slice. The times are simulated.
32 devices in a mesh: rep: 2 (over y), gx: 4 (over z), gy: 4 (over x, core).
Axes of the slice: x: 2, y: 2, z: 4, core: 2. Of those that a mesh axis runs over, the one named last changes fastest.
Arguments:
- normed: bfloat16 [4, 256, 8192], P(None, 'rep', ('gy', 'gx')), parts along dimension 1, may hold values from -6 to 6
- in_weight: bfloat16 [2, 8192, 16384], P(None, 'gy', 'gx'), may hold values from -0.0625 to 0.0625
- conv_weight: float32 [4, 16384], P(None, ('gx', 'gy')), may hold values from -0.8 to 0.8
- conv_bias: float32 [16384], P(('gx', 'gy')), may hold values from -0.8 to 0.8
- x_weight: bfloat16 [16384, 544], P(('gx', 'gy')), may hold values from -0.046875 to 0.046875
- dt_weight: bfloat16 [512, 16384], P(None, ('gx', 'gy')), may hold values from -0.25 to 0.25
- dt_bias: float32 [16384], P(('gx', 'gy')), may hold values from -5 to -0.5
- a_log: float32 [16, 16384], P(None, ('gx', 'gy')), may hold values from 0 to 2.77
- skip: float32 [16384], P(('gx', 'gy')), may hold values from 0.5 to 2
- conv_state: bfloat16 [3, 256, 16384], P(None, 'rep', ('gx', 'gy')), parts along dimension 1, may hold values from -6 to 6
- ssm_state: float32 [256, 16, 16384], P('rep', None, ('gx', 'gy')), parts along dimension 0, may hold values from -6 to 6
- out_weight: bfloat16 [16384, 8192], P('gx', 'gy'), may hold values from -0.046875 to 0.046875
Outputs:
- mixed: bfloat16 [4, 256, 8192], P(None, 'rep', ('gy', 'gx')), parts along dimension 1
- conv_next: bfloat16 [3, 256, 16384], P(None, 'rep', ('gx', 'gy')), parts along dimension 1
- ssm_next: float32 [256, 16, 16384], P('rep', None, ('gx', 'gy')), parts along dimension 0
There are 2 independent parts, one for each index of `rep`. A program takes and returns all parts, laid end to end along the dimension named above; an argument that names none is the same for every part. Nothing has to cross between parts.
All inputs are finite; a program needn't handle non-finite values.
Results may differ from a plain program's by a relative error of at most 0.02.
Values may be sent and summed in bfloat16 or wider, within the bound.
No kernel may reach another device: no remote copies, remote signals or barrier semaphores. Data moves between devices by JAX's collectives and lax.ppermute only.
A program may use at most 192 MiB of HBM per device.

v0:
```python
import jax
import jax.numpy as jnp
from jax import lax
from jax.sharding import PartitionSpec as P

N = 16
CONV = 4
DT = 512


def per_device(
    normed,
    in_weight,
    conv_weight,
    conv_bias,
    x_weight,
    dt_weight,
    dt_bias,
    a_log,
    skip,
    conv_state,
    ssm_state,
    out_weight,
):
    a_rate = -jnp.exp(a_log)
    conv = conv_state
    state = ssm_state
    outputs = []
    for position in range(normed.shape[0]):
        partial_value = jnp.einsum(
            "rd,hde->rhe",
            lax.all_gather(normed[position], "gx", axis=1, tiled=True),
            in_weight,
            preferred_element_type=jnp.float32,
        )
        both_halves = lax.psum_scatter(
            partial_value.astype(jnp.bfloat16), "gy", scatter_dimension=2, tiled=True
        )
        inner_input = both_halves[:, 0, :]
        gate_input = both_halves[:, 1, :]
        accum = conv_bias[None, :] + conv_weight[CONV - 1][None, :] * inner_input.astype(
            jnp.float32
        )
        for tap in range(CONV - 1):
            accum = accum + conv_weight[tap][None, :] * conv[tap].astype(jnp.float32)
        conv_out = jax.nn.silu(accum).astype(jnp.bfloat16)
        conv = jnp.concatenate([conv[1:], inner_input[None]], axis=0)
        proj = lax.psum(
            jnp.dot(conv_out, x_weight, preferred_element_type=jnp.float32), ("gx", "gy")
        )
        step_low = proj[:, :DT].astype(jnp.bfloat16)
        b_in = proj[:, DT : DT + N]
        c_out = proj[:, DT + N :]
        delta = jax.nn.softplus(
            jnp.dot(step_low, dt_weight, preferred_element_type=jnp.float32) + dt_bias[None, :]
        )
        conv_float = conv_out.astype(jnp.float32)
        state = (
            jnp.exp(delta[:, None, :] * a_rate[None, :, :]) * state
            + delta[:, None, :] * b_in[:, :, None] * conv_float[:, None, :]
        )
        result = jnp.sum(c_out[:, :, None] * state, axis=1) + skip[None, :] * conv_float
        gated = (result * jax.nn.silu(gate_input.astype(jnp.float32))).astype(jnp.bfloat16)
        out_partial = jnp.dot(
            lax.all_gather(gated, "gy", axis=1, tiled=True),
            out_weight,
            preferred_element_type=jnp.float32,
        )
        outputs.append(
            lax.psum_scatter(
                out_partial.astype(jnp.bfloat16), "gx", scatter_dimension=1, tiled=True
            )
        )
    return (jnp.stack(outputs, axis=0), conv, state)


def solution(mesh):
    return jax.shard_map(
        per_device,
        mesh=mesh,
        in_specs=(
            P(None, "rep", ("gy", "gx")),
            P(None, "gy", "gx"),
            P(None, ("gx", "gy")),
            P(("gx", "gy")),
            P(("gx", "gy"), None),
            P(None, ("gx", "gy")),
            P(("gx", "gy")),
            P(None, ("gx", "gy")),
            P(("gx", "gy")),
            P(None, "rep", ("gx", "gy")),
            P("rep", None, ("gx", "gy")),
            P("gx", "gy"),
        ),
        out_specs=(
            P(None, "rep", ("gy", "gx")),
            P(None, "rep", ("gx", "gy")),
            P("rep", None, ("gx", "gy")),
        ),
        check_vma=False,
    )
```

profile of v0, /device:TPU:0, one launch (start us, length us, event | category | flops | bytes accessed | tf_op | source)
XLA Modules:
  0.0 492.0 jit_solution(18097147612544890254)
XLA Ops:
  8.5 17.4 %all-gather = bf16[1,128,2048]{2,1,0:T(8,128)(2,1)S(1)} all-gather(bf16[1,128,512]{2,1,0:T(8,128)(2,1)S(1)} %get-tuple-element.20), channel_id=2, replica_groups=mesh['rep'=2,'gx'=4,'gy'=4] {'gx'}, dimensions={2}, use_global_device_ids=true | all-gather | bytes 655360 | tf_op jit(solution)/shard_map/all_gather | solution.py:32
  25.8 16.4 %convolution_convert_fusion.3 = bf16[128,2,4096]{2,0,1:T(8,128)(2,1)} fusion(bf16[2,2048,4096]{2,1,0:T(8,128)(2,1)} %param.13, bf16[1,128,2048]{2,1,0:T(8,128)(2,1)S(1)} %all-gather), kind=kOutput, calls=%fused_computation.11 | convolution fusion | flops 4296015872 | bytes 36175872 | tf_op jit(solution)/shard_map/rd,hde->rhe/dot_general | solution.py:30
  42.3 16.3 %all-gather.1 = bf16[1,128,2048]{2,1,0:T(8,128)(2,1)S(1)} all-gather(bf16[1,128,512]{2,1,0:T(8,128)(2,1)S(1)} %get-tuple-element.21), channel_id=3, replica_groups=mesh['rep'=2,'gx'=4,'gy'=4] {'gx'}, dimensions={2}, use_global_device_ids=true | all-gather | bytes 655360 | tf_op jit(solution)/shard_map/all_gather | solution.py:32
  58.6 16.8 %convolution_convert_fusion.2 = bf16[128,2,4096]{2,0,1:T(8,128)(2,1)} fusion(bf16[2,2048,4096]{2,1,0:T(8,128)(2,1)} %param.13, bf16[1,128,2048]{2,1,0:T(8,128)(2,1)S(1)} %all-gather.1), kind=kOutput, calls=%fused_computation.10 | convolution fusion | flops 4296015872 | bytes 36175872 | tf_op jit(solution)/shard_map/rd,hde->rhe/dot_general | solution.py:30
  75.5 15.8 %all-gather.2 = bf16[1,128,2048]{2,1,0:T(8,128)(2,1)S(1)} all-gather(bf16[1,128,512]{2,1,0:T(8,128)(2,1)S(1)} %get-tuple-element.23), channel_id=4, replica_groups=mesh['rep'=2,'gx'=4,'gy'=4] {'gx'}, dimensions={2}, use_global_device_ids=true | all-gather | bytes 655360 | tf_op jit(solution)/shard_map/all_gather | solution.py:32
  91.3 16.7 %convolution_convert_fusion.1 = bf16[128,2,4096]{2,0,1:T(8,128)(2,1)} fusion(bf16[2,2048,4096]{2,1,0:T(8,128)(2,1)} %param.13, bf16[1,128,2048]{2,1,0:T(8,128)(2,1)S(1)} %all-gather.2), kind=kOutput, calls=%fused_computation.9 | convolution fusion | flops 4296015872 | bytes 36175872 | tf_op jit(solution)/shard_map/rd,hde->rhe/dot_general | solution.py:30
  108.1 14.8 %all-gather.3 = bf16[1,128,2048]{2,1,0:T(8,128)(2,1)S(1)} all-gather(bf16[1,128,512]{2,1,0:T(8,128)(2,1)S(1)} %get-tuple-element.22), channel_id=5, replica_groups=mesh['rep'=2,'gx'=4,'gy'=4] {'gx'}, dimensions={2}, use_global_device_ids=true | all-gather | bytes 655360 | tf_op jit(solution)/shard_map/all_gather | solution.py:32
  122.9 16.9 %convolution_convert_fusion = bf16[128,2,4096]{2,0,1:T(8,128)(2,1)} fusion(bf16[2,2048,4096]{2,1,0:T(8,128)(2,1)} %param.13, bf16[1,128,2048]{2,1,0:T(8,128)(2,1)S(1)} %all-gather.3), kind=kOutput, calls=%fused_computation.8 | convolution fusion | flops 4296015872 | bytes 36175872 | tf_op jit(solution)/shard_map/rd,hde->rhe/dot_general | solution.py:30
  140.2 4.2 reduce-scatter.17.cloned.1.call-done
  144.4 34.0 %reduce-scatter.21.cloned.1.call-done = bf16[128,2,1024]{2,0,1:T(8,128)(2,1)} async-done(((bf16[128,2,4096]{2,0,1:T(8,128)(2,1)}), bf16[128,2,1024]{2,0,1:T(8,128)(2,1)}) %reduce-scatter.21.cloned.1.call-update) | async-done | bytes 524304 | tf_op jit(solution)/shard_map/reduce_scatter | solution.py:36
  191.2 88.6 %all-reduce.3.cloned.1.call-done = (f32[128,544]{0,1:T(8,128)}, f32[128,544]{0,1:T(8,128)}, f32[128,544]{0,1:T(8,128)}, f32[128,544]{0,1:T(8,128)}) async-done(((f32[128,544]{0,1:T(8,128)}, f32[128,544]{0,1:T(8,128)}, f32[128,544]{0,1:T(8,128)}, f32[128,544]{0,1:T(8,128)}), (f32[128,544]{0,1:T(8,128)}, f32[128,544]{0,1:T(8,128)}, f32[128,544]{0,1:T(8,128)}, ...) | async-done | bytes 1114128 | tf_op jit(solution)/shard_map/psum | solution.py:48
  296.9 21.1 %multiply_reduce_fusion.2 = (f32[128,1024]{1,0:T(8,128)S(1)}, f32[128,1024]{1,0:T(8,128)S(1)}, f32[128,1024]{1,0:T(8,128)S(1)}, f32[128,1024]{1,0:T(8,128)S(1)}, f32[128,16,1024]{2,1,0:T(8,128)}) fusion(f32[128,16]{1,0:T(8,128)} %copy.17, f32[128,1024]{1,0:T(8,128)} %get-tuple-element.14, f32[128,16]{1,0:T(8,128)} %copy.18, ...), kind=kLoop, calls=%fused_computation.4 | loop fusion | flops 58195968 | bytes 23199744 | tf_op jit(solution)/shard_map/reduce_sum | solution.py:62
  322.0 14.7 %all-gather.9.cloned.1.call-done = bf16[128,4096]{1,0:T(8,128)(2,1)} async-done(((bf16[128,1024]{1,0:T(8,128)(2,1)}), bf16[128,4096]{1,0:T(8,128)(2,1)}) %all-gather.9.cloned.1.call-update) | async-done | bytes 1048592 | tf_op jit(solution)/shard_map/all_gather | solution.py:65
  336.8 9.2 %convolution_convert_fusion.7 = bf16[128,2048]{1,0:T(8,128)(2,1)} fusion(bf16[128,4096]{1,0:T(8,128)(2,1)} %all-gather.9.cloned.1.call-done, bf16[4096,2048]{1,0:T(8,128)(2,1)} %param.23), kind=kOutput, calls=%fused_computation.15 | convolution fusion | flops 2147745792 | bytes 18350080 | tf_op jit(solution)/shard_map/dot_general | solution.py:64
  346.3 9.3 %all-gather.11.cloned.1.call-done = bf16[128,4096]{1,0:T(8,128)(2,1)} async-done(((bf16[128,1024]{1,0:T(8,128)(2,1)}), bf16[128,4096]{1,0:T(8,128)(2,1)}) %all-gather.11.cloned.1.call-update) | async-done | bytes 1048592 | tf_op jit(solution)/shard_map/all_gather | solution.py:65
  355.6 9.2 %convolution_convert_fusion.6 = bf16[128,2048]{1,0:T(8,128)(2,1)} fusion(bf16[128,4096]{1,0:T(8,128)(2,1)} %all-gather.11.cloned.1.call-done, bf16[4096,2048]{1,0:T(8,128)(2,1)} %param.23), kind=kOutput, calls=%fused_computation.14 | convolution fusion | flops 2147745792 | bytes 18350080 | tf_op jit(solution)/shard_map/dot_general | solution.py:64
  365.0 9.0 %all-gather.13.cloned.1.call-done = bf16[128,4096]{1,0:T(8,128)(2,1)} async-done(((bf16[128,1024]{1,0:T(8,128)(2,1)}), bf16[128,4096]{1,0:T(8,128)(2,1)}) %all-gather.13.cloned.1.call-update) | async-done | bytes 1048592 | tf_op jit(solution)/shard_map/all_gather | solution.py:65
  374.0 9.2 %convolution_convert_fusion.5 = bf16[128,2048]{1,0:T(8,128)(2,1)} fusion(bf16[128,4096]{1,0:T(8,128)(2,1)} %all-gather.13.cloned.1.call-done, bf16[4096,2048]{1,0:T(8,128)(2,1)} %param.23), kind=kOutput, calls=%fused_computation.13 | convolution fusion | flops 2147745792 | bytes 18350080 | tf_op jit(solution)/shard_map/dot_general | solution.py:64
  383.3 9.0 %all-gather.15.cloned.1.call-done = bf16[128,4096]{1,0:T(8,128)(2,1)} async-done(((bf16[128,1024]{1,0:T(8,128)(2,1)}), bf16[128,4096]{1,0:T(8,128)(2,1)}) %all-gather.15.cloned.1.call-update) | async-done | bytes 1048592 | tf_op jit(solution)/shard_map/all_gather | solution.py:65
  392.3 9.3 %convolution_convert_fusion.4 = bf16[128,2048]{1,0:T(8,128)(2,1)} fusion(bf16[128,4096]{1,0:T(8,128)(2,1)} %all-gather.15.cloned.1.call-done, bf16[4096,2048]{1,0:T(8,128)(2,1)} %param.23), kind=kOutput, calls=%fused_computation.12 | convolution fusion | flops 2147745792 | bytes 18350080 | tf_op jit(solution)/shard_map/dot_general | solution.py:64
  403.7 12.4 %reduce-scatter.11.cloned.1.call-done = bf16[128,512]{1,0:T(8,128)(2,1)} async-done(((bf16[128,2048]{1,0:T(8,128)(2,1)}), bf16[128,512]{1,0:T(8,128)(2,1)}) %reduce-scatter.11.cloned.1.call-update) | async-done | bytes 131088 | tf_op jit(solution)/shard_map/reduce_scatter | solution.py:70
  416.1 22.2 %reduce-scatter.15.cloned.1.call-done = bf16[128,512]{1,0:T(8,128)(2,1)} async-done(((bf16[128,2048]{1,0:T(8,128)(2,1)}), bf16[128,512]{1,0:T(8,128)(2,1)}) %reduce-scatter.15.cloned.1.call-update) | async-done | bytes 131088 | tf_op jit(solution)/shard_map/reduce_scatter | solution.py:70
  438.3 22.0 %reduce-scatter.19.cloned.1.call-done = bf16[128,512]{1,0:T(8,128)(2,1)} async-done(((bf16[128,2048]{1,0:T(8,128)(2,1)}), bf16[128,512]{1,0:T(8,128)(2,1)}) %reduce-scatter.19.cloned.1.call-update) | async-done | bytes 131088 | tf_op jit(solution)/shard_map/reduce_scatter | solution.py:70
  460.4 22.7 %reduce-scatter.23.cloned.1.call-done = bf16[128,512]{1,0:T(8,128)(2,1)} async-done(((bf16[128,2048]{1,0:T(8,128)(2,1)}), bf16[128,512]{1,0:T(8,128)(2,1)}) %reduce-scatter.23.cloned.1.call-update) | async-done | bytes 131088 | tf_op jit(solution)/shard_map/reduce_scatter | solution.py:70
  (88 shorter events, 40.1 us)
Async XLA Ops:
  7.2 173.2 %copy-start = (bf16[1024,544]{0,1:T(8,128)(2,1)S(1)}, bf16[1024,544]{0,1:T(8,128)(2,1)}, u32[]{:S(2)}) copy-start(bf16[1024,544]{0,1:T(8,128)(2,1)} %param.16) | copy-start | bytes 3342340
  7.2 133.0 %reduce-scatter.9.cloned.1.call-start = ((), (), s32[]{:S(2)}) async-start(), calls=%async_computation.8 | async-start | bytes 2621440 | tf_op jit(solution)/shard_map/reduce_scatter | solution.py:36
  42.3 97.9 %reduce-scatter.13.cloned.1.call-start = ((), (), s32[]{:S(2)}) async-start(), calls=%async_computation.11 | async-start | bytes 2621440 | tf_op jit(solution)/shard_map/reduce_scatter | solution.py:36
  75.4 68.9 %reduce-scatter.17.cloned.1.call-start = ((), (), s32[]{:S(2)}) async-start(), calls=%async_computation.14 | async-start | bytes 2621440 | tf_op jit(solution)/shard_map/reduce_scatter | solution.py:36
  108.0 70.3 %reduce-scatter.21.cloned.1.call-start = ((), (), s32[]{:S(2)}) async-start(), calls=%async_computation.17 | async-start | bytes 2621440 | tf_op jit(solution)/shard_map/reduce_scatter | solution.py:36
  122.9 55.5 %copy-start.2 = (bf16[3,128,1024]{2,1,0:T(8,128)(2,1)S(1)}, bf16[3,128,1024]{2,1,0:T(8,128)(2,1)}, u32[]{:S(2)}) copy-start(bf16[3,128,1024]{2,1,0:T(8,128)(2,1)} %param.21) | copy-start | bytes 2359300
  122.9 55.5 %copy-start.9 = (f32[1024]{0:T(1024)S(1)}, f32[1024]{0:T(1024)}, u32[]{:S(2)}) copy-start(f32[1024]{0:T(1024)} %param.15) | copy-start | bytes 12292
  139.8 140.0 %all-reduce.3.cloned.1.call-start = ((), (), s32[]{:S(2)}) async-start(), calls=%async_computation.20 | async-start | bytes 2228224 | tf_op jit(solution)/shard_map/psum | solution.py:48
  140.2 46.3 %copy-start.3 = (bf16[128,2,1024]{2,0,1:T(8,128)(2,1)S(1)}, bf16[128,2,1024]{2,0,1:T(8,128)(2,1)}, u32[]{:S(2)}) copy-start(bf16[128,2,1024]{2,0,1:T(8,128)(2,1)} %reduce-scatter.9.cloned.1.call-done) | copy-start | bytes 1572868
  186.4 150.4 %all-gather.9.cloned.1.call-start = ((), (), s32[]{:S(2)}) async-start(), calls=%async_computation.9 | async-start | bytes 1310720 | tf_op jit(solution)/shard_map/all_gather | solution.py:65
  296.9 21.1 %copy-start.4 = (bf16[128,2,1024]{2,0,1:T(8,128)(2,1)S(1)}, bf16[128,2,1024]{2,0,1:T(8,128)(2,1)}, u32[]{:S(2)}) copy-start(bf16[128,2,1024]{2,0,1:T(8,128)(2,1)} %reduce-scatter.13.cloned.1.call-done) | copy-start | bytes 1572868
  296.9 21.1 %copy-start.6 = (bf16[128,2,1024]{2,0,1:T(8,128)(2,1)S(1)}, bf16[128,2,1024]{2,0,1:T(8,128)(2,1)}, u32[]{:S(2)}) copy-start(bf16[128,2,1024]{2,0,1:T(8,128)(2,1)} %reduce-scatter.17.cloned.1.call-done) | copy-start | bytes 1572868
  296.9 21.1 %copy-start.8 = (bf16[128,2,1024]{2,0,1:T(8,128)(2,1)S(1)}, bf16[128,2,1024]{2,0,1:T(8,128)(2,1)}, u32[]{:S(2)}) copy-start(bf16[128,2,1024]{2,0,1:T(8,128)(2,1)} %reduce-scatter.21.cloned.1.call-done) | copy-start | bytes 1572868
  296.9 21.1 %copy-start.12 = (f32[1024]{0:T(1024)S(1)}, f32[1024]{0:T(1024)}, u32[]{:S(2)}) copy-start(f32[1024]{0:T(1024)} %param.20) | copy-start | bytes 12292
  319.7 35.9 %all-gather.11.cloned.1.call-start = ((), (), s32[]{:S(2)}) async-start(), calls=%async_computation.12 | async-start | bytes 1310720 | tf_op jit(solution)/shard_map/all_gather | solution.py:65
  320.5 53.5 %all-gather.13.cloned.1.call-start = ((), (), s32[]{:S(2)}) async-start(), calls=%async_computation.15 | async-start | bytes 1310720 | tf_op jit(solution)/shard_map/all_gather | solution.py:65
  321.2 71.1 %all-gather.15.cloned.1.call-start = ((), (), s32[]{:S(2)}) async-start(), calls=%async_computation.18 | async-start | bytes 1310720 | tf_op jit(solution)/shard_map/all_gather | solution.py:65
  322.0 94.1 %reduce-scatter.11.cloned.1.call-start = ((), (), s32[]{:S(2)}) async-start(), calls=%async_computation.10 | async-start | bytes 655360 | tf_op jit(solution)/shard_map/reduce_scatter | solution.py:70
  346.0 92.3 %reduce-scatter.15.cloned.1.call-start = ((), (), s32[]{:S(2)}) async-start(), calls=%async_computation.13 | async-start | bytes 655360 | tf_op jit(solution)/shard_map/reduce_scatter | solution.py:70
  364.9 95.4 %reduce-scatter.19.cloned.1.call-start = ((), (), s32[]{:S(2)}) async-start(), calls=%async_computation.16 | async-start | bytes 655360 | tf_op jit(solution)/shard_map/reduce_scatter | solution.py:70
  383.2 99.9 %reduce-scatter.23.cloned.1.call-start = ((), (), s32[]{:S(2)}) async-start(), calls=%async_computation.19 | async-start | bytes 655360 | tf_op jit(solution)/shard_map/reduce_scatter | solution.py:70
  383.3 19.4 %copy-start.5 = (bf16[128,2,1024]{2,0,1:T(8,128)(2,1)S(1)}, bf16[128,2,1024]{2,0,1:T(8,128)(2,1)}, u32[]{:S(2)}) copy-start(bf16[128,2,1024]{2,0,1:T(8,128)(2,1)} %reduce-scatter.13.cloned.1.call-done) | copy-start | bytes 1572868
  383.3 19.4 %slice-start = ((bf16[3,128,1024]{2,1,0:T(8,128)(2,1)}), bf16[2,128,1024]{2,1,0:T(8,128)(2,1)S(1)}, s32[]{:S(2)}) async-start(bf16[3,128,1024]{2,1,0:T(8,128)(2,1)} %param.21), calls=%async_computation.21 | async-start | bytes 1048576 | tf_op jit(solution)/shard_map/slice | solution.py:47
  392.3 92.8 %copy-start.1 = (bf16[1024,544]{0,1:T(8,128)(2,1)S(1)}, bf16[1024,544]{0,1:T(8,128)(2,1)}, u32[]{:S(2)}) copy-start(bf16[1024,544]{0,1:T(8,128)(2,1)} %param.16) | copy-start | bytes 3342340
  (3 other events, 53.7 us)
Sparse Core Ops, SparseCore 0:
  42.4 33.2 reduce-scatter.8
  78.9 31.4 reduce-scatter.12
  112.9 31.4 reduce-scatter.16
  146.9 31.4 reduce-scatter.20
  186.5 93.2 all-reduce.2
  319.9 16.8 all-gather.8
  338.9 16.7 all-gather.10
  357.2 16.7 all-gather.12
  375.5 16.7 all-gather.14
  394.4 21.6 reduce-scatter.10
  418.4 19.8 reduce-scatter.14
  440.4 19.8 reduce-scatter.18
  463.2 19.8 reduce-scatter.22
where the time goes:
time: 500 us; the launch traced here: 492 us
  waiting for transfers between devices  250 us (50%)
  matrix products  119 us (24%)
  blocking collectives  64.2 us (13%)
  other arithmetic  33.7 us (7%)
  between operations  14.6 us (3%)
  local copies, waits for them, and re-layouts  8.94 us (2%)
    psum x1, waiting for transfers between devices, per_device(): lax.psum(jnp.dot(conv_out, x_weight, preferred_element_type=jnp.float32),...  88.6 us
    reduce_scatter x4, waiting for transfers between devices, per_device(): lax.psum_scatter(out_partial.astype(jnp.bfloat16), 'gx', scatter_dimensio...  79.4 us
    dot_general x4, matrix products, per_device(): jnp.einsum('rd,hde->rhe', lax.all_gather(normed[position], 'gx', axis=1,...  66.8 us
    all_gather x4, blocking collectives, per_device(): lax.all_gather(normed[position], 'gx', axis=1, tiled=True)  64.2 us
    all_gather x4, waiting for transfers between devices, per_device(): lax.all_gather(gated, 'gy', axis=1, tiled=True)  42.1 us
    reduce_scatter x4, waiting for transfers between devices, per_device(): lax.psum_scatter(partial_value.astype(jnp.bfloat16), 'gy', scatter_dimens...  38.2 us
    dot_general x4, matrix products, per_device(): jnp.dot(lax.all_gather(gated, 'gy', axis=1, tiled=True), out_weight, pref...  37 us
    reduce_sum x1, other arithmetic, per_device(): jnp.sum(c_out[:, :, None] * state, axis=1) + skip[None, :] * conv_float  21.1 us
  transfers between devices with their start and end apart: 13, of which 11 were waited for; matrix products, arithmetic and copies ran while one was open for 19% of the time, Pallas kernels for 0%

commit v1 on v0

--- a/solution.py
+++ b/solution.py
@@ -1,11 +1,304 @@
+import functools
+
 import jax
 import jax.numpy as jnp
 from jax import lax
+from jax.experimental import pallas as pl
+from jax.experimental.pallas import tpu as pltpu
 from jax.sharding import PartitionSpec as P
 
 N = 16
 CONV = 4
 DT = 512
+CHUNKS = 2
+LOG2E = 1.4426950408889634
+BF = jnp.bfloat16
+F32 = jnp.float32
+IN_VMEM = pl.BlockSpec(memory_space=pltpu.VMEM)
+ANYWHERE = pl.BlockSpec(memory_space=pl.ANY)
+SCALARS = pl.BlockSpec(memory_space=pltpu.SMEM)
+
+
+def _params(mib):
+    return pltpu.CompilerParams(vmem_limit_bytes=mib * 1024 * 1024)
+
+
+def _load_kernel(half, source, _, target, sem):
+    copy = pltpu.make_async_copy(source if half is None else source.at[half], target, sem)
+    copy.start()
+    copy.wait()
+
+
+def load(weight, half, after):
+    return pl.pallas_call(
+        functools.partial(_load_kernel, half),
+        out_shape=jax.ShapeDtypeStruct(weight.shape[-2:], weight.dtype),
+        in_specs=[ANYWHERE] * 2,
+        out_specs=IN_VMEM,
+        scratch_shapes=[pltpu.SemaphoreType.DMA],
+        compiler_params=_params(8),
+        name="load",
+    )(weight, after)
+
+
+def _in_kernel(sibling, place, *refs):
+    *pieces, weight, _, out = refs
+    depth = pieces[0].shape[1]
+    channels = out.shape[2]
+    core = jnp.bitwise_xor(jnp.bitwise_and(place[1], 1), sibling)
+    for i in range(2):
+        chip = jnp.bitwise_xor(jnp.right_shift(place[1], 1), 1 - i)
+        columns = pl.ds(pl.multiple_of((chip * 2 + core) * channels, channels), channels)
+        total = None
+        for k, piece in enumerate(pieces):
+            start = pl.multiple_of(jnp.bitwise_xor(place[0], k) * depth, depth)
+            part = jnp.dot(
+                piece[...], weight[pl.ds(start, depth), columns], preferred_element_type=F32
+            )
+            total = part if total is None else total + part
+        out[i] = total.astype(out.dtype)
+
+
+def in_proj(place, pieces, weight, sibling, after):
+    rows = pieces[0].shape[0]
+    channels = weight.shape[1] // 4
+    return pl.pallas_call(
+        functools.partial(_in_kernel, sibling),
+        out_shape=jax.ShapeDtypeStruct((2, rows, channels), BF),
+        in_specs=[SCALARS] + [IN_VMEM] * (len(pieces) + 1) + [ANYWHERE],
+        out_specs=IN_VMEM,
+        compiler_params=_params(8),
+        name="in_proj",
+    )(place, *pieces, weight, after)
+
+
+def _out_kernel(place, g0, g1, g2, g3, weight, *outs):
+    channels = g0.shape[1]
+    width = outs[0].shape[1]
+    for i, out in enumerate(outs):
+        target = jnp.bitwise_xor(place[0], 3 - i)
+        columns = pl.ds(pl.multiple_of(target * width, width), width)
+        total = None
+        for k, piece in enumerate((g0, g1, g2, g3)):
+            start = pl.multiple_of(jnp.bitwise_xor(place[1], k) * channels, channels)
+            part = jnp.dot(
+                piece[...], weight[pl.ds(start, channels), columns], preferred_element_type=F32
+            )
+            total = part if total is None else total + part
+        out[...] = total.astype(out.dtype)
+
+
+def out_proj(place, pieces, out_weight):
+    rows = pieces[0].shape[0]
+    width = out_weight.shape[1] // 4
+    return pl.pallas_call(
+        _out_kernel,
+        out_shape=[jax.ShapeDtypeStruct((rows, width), BF)] * 4,
+        in_specs=[SCALARS] + [IN_VMEM] * 5,
+        out_specs=[IN_VMEM] * 4,
+        compiler_params=_params(8),
+        name="out_proj",
+    )(place, *pieces, out_weight)
+
+
+def _ssm_kernel(
+    steps, low, bc, conv_out, gate, dt_weight, dt_bias, skip, a_log, state, _, new_state, gated,
+    delta, conv, result, spread
+):
+    batch = low.shape[0] // steps
+    width = gate.shape[1]
+
+    @pl.when(pl.program_id(0) == 0)
+    def _():
+        for group in range(steps * batch // 8):
+            some = bc[group * 8 : group * 8 + 8, :]
+            for n in range(2 * N):
+                spread[group * 2 * N + n] = jnp.broadcast_to(some[:, n : n + 1], (8, width))
+
+    delta[...] = jax.nn.softplus(
+        jnp.dot(low[...], dt_weight[...], preferred_element_type=F32) + dt_bias[...]
+    )
+    conv[...] = conv_out[...].astype(F32)
+    rate = jnp.exp(a_log[...]) * (-LOG2E)
+
+    def rows_of(block, carry):
+        first = pl.multiple_of(block * 8, 8)
+        d, dx, acc = [], [], []
+        for t in range(steps):
+            here = pl.ds(t * batch + first, 8)
+            d.append(delta[here, :])
+            dx.append(d[t] * conv[here, :])
+            acc.append(None)
+        for n in range(N):
+            rows = pl.ds(first * N + n, 8, stride=N)
+            s = state[rows, :]
+            a = jnp.broadcast_to(rate[n : n + 1, :], (8, width))
+            for t in range(steps):
+                group = (t * (batch // 8) + block) * 2 * N
+                s = jnp.exp2(d[t] * a) * s + dx[t] * spread[group + n]
+                y = spread[group + N + n] * s
+                acc[t] = y if acc[t] is None else acc[t] + y
+            new_state[rows, :] = s
+        for t in range(steps):
+            result[pl.ds(t * batch + first, 8), :] = acc[t]
+        return carry
+
+    lax.fori_loop(0, batch // 8, rows_of, 0)
+    gate_float = gate[...].astype(F32)
+    gated[...] = (
+        (result[...] + skip[...] * conv[...]) * (gate_float * jax.nn.sigmoid(gate_float))
+    ).astype(gated.dtype)
+
+
+def ssm(chunk, steps, low, bc, conv_out, gate, dt_weight, dt_bias, skip, a_log, state, carry, tile=128):
+    rows, channels = conv_out.shape
+    tile = min(tile, channels)
+    batch = rows // steps
+    kernel = functools.partial(_ssm_kernel, steps)
+    state_spec = pl.BlockSpec((batch * N, tile), lambda j: (chunk, j))
+    column = lambda count: pl.BlockSpec((count, tile), lambda j: (0, j))
+    whole = lambda array: pl.BlockSpec(array.shape, lambda j: (0, 0))
+    args = [low, bc, conv_out, gate, dt_weight, dt_bias, skip, a_log, state]
+    in_specs = [
+        whole(low), whole(bc), column(rows), column(rows), column(DT), column(1), column(1),
+        column(N), state_spec,
+    ]
+    aliases = {}
+    if carry is None:
+        kernel_fn = lambda *refs: kernel(*refs[:9], None, *refs[9:])
+    else:
+        args.append(carry)
+        in_specs.append(pl.BlockSpec(memory_space=pl.ANY))
+        aliases = {9: 0}
+        kernel_fn = kernel
+    return pl.pallas_call(
+        kernel_fn,
+        out_shape=[
+            jax.ShapeDtypeStruct(state.shape, F32),
+            jax.ShapeDtypeStruct((rows, channels), BF),
+        ],
+        grid=(channels // tile,),
+        in_specs=in_specs,
+        out_specs=[state_spec, column(rows)],
+        scratch_shapes=[pltpu.VMEM((rows, tile), F32)] * 3
+        + [pltpu.VMEM((rows // 8 * 2 * N, 8, tile), F32)],
+        input_output_aliases=aliases,
+        compiler_params=_params(10),
+        name="ssm",
+    )(*args)
+
+
+def _swap(array, axis, size, bits):
+    return lax.ppermute(array, axis, [(i, i ^ bits) for i in range(size)])
+
+
+def _core(array):
+    return _swap(array, "gy", 4, 1)
+
+
+def _chip(array):
+    return _swap(array, "gy", 4, 2)
+
+
+def _gx(array, bits):
+    return _swap(array, "gx", 4, bits)
+
+
+def _order(array, *earlier):
+    return lax.optimization_barrier((array, *earlier))[0]
+
+
+def _add(*arrays):
+    return functools.reduce(jnp.add, [a.astype(F32) for a in arrays])
+
+
+def chunked(
+    normed, in_weight, conv_weight, conv_bias, x_weight, dt_weight, dt_bias, a_log, skip,
+    conv_state, ssm_state, out_weight
+):
+    steps, batch, depth = normed.shape
+    channels = conv_bias.shape[0]
+    gy = lax.axis_index("gy")
+    place = jnp.stack([lax.axis_index("gx"), gy]).astype(jnp.int32)
+    core = gy & 1
+    flat_state = ssm_state.reshape(batch * N, channels)
+    piece = batch // CHUNKS
+    rows = steps * piece
+    chunks = range(CHUNKS)
+    cut = [slice(c * piece, (c + 1) * piece) for c in chunks]
+
+    weights = [load(in_weight, 0, place)]
+    weights.append(load(in_weight, 1, weights[0]))
+    gathered = []
+    before = None
+    for c in chunks:
+        own = normed[:, cut[c], :].reshape(rows, depth)
+        if before is not None:
+            own = _order(own, before)
+        two = _gx(own, 2)
+        one = _gx(own, 1)
+        relay = _order(two, weights[c])
+        gathered.append((own, one, two, _gx(relay, 1)))
+        before = relay
+
+    arrived = {}
+    after = weights[1]
+    for half in range(2):
+        for c in chunks:
+            pieces = (_order(gathered[c][0], after),) + gathered[c][1:]
+            away = in_proj(place, pieces, weights[half], 1, after)
+            near = _core(away)
+            kept = in_proj(place, pieces, weights[half], 0, away)
+            summed = _add(kept[0], near[0]).astype(BF)
+            after = summed
+            arrived[half, c] = _add(kept[1], near[1], _chip(summed)).astype(BF)
+    out_copy = load(out_weight, None, after)
+
+    carry = None
+    conv_pieces, outputs = [], []
+    for c in chunks:
+        inner = arrived[0, c].reshape(steps, piece, channels)
+        history = jnp.concatenate([conv_state[:, cut[c], :], inner], axis=0).astype(F32)
+        accum = conv_bias[None, None, :]
+        for tap in range(CONV):
+            accum = accum + conv_weight[tap][None, None, :] * history[tap : tap + steps]
+        conv_out = jax.nn.silu(accum).astype(BF).reshape(rows, channels)
+        conv_pieces.append(inner[steps - CONV + 1 :])
+
+        proj = jnp.dot(conv_out, x_weight, preferred_element_type=F32)
+        half_rows = rows // 2
+        theirs = lax.dynamic_slice_in_dim(proj, (1 - core) * half_rows, half_rows, 0)
+        mine = lax.dynamic_slice_in_dim(proj, core * half_rows, half_rows, 0)
+        mine = _add(mine, _core(theirs.astype(BF)))
+        mine = _add(mine, _chip(mine.astype(BF)))
+        mine = _add(mine, _gx(mine.astype(BF), 1))
+        mine = _add(mine, _gx(mine.astype(BF), 2)).astype(BF)
+        sibling = _core(mine)
+        both = jnp.where(
+            core == 0,
+            jnp.concatenate([mine, sibling], axis=0),
+            jnp.concatenate([sibling, mine], axis=0),
+        )
+        low = both[:, :DT]
+        b_c = both[:, DT:].astype(F32)
+
+        carry, gated = ssm(
+            c, steps, low, b_c, conv_out, arrived[1, c], dt_weight, dt_bias[None, :],
+            skip[None, :], a_log, flat_state, carry,
+        )
+        across = _chip(gated)
+        three, two, one, own = out_proj(
+            place, (gated, _core(gated), across, _core(across)), out_copy
+        )
+        joined = _add(two, _gx(three, 1)).astype(BF)
+        outputs.append(
+            _add(own, _gx(one, 1), _gx(joined, 2)).astype(BF).reshape(steps, piece, depth)
+        )
+    return (
+        jnp.concatenate(outputs, axis=1),
+        jnp.concatenate(conv_pieces, axis=1),
+        carry.reshape(ssm_state.shape),
+    )
 
 
 def per_device(
@@ -75,8 +368,9 @@
 
 
 def solution(mesh):
+    narrow = mesh.shape["gx"] == 4 and mesh.shape["gy"] == 4
     return jax.shard_map(
-        per_device,
+        chunked if narrow else per_device,
         mesh=mesh,
         in_specs=(
             P(None, "rep", ("gy", "gx")),

time: 500 us -> 216 us (0.43); the launches traced: 492 us -> 215 us
  waiting for transfers between devices: 250 us -> 77.1 us
  matrix products: 119 us -> 1.23 us
  Pallas kernels: 0 us -> 72 us
  blocking collectives: 64.2 us -> 0 us
  starting transfers between devices: 0.99 us -> 30.7 us
  other arithmetic: 33.7 us -> 10.4 us
  local copies, waits for them, and re-layouts: 8.94 us -> 22.3 us
  between operations: 14.6 us -> 1.36 us
    dot_general x16 -> x2, matrix products: 119 us -> 1.23 us  [chunked(): proj = jnp.dot(conv_out, x_weight, preferred_element_type=F32)]
    reduce_scatter x8 -> x0, waiting for transfers between devices: 118 us -> none  [the longest x4 79.4 us: per_device(): lax.psum_scatter(out_partial.astype(jnp.bfloat16), 'gx', scatter_dimensio...]
    psum x1 -> x0, waiting for transfers between devices: 88.6 us -> none  [per_device(): lax.psum(jnp.dot(conv_out, x_weight, preferred_element_type=jnp.float32),...]
    ppermute x0 -> x36, waiting for transfers between devices: none -> 77.1 us  [_swap(): return lax.ppermute(array, axis, [(i, i ^ bits) for i in range(size)])]
    pallas_call x0 -> x15, Pallas kernels: none -> 72 us  [the longest x8 25 us: in_proj(): pl.pallas_call(functools.partial(_in_kernel, sibling), out_shape=jax.Shap...]
    all_gather x4 -> x0, blocking collectives: 64.2 us -> none  [per_device(): lax.all_gather(normed[position], 'gx', axis=1, tiled=True)]
    all_gather x4 -> x0, waiting for transfers between devices: 42.1 us -> none  [per_device(): lax.all_gather(gated, 'gy', axis=1, tiled=True)]
    ppermute x0 -> x36, starting transfers between devices: none -> 30.7 us  [_swap(): return lax.ppermute(array, axis, [(i, i ^ bits) for i in range(size)])]
  transfers between devices with their start and end apart: 13 -> 36, of which waited for: 11 -> 16; matrix products, arithmetic and copies ran while one was open for 19% -> 5% of each run, Pallas kernels for 0% -> 30%
where the time goes in v1:
time: 216 us; the launch traced here: 215 us
  waiting for transfers between devices  77.1 us (36%)
  Pallas kernels  72 us (33%)
  starting transfers between devices  30.7 us (14%)
  local copies, waits for them, and re-layouts  22.3 us (10%)
  other arithmetic  10.4 us (5%)
    ppermute x36, waiting for transfers between devices, _swap(): return lax.ppermute(array, axis, [(i, i ^ bits) for i in range(size)])  77.1 us
    ppermute x36, starting transfers between devices, _swap(): return lax.ppermute(array, axis, [(i, i ^ bits) for i in range(size)])  30.7 us
    pallas_call x8, Pallas kernels, in_proj(): pl.pallas_call(functools.partial(_in_kernel, sibling), out_shape=jax.Shap...  25 us
    pallas_call x2, Pallas kernels, ssm(): pl.pallas_call(kernel_fn, out_shape=[jax.ShapeDtypeStruct(state.shape, F3...  23.8 us
    unnamed x50, local copies, waits for them, and re-layouts  20.9 us
    pallas_call x3, Pallas kernels, load(): pl.pallas_call(functools.partial(_load_kernel, half), out_shape=jax.Shape...  13.1 us
    pallas_call x2, Pallas kernels, out_proj(): pl.pallas_call(_out_kernel, out_shape=[jax.ShapeDtypeStruct((rows, width)...  10.2 us
  transfers between devices with their start and end apart: 36, of which 16 were waited for; matrix products, arithmetic and copies ran while one was open for 5% of the time, Pallas kernels for 30%

profile of v1, /device:TPU:0, one launch (start us, length us, event | category | flops | bytes accessed | tf_op | source)
XLA Modules:
  0.0 215.1 jit_solution(1701590249847210589)
XLA Ops:
  1.8 4.1 %collective-permute-start.1 = (bf16[256,512]{1,0:T(8,128)(2,1)S(1)}, bf16[256,512]{1,0:T(8,128)(2,1)S(1)}, u32[]{:S(2)}, u32[]{:S(2)}) collective-permute-start(bf16[256,512]{1,0:T(8,128)(2,1)S(1)} %bitcast.60), channel_id=1, source_target_pairs={{0,8},{4,12},{8,0},{12,4},{1,9},{5,13},{9,1},{13,5},{2,10},{6,14},... | collective-permute-start | bytes 786440 | tf_op jit(solution)/shard_map/ppermute | solution.py:192
  7.6 5.8 %load.3._.refs_4_ = bf16[2048,4096]{1,0:T(8,128)(2,1)S(1)} custom-call(bf16[2,2048,4096]{2,1,0:T(8,128)(2,1)} %source.4, s32[2]{0:T(128)S(1)} %pad_add_fusion._.place), custom_call_target="tpu_custom_call" | custom-call | tf_op jit(solution)/shard_map/load/pallas_call | solution.py:33
  13.4 4.6 %collective-permute-done.1.refs_2_ = bf16[256,512]{1,0:T(8,128)(2,1)S(1)} collective-permute-done((bf16[256,512]{1,0:T(8,128)(2,1)S(1)}, bf16[256,512]{1,0:T(8,128)(2,1)S(1)}, u32[]{:S(2)}, u32[]{:S(2)}) %collective-permute-start.1) | collective-permute-done | bytes 262176 | tf_op jit(solution)/shard_map/ppermute | solution.py:192
  18.6 6.1 %load.4.refs_5_.refs_4_ = bf16[2048,4096]{1,0:T(8,128)(2,1)S(1)} custom-call(bf16[2,2048,4096]{2,1,0:T(8,128)(2,1)} %source.4, bf16[2048,4096]{1,0:T(8,128)(2,1)S(1)} %load.3._.refs_4_), custom_call_target="tpu_custom_call" | custom-call | tf_op jit(solution)/shard_map/load/pallas_call | solution.py:33
  30.5 3.0 %collective-permute-start.11 = (bf16[256,512]{1,0:T(8,128)(2,1)S(1)}, bf16[256,512]{1,0:T(8,128)(2,1)S(1)}, u32[]{:S(2)}, u32[]{:S(2)}) collective-permute-start(bf16[256,512]{1,0:T(8,128)(2,1)S(1)} %bitcast.54), channel_id=1, source_target_pairs={{0,8},{4,12},{8,0},{12,4},{1,9},{5,13},{9,1},{13,5},{2,10},{6,14},... | collective-permute-start | bytes 786440 | tf_op jit(solution)/shard_map/ppermute | solution.py:192
  33.5 12.7 %collective-permute-done.11.refs_2_ = bf16[256,512]{1,0:T(8,128)(2,1)S(1)} collective-permute-done((bf16[256,512]{1,0:T(8,128)(2,1)S(1)}, bf16[256,512]{1,0:T(8,128)(2,1)S(1)}, u32[]{:S(2)}, u32[]{:S(2)}) %collective-permute-start.11) | collective-permute-done | bytes 262176 | tf_op jit(solution)/shard_map/ppermute | solution.py:192
  50.5 3.9 %collective-permute-done.12.refs_3_ = bf16[256,512]{1,0:T(8,128)(2,1)S(1)} collective-permute-done((bf16[256,512]{1,0:T(8,128)(2,1)S(1)}, bf16[256,512]{1,0:T(8,128)(2,1)S(1)}, u32[]{:S(2)}, u32[]{:S(2)}) %collective-permute-start.12) | collective-permute-done | bytes 262176 | tf_op jit(solution)/shard_map/ppermute | solution.py:192
  54.3 4.0 %in_proj.10.refs_5_ = bf16[2,256,1024]{2,1,0:T(8,128)(2,1)} custom-call(s32[2]{0:T(128)S(1)} %pad_add_fusion._.place, bf16[256,512]{1,0:T(8,128)(2,1)S(1)} %bitcast.56, bf16[256,512]{1,0:T(8,128)(2,1)S(1)} %collective-permute-done.10.refs_1_, bf16[256,512]{1,0:T(8,128)(2,1)S(1)} %collective-permute-done.11.refs_2_, ...), custom_call_target="tpu_custom_call" | custom-call | tf_op jit(solution)/shard_map/in_proj/pallas_call | solution.py:65
  60.0 5.8 %copy-done.2 = bf16[2048,4096]{1,0:T(8,128)(2,1)S(1)} copy-done((bf16[2048,4096]{1,0:T(8,128)(2,1)S(1)}, bf16[2048,4096]{1,0:T(8,128)(2,1)}, u32[]{:S(2)}) %copy-start.2) | copy-done | bytes 16777240
  74.3 5.8 %copy-done.4 = bf16[2048,4096]{1,0:T(8,128)(2,1)S(1)} copy-done((bf16[2048,4096]{1,0:T(8,128)(2,1)S(1)}, bf16[2048,4096]{1,0:T(8,128)(2,1)}, u32[]{:S(2)}) %copy-start.4) | copy-done | bytes 16777240
  83.2 3.0 %in_proj.13 = bf16[2,256,1024]{2,1,0:T(8,128)(2,1)S(1)} custom-call(s32[2]{0:T(128)S(1)} %pad_add_fusion._.place, bf16[256,512]{1,0:T(8,128)(2,1)S(1)} %bitcast.65, bf16[256,512]{1,0:T(8,128)(2,1)S(1)} %collective-permute-done.refs_1_, bf16[256,512]{1,0:T(8,128)(2,1)S(1)} %collective-permute-done.1.refs_2_, ...), custom_call_target="tpu_custom_call" | custom-call | tf_op jit(solution)/shard_map/in_proj/pallas_call | solution.py:65
  94.7 4.0 %collective-permute-done.25 = bf16[128,544]{1,0:T(8,128)(2,1)S(1)} collective-permute-done((bf16[128,544]{1,0:T(8,128)(2,1)S(1)}, bf16[128,544]{1,0:T(8,128)(2,1)S(1)}, u32[]{:S(2)}, u32[]{:S(2)}) %collective-permute-start.25) | collective-permute-done | bytes 139296 | tf_op jit(solution)/shard_map/ppermute | solution.py:192
  106.5 3.0 %in_proj.14.refs_5_ = bf16[2,256,1024]{2,1,0:T(8,128)(2,1)S(1)} custom-call(s32[2]{0:T(128)S(1)} %pad_add_fusion._.place, bf16[256,512]{1,0:T(8,128)(2,1)S(1)} %bitcast.58, bf16[256,512]{1,0:T(8,128)(2,1)S(1)} %collective-permute-done.10.refs_1_, bf16[256,512]{1,0:T(8,128)(2,1)S(1)} %collective-permute-done.11.refs_2_, ...), custom_call_target="tpu_custom_call" | custom-call | tf_op jit(solution)/shard_map/in_proj/pallas_call | solution.py:65
  117.1 3.7 %collective-permute-done.8 = bf16[128,544]{1,0:T(8,128)(2,1)S(1)} collective-permute-done((bf16[128,544]{1,0:T(8,128)(2,1)S(1)}, bf16[128,544]{1,0:T(8,128)(2,1)S(1)}, u32[]{:S(2)}, u32[]{:S(2)}) %collective-permute-start.8) | collective-permute-done | bytes 139296 | tf_op jit(solution)/shard_map/ppermute | solution.py:192
  123.4 3.3 %collective-permute-done.15 = bf16[256,1024]{1,0:T(8,128)(2,1)S(1)} collective-permute-done((bf16[256,1024]{1,0:T(8,128)(2,1)S(1)}, bf16[256,1024]{1,0:T(8,128)(2,1)S(1)}, u32[]{:S(2)}, u32[]{:S(2)}) %collective-permute-start.15) | collective-permute-done | bytes 524320 | tf_op jit(solution)/shard_map/ppermute | solution.py:192
  127.1 12.0 %ssm.2 = (f32[2048,1024]{1,0:T(8,128)}, bf16[256,1024]{1,0:T(8,128)(2,1)S(1)}) custom-call(bf16[256,512]{1,0:T(8,128)(2,1)S(1)} %slice.172.refs_0_, f32[256,32]{1,0:T(8,128)S(1)} %slice_convert_fusion.1.refs_1_, bf16[256,1024]{1,0:T(8,128)(2,1)S(1)} %bitcast.69, bf16[256,1024]{1,0:T(8,128)(2,1)S(1)} %fusion.10.refs_3_, bf16[512,1024]{1,0:T(8,128)(2,1)S(1)} %copy-done.6, ...), custom_call_target="tpu_custom_call" | custom-call | tf_op jit(solution)/shard_map/ssm/pallas_call | solution.py:174
  141.2 11.8 %ssm.3 = (f32[2048,1024]{1,0:T(8,128)}, bf16[256,1024]{1,0:T(8,128)(2,1)S(1)}) custom-call(bf16[256,512]{1,0:T(8,128)(2,1)S(1)} %slice.188.low, f32[256,32]{1,0:T(8,128)S(1)} %slice_convert_fusion.bc, bf16[256,1024]{1,0:T(8,128)(2,1)S(1)} %bitcast.67, bf16[256,1024]{1,0:T(8,128)(2,1)S(1)} %fusion.8.gate, ...), custom_call_target="tpu_custom_call", output_to_operand_aliasing={{0}: (9, {})} | custom-call | tf_op jit(solution)/shard_map/ssm/pallas_call | solution.py:174
  153.7 11.5 %collective-permute-done.31.g2 = bf16[256,1024]{1,0:T(8,128)(2,1)S(1)} collective-permute-done((bf16[256,1024]{1,0:T(8,128)(2,1)S(1)}, bf16[256,1024]{1,0:T(8,128)(2,1)S(1)}, u32[]{:S(2)}, u32[]{:S(2)}) %collective-permute-start.31) | collective-permute-done | bytes 524320 | tf_op jit(solution)/shard_map/ppermute | solution.py:192
  165.2 5.8 %copy-done.5 = bf16[4096,2048]{1,0:T(8,128)(2,1)S(1)} copy-done((bf16[4096,2048]{1,0:T(8,128)(2,1)S(1)}, bf16[4096,2048]{1,0:T(8,128)(2,1)}, u32[]{:S(2)}) %copy-start.5) | copy-done | bytes 16777240
  172.2 5.1 %out_proj.2 = (bf16[256,512]{1,0:T(8,128)(2,1)S(1)}, bf16[256,512]{1,0:T(8,128)(2,1)S(1)}, bf16[256,512]{1,0:T(8,128)(2,1)S(1)}, bf16[256,512]{1,0:T(8,128)(2,1)S(1)}) custom-call(s32[2]{0:T(128)S(1)} %pad_add_fusion._.place, bf16[256,1024]{1,0:T(8,128)(2,1)S(1)} %get-tuple-element.28.g0, bf16[256,1024]{1,0:T(8,128)(2,1)S(1)} %collective-permute-done.16.g1, ...), custom_call_target="tpu_custom_call" | custom-call | tf_op jit(solution)/shard_map/out_proj/pallas_call | solution.py:94
  177.6 5.1 %out_proj.3 = (bf16[256,512]{1,0:T(8,128)(2,1)S(1)}, bf16[256,512]{1,0:T(8,128)(2,1)S(1)}, bf16[256,512]{1,0:T(8,128)(2,1)S(1)}, bf16[256,512]{1,0:T(8,128)(2,1)S(1)}) custom-call(s32[2]{0:T(128)S(1)} %pad_add_fusion._.place, bf16[256,1024]{1,0:T(8,128)(2,1)S(1)} %get-tuple-element.35.g0, bf16[256,1024]{1,0:T(8,128)(2,1)S(1)} %collective-permute-done.30.g1, ...), custom_call_target="tpu_custom_call" | custom-call | tf_op jit(solution)/shard_map/out_proj/pallas_call | solution.py:94
  189.0 8.7 %collective-permute-done.34 = bf16[256,512]{1,0:T(8,128)(2,1)S(1)} collective-permute-done((bf16[256,512]{1,0:T(8,128)(2,1)S(1)}, bf16[256,512]{1,0:T(8,128)(2,1)S(1)}, u32[]{:S(2)}, u32[]{:S(2)}) %collective-permute-start.34) | collective-permute-done | bytes 262176 | tf_op jit(solution)/shard_map/ppermute | solution.py:192
  198.8 4.6 %collective-permute-done.20 = bf16[256,512]{1,0:T(8,128)(2,1)S(1)} collective-permute-done((bf16[256,512]{1,0:T(8,128)(2,1)S(1)}, bf16[256,512]{1,0:T(8,128)(2,1)S(1)}, u32[]{:S(2)}, u32[]{:S(2)}) %collective-permute-start.20) | collective-permute-done | bytes 262176 | tf_op jit(solution)/shard_map/ppermute | solution.py:192
  203.5 10.6 %collective-permute-done.33 = bf16[256,512]{1,0:T(8,128)(2,1)S(1)} collective-permute-done((bf16[256,512]{1,0:T(8,128)(2,1)S(1)}, bf16[256,512]{1,0:T(8,128)(2,1)S(1)}, u32[]{:S(2)}, u32[]{:S(2)}) %collective-permute-start.33) | collective-permute-done | bytes 262176 | tf_op jit(solution)/shard_map/ppermute | solution.py:192
  (155 shorter events, 65.9 us)
Async XLA Ops:
  1.8 16.1 %collective-permute-start.1 = (bf16[256,512]{1,0:T(8,128)(2,1)S(1)}, bf16[256,512]{1,0:T(8,128)(2,1)S(1)}, u32[]{:S(2)}, u32[]{:S(2)}) collective-permute-start(bf16[256,512]{1,0:T(8,128)(2,1)S(1)} %bitcast.60), channel_id=1, source_target_pairs={{0,8},{4,12},{8,0},{12,4},{1,9},{5,13},{9,1},{13,5},{2,10},{6,14},... | collective-permute-start | bytes 786440 | tf_op jit(solution)/shard_map/ppermute | solution.py:192
  5.9 18.8 %collective-permute-start = (bf16[256,512]{1,0:T(8,128)(2,1)S(1)}, bf16[256,512]{1,0:T(8,128)(2,1)S(1)}, u32[]{:S(2)}, u32[]{:S(2)}) collective-permute-start(bf16[256,512]{1,0:T(8,128)(2,1)S(1)} %bitcast.61), channel_id=1, source_target_pairs={{0,4},{4,0},{8,12},{12,8},{1,5},{5,1},{9,13},{13,9},{2,6},{6,2},{1... | collective-permute-start | bytes 786440 | tf_op jit(solution)/shard_map/ppermute | solution.py:192
  30.5 18.7 %collective-permute-start.3 = (bf16[2,256,1024]{2,1,0:T(8,128)(2,1)S(1)}, bf16[2,256,1024]{2,1,0:T(8,128)(2,1)S(1)}, u32[]{:S(2)}, u32[]{:S(2)}) collective-permute-start(bf16[2,256,1024]{2,1,0:T(8,128)(2,1)S(1)} %in_proj.8.refs_5_), channel_id=1, source_target_pairs={{0,1},{1,0},{2,3},{3,2},{4,5},{5,4},{6,7},{7,6},{8,9},{9,8},{10,11... | collective-permute-start | bytes 3145736 | tf_op jit(solution)/shard_map/ppermute | solution.py:192
  30.5 15.7 %collective-permute-start.11 = (bf16[256,512]{1,0:T(8,128)(2,1)S(1)}, bf16[256,512]{1,0:T(8,128)(2,1)S(1)}, u32[]{:S(2)}, u32[]{:S(2)}) collective-permute-start(bf16[256,512]{1,0:T(8,128)(2,1)S(1)} %bitcast.54), channel_id=1, source_target_pairs={{0,8},{4,12},{8,0},{12,4},{1,9},{5,13},{9,1},{13,5},{2,10},{6,14},... | collective-permute-start | bytes 786440 | tf_op jit(solution)/shard_map/ppermute | solution.py:192
  33.5 16.9 %collective-permute-start.10 = (bf16[256,512]{1,0:T(8,128)(2,1)S(1)}, bf16[256,512]{1,0:T(8,128)(2,1)S(1)}, u32[]{:S(2)}, u32[]{:S(2)}) collective-permute-start(bf16[256,512]{1,0:T(8,128)(2,1)S(1)} %bitcast.55), channel_id=1, source_target_pairs={{0,4},{4,0},{8,12},{12,8},{1,5},{5,1},{9,13},{13,9},{2,6},{6,2},{1... | collective-permute-start | bytes 786440 | tf_op jit(solution)/shard_map/ppermute | solution.py:192
  58.4 14.7 %collective-permute-start.4 = (bf16[256,1024]{1,0:T(8,128)(2,1)}, bf16[256,1024]{1,0:T(8,128)(2,1)}, u32[]{:S(2)}, u32[]{:S(2)}) collective-permute-start(bf16[256,1024]{1,0:T(8,128)(2,1)} %fusion.12.refs_5_), channel_id=1, source_target_pairs={{0,2},{1,3},{2,0},{3,1},{4,6},{5,7},{6,4},{7,5},{8,10},{9,11},{10,... | collective-permute-start | bytes 1572872 | tf_op jit(solution)/shard_map/ppermute | solution.py:192
  70.1 16.1 %collective-permute-start.23 = (bf16[256,1024]{1,0:T(8,128)(2,1)S(1)}, bf16[256,1024]{1,0:T(8,128)(2,1)S(1)}, u32[]{:S(2)}, u32[]{:S(2)}) collective-permute-start(bf16[256,1024]{1,0:T(8,128)(2,1)S(1)} %fusion.13.refs_5_), channel_id=1, source_target_pairs={{0,2},{1,3},{2,0},{3,1},{4,6},{5,7},{6,4},{7,5},{8,10},{9,11},{10,... | collective-permute-start | bytes 1572872 | tf_op jit(solution)/shard_map/ppermute | solution.py:192
  83.1 22.2 %collective-permute-start.14 = (bf16[2,256,1024]{2,1,0:T(8,128)(2,1)S(1)}, bf16[2,256,1024]{2,1,0:T(8,128)(2,1)S(1)}, u32[]{:S(2)}, u32[]{:S(2)}) collective-permute-start(bf16[2,256,1024]{2,1,0:T(8,128)(2,1)S(1)} %in_proj.12.refs_5_), channel_id=1, source_target_pairs={{0,1},{1,0},{2,3},{3,2},{4,5},{5,4},{6,7},{7,6},{8,9},{9,8},{10,11... | collective-permute-start | bytes 3145736 | tf_op jit(solution)/shard_map/ppermute | solution.py:192
  104.5 12.4 %collective-permute-start.27 = (bf16[128,544]{1,0:T(8,128)(2,1)S(1)}, bf16[128,544]{1,0:T(8,128)(2,1)S(1)}, u32[]{:S(2)}, u32[]{:S(2)}) collective-permute-start(bf16[128,544]{1,0:T(8,128)(2,1)S(1)} %fusion.19), channel_id=1, source_target_pairs={{0,8},{4,12},{8,0},{12,4},{1,9},{5,13},{9,1},{13,5},{2,10},{6,14},... | collective-permute-start | bytes 417800 | tf_op jit(solution)/shard_map/ppermute | solution.py:192
  109.5 11.6 %collective-permute-start.19 = (bf16[2,256,1024]{2,1,0:T(8,128)(2,1)S(1)}, bf16[2,256,1024]{2,1,0:T(8,128)(2,1)S(1)}, u32[]{:S(2)}, u32[]{:S(2)}) collective-permute-start(bf16[2,256,1024]{2,1,0:T(8,128)(2,1)S(1)} %in_proj.14.refs_5_), channel_id=1, source_target_pairs={{0,1},{1,0},{2,3},{3,2},{4,5},{5,4},{6,7},{7,6},{8,9},{9,8},{10,11... | collective-permute-start | bytes 3145736 | tf_op jit(solution)/shard_map/ppermute | solution.py:192
  109.7 11.1 %collective-permute-start.8 = (bf16[128,544]{1,0:T(8,128)(2,1)S(1)}, bf16[128,544]{1,0:T(8,128)(2,1)S(1)}, u32[]{:S(2)}, u32[]{:S(2)}) collective-permute-start(bf16[128,544]{1,0:T(8,128)(2,1)S(1)} %fusion.18), channel_id=1, source_target_pairs={{0,8},{4,12},{8,0},{12,4},{1,9},{5,13},{9,1},{13,5},{2,10},{6,14},... | collective-permute-start | bytes 417800 | tf_op jit(solution)/shard_map/ppermute | solution.py:192
  112.0 14.7 %collective-permute-start.15 = (bf16[256,1024]{1,0:T(8,128)(2,1)S(1)}, bf16[256,1024]{1,0:T(8,128)(2,1)S(1)}, u32[]{:S(2)}, u32[]{:S(2)}) collective-permute-start(bf16[256,1024]{1,0:T(8,128)(2,1)S(1)} %fusion.14.refs_5_), channel_id=1, source_target_pairs={{0,2},{1,3},{2,0},{3,1},{4,6},{5,7},{6,4},{7,5},{8,10},{9,11},{10,... | collective-permute-start | bytes 1572872 | tf_op jit(solution)/shard_map/ppermute | solution.py:192
  121.3 19.7 %collective-permute-start.29 = (bf16[256,1024]{1,0:T(8,128)(2,1)S(1)}, bf16[256,1024]{1,0:T(8,128)(2,1)S(1)}, u32[]{:S(2)}, u32[]{:S(2)}) collective-permute-start(bf16[256,1024]{1,0:T(8,128)(2,1)S(1)} %fusion.15._), channel_id=1, source_target_pairs={{0,2},{1,3},{2,0},{3,1},{4,6},{5,7},{6,4},{7,5},{8,10},{9,11},{10,... | collective-permute-start | bytes 1572872 | tf_op jit(solution)/shard_map/ppermute | solution.py:192
  139.1 14.1 %collective-permute-start.17 = (bf16[256,1024]{1,0:T(8,128)(2,1)S(1)}, bf16[256,1024]{1,0:T(8,128)(2,1)S(1)}, u32[]{:S(2)}, u32[]{:S(2)}) collective-permute-start(bf16[256,1024]{1,0:T(8,128)(2,1)S(1)} %get-tuple-element.28.g0), channel_id=1, source_target_pairs={{0,2},{1,3},{2,0},{3,1},{4,6},{5,7},{6,4},{7,5},{8,10},{9,11},{10,... | collective-permute-start | bytes 1572872 | tf_op jit(solution)/shard_map/ppermute | solution.py:192
  153.0 12.2 %collective-permute-start.31 = (bf16[256,1024]{1,0:T(8,128)(2,1)S(1)}, bf16[256,1024]{1,0:T(8,128)(2,1)S(1)}, u32[]{:S(2)}, u32[]{:S(2)}) collective-permute-start(bf16[256,1024]{1,0:T(8,128)(2,1)S(1)} %get-tuple-element.35.g0), channel_id=1, source_target_pairs={{0,2},{1,3},{2,0},{3,1},{4,6},{5,7},{6,4},{7,5},{8,10},{9,11},{10,... | collective-permute-start | bytes 1572872 | tf_op jit(solution)/shard_map/ppermute | solution.py:192
  153.2 19.0 %collective-permute-start.16 = (bf16[256,1024]{1,0:T(8,128)(2,1)S(1)}, bf16[256,1024]{1,0:T(8,128)(2,1)S(1)}, u32[]{:S(2)}, u32[]{:S(2)}) collective-permute-start(bf16[256,1024]{1,0:T(8,128)(2,1)S(1)} %get-tuple-element.28.g0), channel_id=1, source_target_pairs={{0,1},{1,0},{2,3},{3,2},{4,5},{5,4},{6,7},{7,6},{8,9},{9,8},{10,11... | collective-permute-start | bytes 1572872 | tf_op jit(solution)/shard_map/ppermute | solution.py:192
  153.2 19.0 %collective-permute-start.18 = (bf16[256,1024]{1,0:T(8,128)(2,1)S(1)}, bf16[256,1024]{1,0:T(8,128)(2,1)S(1)}, u32[]{:S(2)}, u32[]{:S(2)}) collective-permute-start(bf16[256,1024]{1,0:T(8,128)(2,1)S(1)} %collective-permute-done.17.g2), channel_id=1, source_target_pairs={{0,1},{1,0},{2,3},{3,2},{4,5},{5,4},{6,7},{7,6},{8,9},{9,8},{10,11... | collective-permute-start | bytes 1572872 | tf_op jit(solution)/shard_map/ppermute | solution.py:192
  153.7 23.9 %collective-permute-start.30 = (bf16[256,1024]{1,0:T(8,128)(2,1)S(1)}, bf16[256,1024]{1,0:T(8,128)(2,1)S(1)}, u32[]{:S(2)}, u32[]{:S(2)}) collective-permute-start(bf16[256,1024]{1,0:T(8,128)(2,1)S(1)} %get-tuple-element.35.g0), channel_id=1, source_target_pairs={{0,1},{1,0},{2,3},{3,2},{4,5},{5,4},{6,7},{7,6},{8,9},{9,8},{10,11... | collective-permute-start | bytes 1572872 | tf_op jit(solution)/shard_map/ppermute | solution.py:192
  165.2 12.4 %collective-permute-start.32 = (bf16[256,1024]{1,0:T(8,128)(2,1)S(1)}, bf16[256,1024]{1,0:T(8,128)(2,1)S(1)}, u32[]{:S(2)}, u32[]{:S(2)}) collective-permute-start(bf16[256,1024]{1,0:T(8,128)(2,1)S(1)} %collective-permute-done.31.g2), channel_id=1, source_target_pairs={{0,1},{1,0},{2,3},{3,2},{4,5},{5,4},{6,7},{7,6},{8,9},{9,8},{10,11... | collective-permute-start | bytes 1572872 | tf_op jit(solution)/shard_map/ppermute | solution.py:192
  182.7 15.0 %collective-permute-start.34 = (bf16[256,512]{1,0:T(8,128)(2,1)S(1)}, bf16[256,512]{1,0:T(8,128)(2,1)S(1)}, u32[]{:S(2)}, u32[]{:S(2)}) collective-permute-start(bf16[256,512]{1,0:T(8,128)(2,1)S(1)} %get-tuple-element.39), channel_id=1, source_target_pairs={{0,4},{4,0},{8,12},{12,8},{1,5},{5,1},{9,13},{13,9},{2,6},{6,2},{1... | collective-permute-start | bytes 786440 | tf_op jit(solution)/shard_map/ppermute | solution.py:192
  184.6 18.8 %collective-permute-start.20 = (bf16[256,512]{1,0:T(8,128)(2,1)S(1)}, bf16[256,512]{1,0:T(8,128)(2,1)S(1)}, u32[]{:S(2)}, u32[]{:S(2)}) collective-permute-start(bf16[256,512]{1,0:T(8,128)(2,1)S(1)} %get-tuple-element.31), channel_id=1, source_target_pairs={{0,4},{4,0},{8,12},{12,8},{1,5},{5,1},{9,13},{13,9},{2,6},{6,2},{1... | collective-permute-start | bytes 786440 | tf_op jit(solution)/shard_map/ppermute | solution.py:192
  186.5 16.9 %collective-permute-start.22 = (bf16[256,512]{1,0:T(8,128)(2,1)S(1)}, bf16[256,512]{1,0:T(8,128)(2,1)S(1)}, u32[]{:S(2)}, u32[]{:S(2)}) collective-permute-start(bf16[256,512]{1,0:T(8,128)(2,1)S(1)} %add_convert_fusion.7), channel_id=1, source_target_pairs={{0,8},{4,12},{8,0},{12,4},{1,9},{5,13},{9,1},{13,5},{2,10},{6,14},... | collective-permute-start | bytes 786440 | tf_op jit(solution)/shard_map/ppermute | solution.py:192
  187.2 26.9 %collective-permute-start.33 = (bf16[256,512]{1,0:T(8,128)(2,1)S(1)}, bf16[256,512]{1,0:T(8,128)(2,1)S(1)}, u32[]{:S(2)}, u32[]{:S(2)}) collective-permute-start(bf16[256,512]{1,0:T(8,128)(2,1)S(1)} %get-tuple-element.37), channel_id=1, source_target_pairs={{0,4},{4,0},{8,12},{12,8},{1,5},{5,1},{9,13},{13,9},{2,6},{6,2},{1... | collective-permute-start | bytes 786440 | tf_op jit(solution)/shard_map/ppermute | solution.py:192
  197.8 16.4 %collective-permute-start.35 = (bf16[256,512]{1,0:T(8,128)(2,1)S(1)}, bf16[256,512]{1,0:T(8,128)(2,1)S(1)}, u32[]{:S(2)}, u32[]{:S(2)}) collective-permute-start(bf16[256,512]{1,0:T(8,128)(2,1)S(1)} %add_convert_fusion.5), channel_id=1, source_target_pairs={{0,8},{4,12},{8,0},{12,4},{1,9},{5,13},{9,1},{13,5},{2,10},{6,14},... | collective-permute-start | bytes 786440 | tf_op jit(solution)/shard_map/ppermute | solution.py:192
  (37 other events, 411.8 us)

commit v2 on v1

--- a/solution.py
+++ b/solution.py
@@ -16,6 +16,7 @@
 F32 = jnp.float32
 IN_VMEM = pl.BlockSpec(memory_space=pltpu.VMEM)
 ANYWHERE = pl.BlockSpec(memory_space=pl.ANY)
+IN_HBM = pl.BlockSpec(memory_space=pltpu.HBM)
 SCALARS = pl.BlockSpec(memory_space=pltpu.SMEM)
 
 
@@ -72,17 +73,28 @@
     )(place, *pieces, weight, after)
 
 
-def _out_kernel(place, g0, g1, g2, g3, weight, *outs):
+def _out_kernel(place, g0, g1, g2, g3, weight, *refs):
+    *outs, held, sems = refs
     channels = g0.shape[1]
-    width = outs[0].shape[1]
+    count, _, width = held.shape
+    copies = []
+    for i in range(count):
+        target = jnp.bitwise_xor(place[0], 3 - i)
+        copies.append(
+            pltpu.make_async_copy(
+                weight.at[:, pl.ds(pl.multiple_of(target * width, width), width)],
+                held.at[i],
+                sems.at[i],
+            )
+        )
+        copies[i].start()
     for i, out in enumerate(outs):
-        target = jnp.bitwise_xor(place[0], 3 - i)
-        columns = pl.ds(pl.multiple_of(target * width, width), width)
+        copies[i].wait()
         total = None
         for k, piece in enumerate((g0, g1, g2, g3)):
             start = pl.multiple_of(jnp.bitwise_xor(place[1], k) * channels, channels)
             part = jnp.dot(
-                piece[...], weight[pl.ds(start, channels), columns], preferred_element_type=F32
+                piece[...], held[i, pl.ds(start, channels), :], preferred_element_type=F32
             )
             total = part if total is None else total + part
         out[...] = total.astype(out.dtype)
@@ -94,96 +106,123 @@
     return pl.pallas_call(
         _out_kernel,
         out_shape=[jax.ShapeDtypeStruct((rows, width), BF)] * 4,
-        in_specs=[SCALARS] + [IN_VMEM] * 5,
+        in_specs=[SCALARS] + [IN_VMEM] * 4 + [IN_HBM],
         out_specs=[IN_VMEM] * 4,
-        compiler_params=_params(8),
+        scratch_shapes=[
+            pltpu.VMEM((4, out_weight.shape[0], width), BF),
+            pltpu.SemaphoreType.DMA((4,)),
+        ],
+        compiler_params=_params(50),
         name="out_proj",
     )(place, *pieces, out_weight)
 
 
 def _ssm_kernel(
-    steps, low, bc, conv_out, gate, dt_weight, dt_bias, skip, a_log, state, _, new_state, gated,
-    delta, conv, result, spread
+    chunk, steps, low, bc, conv_out, dt_weight, dt_bias, skip, a_log, state, _, new_state, mixed,
+    held, delta, conv, result, spread, arrive, leave
 ):
     batch = low.shape[0] // steps
-    width = gate.shape[1]
-
-    @pl.when(pl.program_id(0) == 0)
-    def _():
-        for group in range(steps * batch // 8):
-            some = bc[group * 8 : group * 8 + 8, :]
-            for n in range(2 * N):
-                spread[group * 2 * N + n] = jnp.broadcast_to(some[:, n : n + 1], (8, width))
-
-    delta[...] = jax.nn.softplus(
-        jnp.dot(low[...], dt_weight[...], preferred_element_type=F32) + dt_bias[...]
-    )
-    conv[...] = conv_out[...].astype(F32)
-    rate = jnp.exp(a_log[...]) * (-LOG2E)
-
-    def rows_of(block, carry):
-        first = pl.multiple_of(block * 8, 8)
-        d, dx, acc = [], [], []
-        for t in range(steps):
-            here = pl.ds(t * batch + first, 8)
-            d.append(delta[here, :])
-            dx.append(d[t] * conv[here, :])
-            acc.append(None)
-        for n in range(N):
-            rows = pl.ds(first * N + n, 8, stride=N)
-            s = state[rows, :]
-            a = jnp.broadcast_to(rate[n : n + 1, :], (8, width))
-            for t in range(steps):
-                group = (t * (batch // 8) + block) * 2 * N
-                s = jnp.exp2(d[t] * a) * s + dx[t] * spread[group + n]
-                y = spread[group + N + n] * s
-                acc[t] = y if acc[t] is None else acc[t] + y
-            new_state[rows, :] = s
-        for t in range(steps):
-            result[pl.ds(t * batch + first, 8), :] = acc[t]
-        return carry
-
-    lax.fori_loop(0, batch // 8, rows_of, 0)
-    gate_float = gate[...].astype(F32)
-    gated[...] = (
-        (result[...] + skip[...] * conv[...]) * (gate_float * jax.nn.sigmoid(gate_float))
-    ).astype(gated.dtype)
-
-
-def ssm(chunk, steps, low, bc, conv_out, gate, dt_weight, dt_bias, skip, a_log, state, carry, tile=128):
+    count, height, lanes = held.shape
+    mine = pl.ds(chunk * height, height)
+    columns = [pl.ds(j * lanes, lanes) for j in range(count)]
+    copies = [
+        pltpu.make_async_copy(state.at[mine, columns[j]], held.at[j], arrive.at[j])
+        for j in range(count)
+    ]
+    for copy in copies:
+        copy.start()
+
+    for group in range(steps * batch // 8):
+        some = bc[group * 8 : group * 8 + 8, :]
+        for n in range(2 * N):
+            spread[group * 2 * N + n] = jnp.broadcast_to(some[:, n : n + 1], (8, lanes))
+
+    width = delta.shape[1]
+    per = width // lanes
+    outgoing = []
+    for j in range(0, count, per):
+        here = slice(j * lanes, j * lanes + width)
+        delta[...] = jax.nn.softplus(
+            jnp.dot(low[...], dt_weight[:, here], preferred_element_type=F32) + dt_bias[:, here]
+        )
+        conv[...] = conv_out[:, here].astype(F32)
+        rate = jnp.exp(a_log[:, here]) * (-LOG2E)
+        for h in range(per):
+            copies[j + h].wait()
+
+        def rows_of(block, carry, j=j, rate=rate):
+            first = pl.multiple_of(block * 8, 8)
+            pairs = [(t, h) for t in range(steps) for h in range(per)]
+            d, dx, acc = {}, {}, {}
+            for t, h in pairs:
+                place = pl.ds(t * batch + first, 8), slice(h * lanes, (h + 1) * lanes)
+                d[t, h] = delta[place]
+                dx[t, h] = d[t, h] * conv[place]
+            for n in range(N):
+                rows = pl.ds(first * N + n, 8, stride=N)
+                s = [held[j + h, rows, :] for h in range(per)]
+                a = [
+                    jnp.broadcast_to(rate[n : n + 1, h * lanes : (h + 1) * lanes], (8, lanes))
+                    for h in range(per)
+                ]
+                for t in range(steps):
+                    group = (t * (batch // 8) + block) * 2 * N
+                    b = spread[group + n]
+                    c = spread[group + N + n]
+                    for h in range(per):
+                        s[h] = jnp.exp2(d[t, h] * a[h]) * s[h] + dx[t, h] * b
+                        y = c * s[h]
+                        acc[t, h] = y if n == 0 else acc[t, h] + y
+                for h in range(per):
+                    held[j + h, rows, :] = s[h]
+            for t, h in pairs:
+                place = pl.ds(t * batch + first, 8), slice(h * lanes, (h + 1) * lanes)
+                result[place] = acc[t, h]
+            return carry
+
+        lax.fori_loop(0, batch // 8, rows_of, 0)
+        for h in range(per):
+            copy = pltpu.make_async_copy(
+                held.at[j + h], new_state.at[mine, columns[j + h]], leave.at[j + h]
+            )
+            copy.start()
+            outgoing.append(copy)
+        mixed[:, here] = result[...] + skip[:, here] * conv[...]
+    for copy in outgoing:
+        copy.wait()
+
+
+def ssm(chunk, steps, low, bc, conv_out, dt_weight, dt_bias, skip, a_log, state, carry):
     rows, channels = conv_out.shape
-    tile = min(tile, channels)
-    batch = rows // steps
-    kernel = functools.partial(_ssm_kernel, steps)
-    state_spec = pl.BlockSpec((batch * N, tile), lambda j: (chunk, j))
-    column = lambda count: pl.BlockSpec((count, tile), lambda j: (0, j))
-    whole = lambda array: pl.BlockSpec(array.shape, lambda j: (0, 0))
-    args = [low, bc, conv_out, gate, dt_weight, dt_bias, skip, a_log, state]
-    in_specs = [
-        whole(low), whole(bc), column(rows), column(rows), column(DT), column(1), column(1),
-        column(N), state_spec,
-    ]
+    height = rows // steps * N
+    lanes = 128
+    count = channels // lanes
+    width = 2 * lanes
+    kernel = functools.partial(_ssm_kernel, chunk, steps)
+    args = [low, bc, conv_out, dt_weight, dt_bias, skip, a_log, state]
+    in_specs = [IN_VMEM] * 7 + [IN_HBM]
     aliases = {}
     if carry is None:
-        kernel_fn = lambda *refs: kernel(*refs[:9], None, *refs[9:])
+        kernel_fn = lambda *refs: kernel(*refs[:8], None, *refs[8:])
     else:
         args.append(carry)
-        in_specs.append(pl.BlockSpec(memory_space=pl.ANY))
-        aliases = {9: 0}
+        in_specs.append(IN_HBM)
+        aliases = {8: 0}
         kernel_fn = kernel
     return pl.pallas_call(
         kernel_fn,
         out_shape=[
             jax.ShapeDtypeStruct(state.shape, F32),
-            jax.ShapeDtypeStruct((rows, channels), BF),
+            jax.ShapeDtypeStruct((rows, channels), F32),
         ],
-        grid=(channels // tile,),
         in_specs=in_specs,
-        out_specs=[state_spec, column(rows)],
-        scratch_shapes=[pltpu.VMEM((rows, tile), F32)] * 3
-        + [pltpu.VMEM((rows // 8 * 2 * N, 8, tile), F32)],
+        out_specs=[IN_HBM, IN_VMEM],
+        scratch_shapes=[pltpu.VMEM((count, height, lanes), F32)]
+        + [pltpu.VMEM((rows, width), F32)] * 3
+        + [pltpu.VMEM((rows // 8 * 2 * N, 8, lanes), F32)]
+        + [pltpu.SemaphoreType.DMA((count,))] * 2,
         input_output_aliases=aliases,
-        compiler_params=_params(10),
+        compiler_params=_params(16),
         name="ssm",
     )(*args)
 
@@ -227,35 +266,34 @@
     chunks = range(CHUNKS)
     cut = [slice(c * piece, (c + 1) * piece) for c in chunks]
 
-    weights = [load(in_weight, 0, place)]
-    weights.append(load(in_weight, 1, weights[0]))
     gathered = []
     before = None
+    weight = load(in_weight, 0, place)
     for c in chunks:
         own = normed[:, cut[c], :].reshape(rows, depth)
         if before is not None:
             own = _order(own, before)
         two = _gx(own, 2)
         one = _gx(own, 1)
-        relay = _order(two, weights[c])
+        relay = _order(two, weight)
         gathered.append((own, one, two, _gx(relay, 1)))
         before = relay
 
     arrived = {}
-    after = weights[1]
+    after = weight
     for half in range(2):
+        if half:
+            weight = load(in_weight, 1, after)
         for c in chunks:
             pieces = (_order(gathered[c][0], after),) + gathered[c][1:]
-            away = in_proj(place, pieces, weights[half], 1, after)
+            away = in_proj(place, pieces, weight, 1, after)
             near = _core(away)
-            kept = in_proj(place, pieces, weights[half], 0, away)
+            kept = in_proj(place, pieces, weight, 0, away)
             summed = _add(kept[0], near[0]).astype(BF)
             after = summed
             arrived[half, c] = _add(kept[1], near[1], _chip(summed)).astype(BF)
-    out_copy = load(out_weight, None, after)
-
-    carry = None
-    conv_pieces, outputs = [], []
+
+    conv_pieces, sums = [], []
     for c in chunks:
         inner = arrived[0, c].reshape(steps, piece, channels)
         history = jnp.concatenate([conv_state[:, cut[c], :], inner], axis=0).astype(F32)
@@ -282,20 +320,41 @@
         low = both[:, :DT]
         b_c = both[:, DT:].astype(F32)
 
-        carry, gated = ssm(
-            c, steps, low, b_c, conv_out, arrived[1, c], dt_weight, dt_bias[None, :],
-            skip[None, :], a_log, flat_state, carry,
-        )
-        across = _chip(gated)
-        three, two, one, own = out_proj(
-            place, (gated, _core(gated), across, _core(across)), out_copy
-        )
-        joined = _add(two, _gx(three, 1)).astype(BF)
-        outputs.append(
-            _add(own, _gx(one, 1), _gx(joined, 2)).astype(BF).reshape(steps, piece, depth)
-        )
+        sums.append((low, b_c, conv_out))
+
+    scan = functools.partial(
+        ssm, dt_weight=dt_weight, dt_bias=dt_bias[None, :], skip=skip[None, :], a_log=a_log,
+        state=flat_state,
+    )
+
+    def gate_by(c, result):
+        return (result * jax.nn.silu(arrived[1, c].astype(F32))).astype(BF)
+
+    def finish(own, first, second):
+        return _add(own, first, second).astype(BF).reshape(steps, piece, depth)
+
+    low, b_c, conv_out = sums[0]
+    carry, result = scan(0, steps, _order(low, arrived[1, 0]), b_c, conv_out, carry=None)
+    gated0 = gate_by(0, result)
+    across0 = _chip(gated0)
+    carry, result = scan(1, steps, *sums[1], carry=carry)
+    gated1 = gate_by(1, result)
+    across1 = _chip(gated1)
+    three0, two0, one0, own0 = out_proj(
+        place, (gated0, _core(gated0), across0, _core(across0)), out_weight
+    )
+    three0 = _gx(three0, 1)
+    one0 = _gx(one0, 1)
+    across1 = _order(across1, own0)
+    three1, two1, one1, own1 = out_proj(
+        place, (gated1, _core(gated1), across1, _core(across1)), out_weight
+    )
+    three1 = _gx(_order(three1, three0, one0), 1)
+    one1 = _gx(one1, 1)
+    two0 = _gx(_add(two0, three0).astype(BF), 2)
+    two1 = _gx(_add(two1, three1).astype(BF), 2)
     return (
-        jnp.concatenate(outputs, axis=1),
+        jnp.concatenate([finish(own0, one0, two0), finish(own1, one1, two1)], axis=1),
         jnp.concatenate(conv_pieces, axis=1),
         carry.reshape(ssm_state.shape),
     )

time: 216 us -> 212 us (0.981)
  local copies, waits for them, and re-layouts: 22.3 us -> 7.69 us
  starting transfers between devices: 30.7 us -> 38.2 us
    unnamed x50 -> x36, local copies, waits for them, and re-layouts: 20.9 us -> 6.29 us
    ppermute x36, starting transfers between devices: 30.7 us -> 38.2 us  [_swap(): return lax.ppermute(array, axis, [(i, i ^ bits) for i in range(size)])]
    pallas_call x2, Pallas kernels: 10.2 us -> 15.9 us  [out_proj(): pl.pallas_call(_out_kernel, out_shape=[jax.ShapeDtypeStruct((rows, width)...]
    pallas_call x2, Pallas kernels: 23.8 us -> 20.7 us  [ssm(): pl.pallas_call(kernel_fn, out_shape=[jax.ShapeDtypeStruct(state.shape, F3...]
    pallas_call x3 -> x2, Pallas kernels: 13.1 us -> 11.6 us  [load(): pl.pallas_call(functools.partial(_load_kernel, half), out_shape=jax.Shape...]
  transfers between devices with their start and end apart: 36 -> 36, of which waited for: 16 -> 20; matrix products, arithmetic and copies ran while one was open for 5% -> 5% of each run, Pallas kernels for 30% -> 31%
where the time goes in v2:
time: 212 us; the launch traced here: 211 us
  waiting for transfers between devices  78.7 us (37%)
  Pallas kernels  73.1 us (34%)
  starting transfers between devices  38.2 us (18%)
  other arithmetic  10.9 us (5%)
  local copies, waits for them, and re-layouts  7.69 us (4%)
    ppermute x36, waiting for transfers between devices, _swap(): return lax.ppermute(array, axis, [(i, i ^ bits) for i in range(size)])  78.7 us
    ppermute x36, starting transfers between devices, _swap(): return lax.ppermute(array, axis, [(i, i ^ bits) for i in range(size)])  38.2 us
    pallas_call x8, Pallas kernels, in_proj(): pl.pallas_call(functools.partial(_in_kernel, sibling), out_shape=jax.Shap...  24.9 us
    pallas_call x2, Pallas kernels, ssm(): pl.pallas_call(kernel_fn, out_shape=[jax.ShapeDtypeStruct(state.shape, F3...  20.7 us
    pallas_call x2, Pallas kernels, out_proj(): pl.pallas_call(_out_kernel, out_shape=[jax.ShapeDtypeStruct((rows, width)...  15.9 us
    pallas_call x2, Pallas kernels, load(): pl.pallas_call(functools.partial(_load_kernel, half), out_shape=jax.Shape...  11.6 us
    unnamed x36, local copies, waits for them, and re-layouts  6.29 us
  transfers between devices with their start and end apart: 36, of which 20 were waited for; matrix products, arithmetic and copies ran while one was open for 5% of the time, Pallas kernels for 31%

profile of v2, /device:TPU:0, one launch (start us, length us, event | category | flops | bytes accessed | tf_op | source)
XLA Modules:
  0.0 211.2 jit_solution(9495068765805325743)
XLA Ops:
  1.8 4.1 %collective-permute-start.1 = (bf16[256,512]{1,0:T(8,128)(2,1)S(1)}, bf16[256,512]{1,0:T(8,128)(2,1)S(1)}, u32[]{:S(2)}, u32[]{:S(2)}) collective-permute-start(bf16[256,512]{1,0:T(8,128)(2,1)S(1)} %bitcast.60), channel_id=1, source_target_pairs={{0,8},{4,12},{8,0},{12,4},{1,9},{5,13},{9,1},{13,5},{2,10},{6,14},... | collective-permute-start | bytes 786440 | tf_op jit(solution)/shard_map/ppermute | solution.py:231
  7.6 5.8 %load.2.refs_4_.refs_5_ = bf16[2048,4096]{1,0:T(8,128)(2,1)S(1)} custom-call(bf16[2,2048,4096]{2,1,0:T(8,128)(2,1)} %source.3, s32[2]{0:T(128)S(1)} %pad_add_fusion._.place), custom_call_target="tpu_custom_call" | custom-call | tf_op jit(solution)/shard_map/load/pallas_call | solution.py:34
  13.4 4.6 %collective-permute-done.1.refs_2_ = bf16[256,512]{1,0:T(8,128)(2,1)S(1)} collective-permute-done((bf16[256,512]{1,0:T(8,128)(2,1)S(1)}, bf16[256,512]{1,0:T(8,128)(2,1)S(1)}, u32[]{:S(2)}, u32[]{:S(2)}) %collective-permute-start.1) | collective-permute-done | bytes 262176 | tf_op jit(solution)/shard_map/ppermute | solution.py:231
  18.6 6.8 %collective-permute-done.2.refs_3_ = bf16[256,512]{1,0:T(8,128)(2,1)S(1)} collective-permute-done((bf16[256,512]{1,0:T(8,128)(2,1)S(1)}, bf16[256,512]{1,0:T(8,128)(2,1)S(1)}, u32[]{:S(2)}, u32[]{:S(2)}) %collective-permute-start.2) | collective-permute-done | bytes 262176 | tf_op jit(solution)/shard_map/ppermute | solution.py:231
  25.4 3.0 %in_proj.8.refs_5_ = bf16[2,256,1024]{2,1,0:T(8,128)(2,1)S(1)} custom-call(s32[2]{0:T(128)S(1)} %pad_add_fusion._.place, bf16[256,512]{1,0:T(8,128)(2,1)S(1)} %bitcast.62, bf16[256,512]{1,0:T(8,128)(2,1)S(1)} %collective-permute-done.refs_1_, bf16[256,512]{1,0:T(8,128)(2,1)S(1)} %collective-permute-done.1.refs_2_, ...), custom_call_target="tpu_custom_call" | custom-call | tf_op jit(solution)/shard_map/in_proj/pallas_call | solution.py:66
  28.5 3.1 %collective-permute-start.11 = (bf16[256,512]{1,0:T(8,128)(2,1)S(1)}, bf16[256,512]{1,0:T(8,128)(2,1)S(1)}, u32[]{:S(2)}, u32[]{:S(2)}) collective-permute-start(bf16[256,512]{1,0:T(8,128)(2,1)S(1)} %bitcast.54), channel_id=1, source_target_pairs={{0,8},{4,12},{8,0},{12,4},{1,9},{5,13},{9,1},{13,5},{2,10},{6,14},... | collective-permute-start | bytes 786440 | tf_op jit(solution)/shard_map/ppermute | solution.py:231
  33.3 10.9 %collective-permute-done.11.refs_2_ = bf16[256,512]{1,0:T(8,128)(2,1)S(1)} collective-permute-done((bf16[256,512]{1,0:T(8,128)(2,1)S(1)}, bf16[256,512]{1,0:T(8,128)(2,1)S(1)}, u32[]{:S(2)}, u32[]{:S(2)}) %collective-permute-start.11) | collective-permute-done | bytes 262176 | tf_op jit(solution)/shard_map/ppermute | solution.py:231
  49.1 3.1 %collective-permute-done.12.refs_3_ = bf16[256,512]{1,0:T(8,128)(2,1)S(1)} collective-permute-done((bf16[256,512]{1,0:T(8,128)(2,1)S(1)}, bf16[256,512]{1,0:T(8,128)(2,1)S(1)}, u32[]{:S(2)}, u32[]{:S(2)}) %collective-permute-start.12) | collective-permute-done | bytes 262176 | tf_op jit(solution)/shard_map/ppermute | solution.py:231
  52.2 4.0 %in_proj.10.refs_5_ = bf16[2,256,1024]{2,1,0:T(8,128)(2,1)} custom-call(s32[2]{0:T(128)S(1)} %pad_add_fusion._.place, bf16[256,512]{1,0:T(8,128)(2,1)S(1)} %bitcast.56, bf16[256,512]{1,0:T(8,128)(2,1)S(1)} %collective-permute-done.10.refs_1_, bf16[256,512]{1,0:T(8,128)(2,1)S(1)} %collective-permute-done.11.refs_2_, ...), custom_call_target="tpu_custom_call" | custom-call | tf_op jit(solution)/shard_map/in_proj/pallas_call | solution.py:66
  57.8 5.8 %copy-done.2 = bf16[2048,4096]{1,0:T(8,128)(2,1)S(1)} copy-done((bf16[2048,4096]{1,0:T(8,128)(2,1)S(1)}, bf16[2048,4096]{1,0:T(8,128)(2,1)}, u32[]{:S(2)}) %copy-start.2) | copy-done | bytes 16777240
  72.2 5.8 %load.3.refs_4_ = bf16[2048,4096]{1,0:T(8,128)(2,1)S(1)} custom-call(bf16[2,2048,4096]{2,1,0:T(8,128)(2,1)} %source.3, bf16[256,1024]{1,0:T(8,128)(2,1)S(1)} %fusion.23._.refs_5_), custom_call_target="tpu_custom_call" | custom-call | tf_op jit(solution)/shard_map/load/pallas_call | solution.py:34
  78.0 3.0 %in_proj.12.refs_5_ = bf16[2,256,1024]{2,1,0:T(8,128)(2,1)S(1)} custom-call(s32[2]{0:T(128)S(1)} %pad_add_fusion._.place, bf16[256,512]{1,0:T(8,128)(2,1)S(1)} %bitcast.64, bf16[256,512]{1,0:T(8,128)(2,1)S(1)} %collective-permute-done.refs_1_, bf16[256,512]{1,0:T(8,128)(2,1)S(1)} %collective-permute-done.1.refs_2_, ...), custom_call_target="tpu_custom_call" | custom-call | tf_op jit(solution)/shard_map/in_proj/pallas_call | solution.py:66
  92.6 4.0 %collective-permute-done.6 = bf16[128,544]{1,0:T(8,128)(2,1)S(1)} collective-permute-done((bf16[128,544]{1,0:T(8,128)(2,1)S(1)}, bf16[128,544]{1,0:T(8,128)(2,1)S(1)}, u32[]{:S(2)}, u32[]{:S(2)}) %collective-permute-start.6) | collective-permute-done | bytes 139296 | tf_op jit(solution)/shard_map/ppermute | solution.py:231
  112.4 3.0 %in_proj.15 = bf16[2,256,1024]{2,1,0:T(8,128)(2,1)S(1)} custom-call(s32[2]{0:T(128)S(1)} %pad_add_fusion._.place, bf16[256,512]{1,0:T(8,128)(2,1)S(1)} %bitcast.59, bf16[256,512]{1,0:T(8,128)(2,1)S(1)} %collective-permute-done.10.refs_1_, bf16[256,512]{1,0:T(8,128)(2,1)S(1)} %collective-permute-done.11.refs_2_, ...), custom_call_target="tpu_custom_call" | custom-call | tf_op jit(solution)/shard_map/in_proj/pallas_call | solution.py:66
  118.0 10.5 %ssm.2 = (f32[2048,1024]{1,0:T(8,128)}, f32[256,1024]{1,0:T(8,128)S(1)}) custom-call(bf16[256,512]{1,0:T(8,128)(2,1)S(1)} %slice.172.refs_0_, f32[256,32]{1,0:T(8,128)S(1)} %slice_convert_fusion.1.refs_1_, bf16[256,1024]{1,0:T(8,128)(2,1)S(1)} %bitcast.69, bf16[512,1024]{1,0:T(8,128)(2,1)S(1)} %copy-done.3, f32[1,1024]{1,0:T(1,128)S(1)} %bitcast.70, ...), custom_call_target="tpu_custom_call" | custom-call | tf_op jit(solution)/shard_map/ssm/pallas_call | solution.py:212
  133.1 10.3 %ssm.3 = (f32[2048,1024]{1,0:T(8,128)}, f32[256,1024]{1,0:T(8,128)S(1)}) custom-call(bf16[256,512]{1,0:T(8,128)(2,1)S(1)} %slice.186.low, f32[256,32]{1,0:T(8,128)S(1)} %slice_convert_fusion.bc, bf16[256,1024]{1,0:T(8,128)(2,1)S(1)} %bitcast.67, bf16[512,1024]{1,0:T(8,128)(2,1)S(1)} %copy-done.3, ...), custom_call_target="tpu_custom_call", output_to_operand_aliasing={{0}: (8, {})} | custom-call | tf_op jit(solution)/shard_map/ssm/pallas_call | solution.py:212
  143.8 9.5 %collective-permute-done.29 = bf16[256,1024]{1,0:T(8,128)(2,1)S(1)} collective-permute-done((bf16[256,1024]{1,0:T(8,128)(2,1)S(1)}, bf16[256,1024]{1,0:T(8,128)(2,1)S(1)}, u32[]{:S(2)}, u32[]{:S(2)}) %collective-permute-start.29) | collective-permute-done | bytes 524320 | tf_op jit(solution)/shard_map/ppermute | solution.py:231
  155.5 7.9 %out_proj.2 = (bf16[256,512]{1,0:T(8,128)(2,1)S(1)}, bf16[256,512]{1,0:T(8,128)(2,1)S(1)}, bf16[256,512]{1,0:T(8,128)(2,1)S(1)}, bf16[256,512]{1,0:T(8,128)(2,1)S(1)}) custom-call(s32[2]{0:T(128)S(1)} %pad_add_fusion._.place, bf16[256,1024]{1,0:T(8,128)(2,1)S(1)} %fusion.21.g0, bf16[256,1024]{1,0:T(8,128)(2,1)S(1)} %collective-permute-done.16.g1, ...), custom_call_target="tpu_custom_call" | custom-call | tf_op jit(solution)/shard_map/out_proj/pallas_call | solution.py:106
  166.2 4.0 %collective-permute-start.19 = (bf16[256,512]{1,0:T(8,128)(2,1)S(1)}, bf16[256,512]{1,0:T(8,128)(2,1)S(1)}, u32[]{:S(2)}, u32[]{:S(2)}) collective-permute-start(bf16[256,512]{1,0:T(8,128)(2,1)S(1)} %get-tuple-element.34), channel_id=1, source_target_pairs={{0,4},{4,0},{8,12},{12,8},{1,5},{5,1},{9,13},{13,9},{2,6},{6,2},{1... | collective-permute-start | bytes 786440 | tf_op jit(solution)/shard_map/ppermute | solution.py:231
  170.3 7.9 %out_proj.3 = (bf16[256,512]{1,0:T(8,128)(2,1)S(1)}, bf16[256,512]{1,0:T(8,128)(2,1)S(1)}, bf16[256,512]{1,0:T(8,128)(2,1)S(1)}, bf16[256,512]{1,0:T(8,128)(2,1)S(1)}) custom-call(s32[2]{0:T(128)S(1)} %pad_add_fusion._.place, bf16[256,1024]{1,0:T(8,128)(2,1)S(1)} %fusion.20.g0, bf16[256,1024]{1,0:T(8,128)(2,1)S(1)} %collective-permute-done.30.g1, ...), custom_call_target="tpu_custom_call" | custom-call | tf_op jit(solution)/shard_map/out_proj/pallas_call | solution.py:106
  178.2 4.6 %collective-permute-done.20 = bf16[256,512]{1,0:T(8,128)(2,1)S(1)} collective-permute-done((bf16[256,512]{1,0:T(8,128)(2,1)S(1)}, bf16[256,512]{1,0:T(8,128)(2,1)S(1)}, u32[]{:S(2)}, u32[]{:S(2)}) %collective-permute-start.20) | collective-permute-done | bytes 262176 | tf_op jit(solution)/shard_map/ppermute | solution.py:231
  186.0 9.5 %collective-permute-done.34 = bf16[256,512]{1,0:T(8,128)(2,1)S(1)} collective-permute-done((bf16[256,512]{1,0:T(8,128)(2,1)S(1)}, bf16[256,512]{1,0:T(8,128)(2,1)S(1)}, u32[]{:S(2)}, u32[]{:S(2)}) %collective-permute-start.34) | collective-permute-done | bytes 262176 | tf_op jit(solution)/shard_map/ppermute | solution.py:231
  200.4 5.3 %collective-permute-done.33 = bf16[256,512]{1,0:T(8,128)(2,1)S(1)} collective-permute-done((bf16[256,512]{1,0:T(8,128)(2,1)S(1)}, bf16[256,512]{1,0:T(8,128)(2,1)S(1)}, u32[]{:S(2)}, u32[]{:S(2)}) %collective-permute-start.33) | collective-permute-done | bytes 262176 | tf_op jit(solution)/shard_map/ppermute | solution.py:231
  205.7 4.5 %collective-permute-done.35 = bf16[256,512]{1,0:T(8,128)(2,1)S(1)} collective-permute-done((bf16[256,512]{1,0:T(8,128)(2,1)S(1)}, bf16[256,512]{1,0:T(8,128)(2,1)S(1)}, u32[]{:S(2)}, u32[]{:S(2)}) %collective-permute-start.35) | collective-permute-done | bytes 262176 | tf_op jit(solution)/shard_map/ppermute | solution.py:231
  (140 shorter events, 69.1 us)
Async XLA Ops:
  1.8 16.1 %collective-permute-start.1 = (bf16[256,512]{1,0:T(8,128)(2,1)S(1)}, bf16[256,512]{1,0:T(8,128)(2,1)S(1)}, u32[]{:S(2)}, u32[]{:S(2)}) collective-permute-start(bf16[256,512]{1,0:T(8,128)(2,1)S(1)} %bitcast.60), channel_id=1, source_target_pairs={{0,8},{4,12},{8,0},{12,4},{1,9},{5,13},{9,1},{13,5},{2,10},{6,14},... | collective-permute-start | bytes 786440 | tf_op jit(solution)/shard_map/ppermute | solution.py:231
  5.9 12.6 %collective-permute-start = (bf16[256,512]{1,0:T(8,128)(2,1)S(1)}, bf16[256,512]{1,0:T(8,128)(2,1)S(1)}, u32[]{:S(2)}, u32[]{:S(2)}) collective-permute-start(bf16[256,512]{1,0:T(8,128)(2,1)S(1)} %bitcast.61), channel_id=1, source_target_pairs={{0,4},{4,0},{8,12},{12,8},{1,5},{5,1},{9,13},{13,9},{2,6},{6,2},{1... | collective-permute-start | bytes 786440 | tf_op jit(solution)/shard_map/ppermute | solution.py:231
  28.4 19.5 %collective-permute-start.3 = (bf16[2,256,1024]{2,1,0:T(8,128)(2,1)S(1)}, bf16[2,256,1024]{2,1,0:T(8,128)(2,1)S(1)}, u32[]{:S(2)}, u32[]{:S(2)}) collective-permute-start(bf16[2,256,1024]{2,1,0:T(8,128)(2,1)S(1)} %in_proj.8.refs_5_), channel_id=1, source_target_pairs={{0,1},{1,0},{2,3},{3,2},{4,5},{5,4},{6,7},{7,6},{8,9},{9,8},{10,11... | collective-permute-start | bytes 3145736 | tf_op jit(solution)/shard_map/ppermute | solution.py:231
  28.5 15.7 %collective-permute-start.11 = (bf16[256,512]{1,0:T(8,128)(2,1)S(1)}, bf16[256,512]{1,0:T(8,128)(2,1)S(1)}, u32[]{:S(2)}, u32[]{:S(2)}) collective-permute-start(bf16[256,512]{1,0:T(8,128)(2,1)S(1)} %bitcast.54), channel_id=1, source_target_pairs={{0,8},{4,12},{8,0},{12,4},{1,9},{5,13},{9,1},{13,5},{2,10},{6,14},... | collective-permute-start | bytes 786440 | tf_op jit(solution)/shard_map/ppermute | solution.py:231
  31.6 17.5 %collective-permute-start.10 = (bf16[256,512]{1,0:T(8,128)(2,1)S(1)}, bf16[256,512]{1,0:T(8,128)(2,1)S(1)}, u32[]{:S(2)}, u32[]{:S(2)}) collective-permute-start(bf16[256,512]{1,0:T(8,128)(2,1)S(1)} %bitcast.55), channel_id=1, source_target_pairs={{0,4},{4,0},{8,12},{12,8},{1,5},{5,1},{9,13},{13,9},{2,6},{6,2},{1... | collective-permute-start | bytes 786440 | tf_op jit(solution)/shard_map/ppermute | solution.py:231
  56.2 10.4 %collective-permute-start.13 = (bf16[2,256,1024]{2,1,0:T(8,128)(2,1)}, bf16[2,256,1024]{2,1,0:T(8,128)(2,1)}, u32[]{:S(2)}, u32[]{:S(2)}) collective-permute-start(bf16[2,256,1024]{2,1,0:T(8,128)(2,1)} %in_proj.10.refs_5_), channel_id=1, source_target_pairs={{0,1},{1,0},{2,3},{3,2},{4,5},{5,4},{6,7},{7,6},{8,9},{9,8},{10,11... | collective-permute-start | bytes 3145736 | tf_op jit(solution)/shard_map/ppermute | solution.py:231
  56.2 14.7 %collective-permute-start.4 = (bf16[256,1024]{1,0:T(8,128)(2,1)}, bf16[256,1024]{1,0:T(8,128)(2,1)}, u32[]{:S(2)}, u32[]{:S(2)}) collective-permute-start(bf16[256,1024]{1,0:T(8,128)(2,1)} %fusion.22.refs_5_), channel_id=1, source_target_pairs={{0,2},{1,3},{2,0},{3,1},{4,6},{5,7},{6,4},{7,5},{8,10},{9,11},{10,... | collective-permute-start | bytes 1572872 | tf_op jit(solution)/shard_map/ppermute | solution.py:231
  68.0 16.1 %collective-permute-start.22 = (bf16[256,1024]{1,0:T(8,128)(2,1)S(1)}, bf16[256,1024]{1,0:T(8,128)(2,1)S(1)}, u32[]{:S(2)}, u32[]{:S(2)}) collective-permute-start(bf16[256,1024]{1,0:T(8,128)(2,1)S(1)} %fusion.23._.refs_5_), channel_id=1, source_target_pairs={{0,2},{1,3},{2,0},{3,1},{4,6},{5,7},{6,4},{7,5},{8,10},{9,11},{10,... | collective-permute-start | bytes 1572872 | tf_op jit(solution)/shard_map/ppermute | solution.py:231
  81.0 24.0 %collective-permute-start.14 = (bf16[2,256,1024]{2,1,0:T(8,128)(2,1)S(1)}, bf16[2,256,1024]{2,1,0:T(8,128)(2,1)S(1)}, u32[]{:S(2)}, u32[]{:S(2)}) collective-permute-start(bf16[2,256,1024]{2,1,0:T(8,128)(2,1)S(1)} %in_proj.12.refs_5_), channel_id=1, source_target_pairs={{0,1},{1,0},{2,3},{3,2},{4,5},{5,4},{6,7},{7,6},{8,9},{9,8},{10,11... | collective-permute-start | bytes 3145736 | tf_op jit(solution)/shard_map/ppermute | solution.py:231
  99.8 12.4 %collective-permute-start.25 = (bf16[128,544]{1,0:T(8,128)(2,1)S(1)}, bf16[128,544]{1,0:T(8,128)(2,1)S(1)}, u32[]{:S(2)}, u32[]{:S(2)}) collective-permute-start(bf16[128,544]{1,0:T(8,128)(2,1)S(1)} %fusion.27), channel_id=1, source_target_pairs={{0,4},{4,0},{8,12},{12,8},{1,5},{5,1},{9,13},{13,9},{2,6},{6,2},{1... | collective-permute-start | bytes 417800 | tf_op jit(solution)/shard_map/ppermute | solution.py:231
  105.2 12.5 %collective-permute-start.15 = (bf16[256,1024]{1,0:T(8,128)(2,1)S(1)}, bf16[256,1024]{1,0:T(8,128)(2,1)S(1)}, u32[]{:S(2)}, u32[]{:S(2)}) collective-permute-start(bf16[256,1024]{1,0:T(8,128)(2,1)S(1)} %fusion.24.refs_5_), channel_id=1, source_target_pairs={{0,2},{1,3},{2,0},{3,1},{4,6},{5,7},{6,4},{7,5},{8,10},{9,11},{10,... | collective-permute-start | bytes 1572872 | tf_op jit(solution)/shard_map/ppermute | solution.py:231
  110.1 20.2 %collective-permute-start.28 = (bf16[2,256,1024]{2,1,0:T(8,128)(2,1)S(1)}, bf16[2,256,1024]{2,1,0:T(8,128)(2,1)S(1)}, u32[]{:S(2)}, u32[]{:S(2)}) collective-permute-start(bf16[2,256,1024]{2,1,0:T(8,128)(2,1)S(1)} %in_proj.14.refs_5_), channel_id=1, source_target_pairs={{0,1},{1,0},{2,3},{3,2},{4,5},{5,4},{6,7},{7,6},{8,9},{9,8},{10,11... | collective-permute-start | bytes 3145736 | tf_op jit(solution)/shard_map/ppermute | solution.py:231
  112.3 18.8 %collective-permute-start.26 = (bf16[128,544]{1,0:T(8,128)(2,1)S(1)}, bf16[128,544]{1,0:T(8,128)(2,1)S(1)}, u32[]{:S(2)}, u32[]{:S(2)}) collective-permute-start(bf16[128,544]{1,0:T(8,128)(2,1)S(1)} %fusion.29), channel_id=1, source_target_pairs={{0,8},{4,12},{8,0},{12,4},{1,9},{5,13},{9,1},{13,5},{2,10},{6,14},... | collective-permute-start | bytes 417800 | tf_op jit(solution)/shard_map/ppermute | solution.py:231
  128.8 14.9 %collective-permute-start.17 = (bf16[256,1024]{1,0:T(8,128)(2,1)S(1)}, bf16[256,1024]{1,0:T(8,128)(2,1)S(1)}, u32[]{:S(2)}, u32[]{:S(2)}) collective-permute-start(bf16[256,1024]{1,0:T(8,128)(2,1)S(1)} %fusion.21.g0), channel_id=1, source_target_pairs={{0,2},{1,3},{2,0},{3,1},{4,6},{5,7},{6,4},{7,5},{8,10},{9,11},{10,... | collective-permute-start | bytes 1572872 | tf_op jit(solution)/shard_map/ppermute | solution.py:231
  130.6 22.7 %collective-permute-start.29 = (bf16[256,1024]{1,0:T(8,128)(2,1)S(1)}, bf16[256,1024]{1,0:T(8,128)(2,1)S(1)}, u32[]{:S(2)}, u32[]{:S(2)}) collective-permute-start(bf16[256,1024]{1,0:T(8,128)(2,1)S(1)} %fusion.25), channel_id=1, source_target_pairs={{0,2},{1,3},{2,0},{3,1},{4,6},{5,7},{6,4},{7,5},{8,10},{9,11},{10,... | collective-permute-start | bytes 1572872 | tf_op jit(solution)/shard_map/ppermute | solution.py:231
  132.8 22.6 %collective-permute-start.16 = (bf16[256,1024]{1,0:T(8,128)(2,1)S(1)}, bf16[256,1024]{1,0:T(8,128)(2,1)S(1)}, u32[]{:S(2)}, u32[]{:S(2)}) collective-permute-start(bf16[256,1024]{1,0:T(8,128)(2,1)S(1)} %fusion.21.g0), channel_id=1, source_target_pairs={{0,1},{1,0},{2,3},{3,2},{4,5},{5,4},{6,7},{7,6},{8,9},{9,8},{10,11... | collective-permute-start | bytes 1572872 | tf_op jit(solution)/shard_map/ppermute | solution.py:231
  143.7 11.8 %collective-permute-start.18 = (bf16[256,1024]{1,0:T(8,128)(2,1)S(1)}, bf16[256,1024]{1,0:T(8,128)(2,1)S(1)}, u32[]{:S(2)}, u32[]{:S(2)}) collective-permute-start(bf16[256,1024]{1,0:T(8,128)(2,1)S(1)} %collective-permute-done.17.g2), channel_id=1, source_target_pairs={{0,1},{1,0},{2,3},{3,2},{4,5},{5,4},{6,7},{7,6},{8,9},{9,8},{10,11... | collective-permute-start | bytes 1572872 | tf_op jit(solution)/shard_map/ppermute | solution.py:231
  153.7 12.5 %collective-permute-start.31 = (bf16[256,1024]{1,0:T(8,128)(2,1)S(1)}, bf16[256,1024]{1,0:T(8,128)(2,1)S(1)}, u32[]{:S(2)}, u32[]{:S(2)}) collective-permute-start(bf16[256,1024]{1,0:T(8,128)(2,1)S(1)} %fusion.20.g0), channel_id=1, source_target_pairs={{0,2},{1,3},{2,0},{3,1},{4,6},{5,7},{6,4},{7,5},{8,10},{9,11},{10,... | collective-permute-start | bytes 1572872 | tf_op jit(solution)/shard_map/ppermute | solution.py:231
  166.2 12.0 %collective-permute-start.19 = (bf16[256,512]{1,0:T(8,128)(2,1)S(1)}, bf16[256,512]{1,0:T(8,128)(2,1)S(1)}, u32[]{:S(2)}, u32[]{:S(2)}) collective-permute-start(bf16[256,512]{1,0:T(8,128)(2,1)S(1)} %get-tuple-element.34), channel_id=1, source_target_pairs={{0,4},{4,0},{8,12},{12,8},{1,5},{5,1},{9,13},{13,9},{2,6},{6,2},{1... | collective-permute-start | bytes 786440 | tf_op jit(solution)/shard_map/ppermute | solution.py:231
  170.2 12.6 %collective-permute-start.20 = (bf16[256,512]{1,0:T(8,128)(2,1)S(1)}, bf16[256,512]{1,0:T(8,128)(2,1)S(1)}, u32[]{:S(2)}, u32[]{:S(2)}) collective-permute-start(bf16[256,512]{1,0:T(8,128)(2,1)S(1)} %get-tuple-element.36), channel_id=1, source_target_pairs={{0,4},{4,0},{8,12},{12,8},{1,5},{5,1},{9,13},{13,9},{2,6},{6,2},{1... | collective-permute-start | bytes 786440 | tf_op jit(solution)/shard_map/ppermute | solution.py:231
  182.8 12.7 %collective-permute-start.34 = (bf16[256,512]{1,0:T(8,128)(2,1)S(1)}, bf16[256,512]{1,0:T(8,128)(2,1)S(1)}, u32[]{:S(2)}, u32[]{:S(2)}) collective-permute-start(bf16[256,512]{1,0:T(8,128)(2,1)S(1)} %get-tuple-element.45), channel_id=1, source_target_pairs={{0,4},{4,0},{8,12},{12,8},{1,5},{5,1},{9,13},{13,9},{2,6},{6,2},{1... | collective-permute-start | bytes 786440 | tf_op jit(solution)/shard_map/ppermute | solution.py:231
  184.7 15.6 %collective-permute-start.21 = (bf16[256,512]{1,0:T(8,128)(2,1)S(1)}, bf16[256,512]{1,0:T(8,128)(2,1)S(1)}, u32[]{:S(2)}, u32[]{:S(2)}) collective-permute-start(bf16[256,512]{1,0:T(8,128)(2,1)S(1)} %add_convert_fusion.7), channel_id=1, source_target_pairs={{0,8},{4,12},{8,0},{12,4},{1,9},{5,13},{9,1},{13,5},{2,10},{6,14},... | collective-permute-start | bytes 786440 | tf_op jit(solution)/shard_map/ppermute | solution.py:231
  185.5 20.2 %collective-permute-start.33 = (bf16[256,512]{1,0:T(8,128)(2,1)S(1)}, bf16[256,512]{1,0:T(8,128)(2,1)S(1)}, u32[]{:S(2)}, u32[]{:S(2)}) collective-permute-start(bf16[256,512]{1,0:T(8,128)(2,1)S(1)} %get-tuple-element.42), channel_id=1, source_target_pairs={{0,4},{4,0},{8,12},{12,8},{1,5},{5,1},{9,13},{13,9},{2,6},{6,2},{1... | collective-permute-start | bytes 786440 | tf_op jit(solution)/shard_map/ppermute | solution.py:231
  195.6 14.7 %collective-permute-start.35 = (bf16[256,512]{1,0:T(8,128)(2,1)S(1)}, bf16[256,512]{1,0:T(8,128)(2,1)S(1)}, u32[]{:S(2)}, u32[]{:S(2)}) collective-permute-start(bf16[256,512]{1,0:T(8,128)(2,1)S(1)} %add_convert_fusion.5), channel_id=1, source_target_pairs={{0,8},{4,12},{8,0},{12,4},{1,9},{5,13},{9,1},{13,5},{2,10},{6,14},... | collective-permute-start | bytes 786440 | tf_op jit(solution)/shard_map/ppermute | solution.py:231
  (30 other events, 268.5 us)

commit v3 on v2

--- a/solution.py
+++ b/solution.py
@@ -20,6 +20,12 @@
 SCALARS = pl.BlockSpec(memory_space=pltpu.SMEM)
 
 
+def _cost(microseconds):
+    return pl.CostEstimate(
+        flops=int(microseconds * 1.1e9), bytes_accessed=1, transcendentals=0
+    )
+
+
 def _params(mib):
     return pltpu.CompilerParams(vmem_limit_bytes=mib * 1024 * 1024)
 
@@ -42,7 +48,7 @@
     )(weight, after)
 
 
-def _in_kernel(sibling, place, *refs):
+def _held_kernel(sibling, place, *refs):
     *pieces, weight, _, out = refs
     depth = pieces[0].shape[1]
     channels = out.shape[2]
@@ -60,14 +66,15 @@
         out[i] = total.astype(out.dtype)
 
 
-def in_proj(place, pieces, weight, sibling, after):
+def held_proj(place, pieces, weight, sibling, after):
     rows = pieces[0].shape[0]
     channels = weight.shape[1] // 4
     return pl.pallas_call(
-        functools.partial(_in_kernel, sibling),
+        functools.partial(_held_kernel, sibling),
         out_shape=jax.ShapeDtypeStruct((2, rows, channels), BF),
         in_specs=[SCALARS] + [IN_VMEM] * (len(pieces) + 1) + [ANYWHERE],
         out_specs=IN_VMEM,
+        cost_estimate=_cost(100),
         compiler_params=_params(8),
         name="in_proj",
     )(place, *pieces, weight, after)
@@ -112,6 +119,7 @@
             pltpu.VMEM((4, out_weight.shape[0], width), BF),
             pltpu.SemaphoreType.DMA((4,)),
         ],
+        cost_estimate=_cost(0.001),
         compiler_params=_params(50),
         name="out_proj",
     )(place, *pieces, out_weight)
@@ -222,6 +230,7 @@
         + [pltpu.VMEM((rows // 8 * 2 * N, 8, lanes), F32)]
         + [pltpu.SemaphoreType.DMA((count,))] * 2,
         input_output_aliases=aliases,
+        cost_estimate=_cost(0.001),
         compiler_params=_params(16),
         name="ssm",
     )(*args)
@@ -266,96 +275,118 @@
     chunks = range(CHUNKS)
     cut = [slice(c * piece, (c + 1) * piece) for c in chunks]
 
-    gathered = []
-    before = None
-    weight = load(in_weight, 0, place)
-    for c in chunks:
-        own = normed[:, cut[c], :].reshape(rows, depth)
-        if before is not None:
-            own = _order(own, before)
-        two = _gx(own, 2)
-        one = _gx(own, 1)
-        relay = _order(two, weight)
-        gathered.append((own, one, two, _gx(relay, 1)))
-        before = relay
-
-    arrived = {}
-    after = weight
-    for half in range(2):
-        if half:
-            weight = load(in_weight, 1, after)
-        for c in chunks:
-            pieces = (_order(gathered[c][0], after),) + gathered[c][1:]
-            away = in_proj(place, pieces, weight, 1, after)
-            near = _core(away)
-            kept = in_proj(place, pieces, weight, 0, away)
-            summed = _add(kept[0], near[0]).astype(BF)
-            after = summed
-            arrived[half, c] = _add(kept[1], near[1], _chip(summed)).astype(BF)
-
-    conv_pieces, sums = [], []
-    for c in chunks:
-        inner = arrived[0, c].reshape(steps, piece, channels)
-        history = jnp.concatenate([conv_state[:, cut[c], :], inner], axis=0).astype(F32)
+
+    half_rows = rows // 2
+    kept, near = {}, {}
+
+    def multiply(half, c, pieces, after):
+        away = held_proj(place, pieces, weights[half], 1, after)
+        near[half, c] = _core(away)
+        kept[half, c] = held_proj(place, pieces, weights[half], 0, away)
+        return away
+
+    def cross(c, half):
+        summed = _add(kept[half, c][0], near[half, c][0]).astype(BF)
+        return summed, (kept[half, c][1], near[half, c][1], _chip(summed))
+
+    def convolve(c, parts):
+        values = _add(*parts).astype(BF).reshape(steps, piece, channels)
+        history = jnp.concatenate([conv_state[:, cut[c], :], values], axis=0).astype(F32)
         accum = conv_bias[None, None, :]
         for tap in range(CONV):
             accum = accum + conv_weight[tap][None, None, :] * history[tap : tap + steps]
         conv_out = jax.nn.silu(accum).astype(BF).reshape(rows, channels)
-        conv_pieces.append(inner[steps - CONV + 1 :])
-
+        return conv_out, values[steps - CONV + 1 :]
+
+    def project(conv_out):
         proj = jnp.dot(conv_out, x_weight, preferred_element_type=F32)
-        half_rows = rows // 2
         theirs = lax.dynamic_slice_in_dim(proj, (1 - core) * half_rows, half_rows, 0)
         mine = lax.dynamic_slice_in_dim(proj, core * half_rows, half_rows, 0)
-        mine = _add(mine, _core(theirs.astype(BF)))
-        mine = _add(mine, _chip(mine.astype(BF)))
-        mine = _add(mine, _gx(mine.astype(BF), 1))
-        mine = _add(mine, _gx(mine.astype(BF), 2)).astype(BF)
+        theirs = theirs.astype(BF)
+        mine = _add(mine, _core(theirs))
+        return theirs, mine, mine.astype(BF)
+
+    one_away = lambda array: _gx(array, 1)
+    two_away = lambda array: _gx(array, 2)
+
+    def reduce(mine, sent):
+        mine = _add(mine, _chip(sent))
+        mine = _add(mine, one_away(mine.astype(BF)))
+        mine = _add(mine, two_away(mine.astype(BF))).astype(BF)
         sibling = _core(mine)
-        both = jnp.where(
-            core == 0,
-            jnp.concatenate([mine, sibling], axis=0),
-            jnp.concatenate([sibling, mine], axis=0),
-        )
-        low = both[:, :DT]
-        b_c = both[:, DT:].astype(F32)
-
-        sums.append((low, b_c, conv_out))
+        first = jnp.where(core == 0, mine, sibling)
+        second = jnp.where(core == 0, sibling, mine)
+        both = jnp.concatenate([first, second], axis=0)
+        return mine, both[:, :DT], both[:, DT:].astype(F32)
+
+    owns = [normed[:, cut[c], :].reshape(rows, depth) for c in chunks]
+    weights = [load(in_weight, 0, place)]
+    held0 = weights[0]
+    two = _gx(owns[0], 2)
+    one = _gx(owns[0], 1)
+    relay = _order(two, held0)
+    pieces0 = (owns[0], one, two, _gx(relay, 1))
+    second = _order(owns[1], relay)
+    two = _gx(second, 2)
+    one = _gx(second, 1)
+    away0 = multiply(0, 0, pieces0, held0)
+    kept0 = kept[0, 0]
+    summed0, parts = cross(0, 0)
+    pieces1 = (second, one, two, _gx(_order(two, summed0), 1))
+    conv0, next0 = convolve(0, parts)
+    theirs0, mine, far0 = project(conv0)
+    multiply(0, 1, (_order(second, summed0), *pieces1[1:]), summed0)
+    summed1, parts = cross(1, 0)
+    fin0, low0, b_c0 = reduce(mine, far0)
+    weights.append(load(in_weight, 1, summed1))
+    ag0 = multiply(1, 0, (_order(owns[0], summed1), *pieces0[1:]), weights[1])
+    kg0 = kept[1, 0]
+    left, right, over = parts
+    conv1, next1 = convolve(1, (left, right, _order(over, kg0)))
+    theirs1, mine, far1 = project(conv1)
+    kept[1, 0] = _order(kept[1, 0], far1)
+    sg0, gate0 = cross(0, 1)
+    multiply(1, 1, (_order(second, sg0), *pieces1[1:]), kg0)
+    fin1, low1, b_c1 = reduce(mine, far1)
+    kept[1, 1] = _order(kept[1, 1], far1)
+    gate1 = cross(1, 1)[1]
+    gate0 = _add(*gate0).astype(BF)
+    gate1 = _add(*gate1).astype(BF)
 
     scan = functools.partial(
         ssm, dt_weight=dt_weight, dt_bias=dt_bias[None, :], skip=skip[None, :], a_log=a_log,
         state=flat_state,
     )
 
-    def gate_by(c, result):
-        return (result * jax.nn.silu(arrived[1, c].astype(F32))).astype(BF)
+    def gate_by(gate, result):
+        return (result * jax.nn.silu(gate.astype(F32))).astype(BF)
 
     def finish(own, first, second):
         return _add(own, first, second).astype(BF).reshape(steps, piece, depth)
 
-    low, b_c, conv_out = sums[0]
-    carry, result = scan(0, steps, _order(low, arrived[1, 0]), b_c, conv_out, carry=None)
-    gated0 = gate_by(0, result)
+    carry, result = scan(0, steps, _order(low0, gate0), b_c0, conv0, carry=None)
+    gated0 = gate_by(gate0, result)
     across0 = _chip(gated0)
-    carry, result = scan(1, steps, *sums[1], carry=carry)
-    gated1 = gate_by(1, result)
+    carry, result = scan(1, steps, low1, b_c1, conv1, carry=carry)
+    gated1 = gate_by(gate1, result)
     across1 = _chip(gated1)
     three0, two0, one0, own0 = out_proj(
         place, (gated0, _core(gated0), across0, _core(across0)), out_weight
     )
     three0 = _gx(three0, 1)
     one0 = _gx(one0, 1)
-    across1 = _order(across1, own0)
+    joined0 = _add(two0, three0).astype(BF)
+    two0 = _gx(joined0, 2)
+    near1 = _core(across1)
     three1, two1, one1, own1 = out_proj(
-        place, (gated1, _core(gated1), across1, _core(across1)), out_weight
-    )
-    three1 = _gx(_order(three1, three0, one0), 1)
+        place, (gated1, _core(gated1), across1, near1), out_weight
+    )
+    three1 = _gx(_order(three1, one0), 1)
     one1 = _gx(one1, 1)
-    two0 = _gx(_add(two0, three0).astype(BF), 2)
     two1 = _gx(_add(two1, three1).astype(BF), 2)
     return (
         jnp.concatenate([finish(own0, one0, two0), finish(own1, one1, two1)], axis=1),
-        jnp.concatenate(conv_pieces, axis=1),
+        jnp.concatenate([next0, next1], axis=1),
         carry.reshape(ssm_state.shape),
     )
 

time: 212 us -> 209 us (0.986)
  starting transfers between devices: 38.2 us -> 31.3 us
  waiting for transfers between devices: 78.7 us -> 72.6 us
  other arithmetic: 10.9 us -> 16.9 us
  local copies, waits for them, and re-layouts: 7.69 us -> 10.9 us
    ppermute x36, starting transfers between devices: 38.2 us -> 31.3 us  [_swap(): return lax.ppermute(array, axis, [(i, i ^ bits) for i in range(size)])]
    ppermute x36, waiting for transfers between devices: 78.7 us -> 72.6 us  [_swap(): return lax.ppermute(array, axis, [(i, i ^ bits) for i in range(size)])]
    convert_element_type x22, other arithmetic: 8.68 us -> 14.7 us  [the longest x2 3.77 us: convolve(): values = _add(*parts).astype(BF).reshape(steps, piece, channels)]
    unnamed x36 -> x110, local copies, waits for them, and re-layouts: 6.29 us -> 7.41 us
  transfers between devices with their start and end apart: 36 -> 36, of which waited for: 20 -> 17; matrix products, arithmetic and copies ran while one was open for 5% -> 8% of each run, Pallas kernels for 31% -> 36%
where the time goes in v3:
time: 209 us
  Pallas kernels  74.3 us (36%)
  waiting for transfers between devices  72.6 us (35%)
  starting transfers between devices  31.3 us (15%)
  other arithmetic  16.9 us (8%)
  local copies, waits for them, and re-layouts  10.9 us (5%)
    ppermute x36, waiting for transfers between devices, _swap(): return lax.ppermute(array, axis, [(i, i ^ bits) for i in range(size)])  72.6 us
    ppermute x36, starting transfers between devices, _swap(): return lax.ppermute(array, axis, [(i, i ^ bits) for i in range(size)])  31.3 us
    pallas_call x8, Pallas kernels, held_proj(): pl.pallas_call(functools.partial(_held_kernel, sibling), out_shape=jax.Sh...  26.2 us
    pallas_call x2, Pallas kernels, ssm(): pl.pallas_call(kernel_fn, out_shape=[jax.ShapeDtypeStruct(state.shape, F3...  20.7 us
    pallas_call x2, Pallas kernels, out_proj(): pl.pallas_call(_out_kernel, out_shape=[jax.ShapeDtypeStruct((rows, width)...  15.9 us
    pallas_call x2, Pallas kernels, load(): pl.pallas_call(functools.partial(_load_kernel, half), out_shape=jax.Shape...  11.6 us
    unnamed x110, local copies, waits for them, and re-layouts  7.41 us
  transfers between devices with their start and end apart: 36, of which 17 were waited for; matrix products, arithmetic and copies ran while one was open for 8% of the time, Pallas kernels for 36%

profile of v3, /device:TPU:0, one launch (start us, length us, event | category | flops | bytes accessed | tf_op | source)
XLA Modules:
  0.0 208.9 jit_solution(178560152391177947)
XLA Ops:
  2.5 4.0 %collective-permute-start.1 = (bf16[256,512]{1,0:T(8,128)(2,1)S(1)}, bf16[256,512]{1,0:T(8,128)(2,1)S(1)}, u32[]{:S(2)}, u32[]{:S(2)}) collective-permute-start(bf16[256,512]{1,0:T(8,128)(2,1)S(1)} %bitcast.56), channel_id=1, source_target_pairs={{0,8},{4,12},{8,0},{12,4},{1,9},{5,13},{9,1},{13,5},{2,10},{6,14},... | collective-permute-start | bytes 786440 | tf_op jit(solution)/shard_map/ppermute | solution.py:240
  8.2 5.8 %load.2.refs_4_.refs_5_ = bf16[2048,4096]{1,0:T(8,128)(2,1)S(1)} custom-call(bf16[2,2048,4096]{2,1,0:T(8,128)(2,1)} %source.3, s32[2]{0:T(128)S(1)} %pad_add_fusion._.place), custom_call_target="tpu_custom_call" | custom-call | tf_op jit(solution)/shard_map/load/pallas_call | solution.py:40
  14.0 4.6 %collective-permute-done.1.refs_2_ = bf16[256,512]{1,0:T(8,128)(2,1)S(1)} collective-permute-done((bf16[256,512]{1,0:T(8,128)(2,1)S(1)}, bf16[256,512]{1,0:T(8,128)(2,1)S(1)}, u32[]{:S(2)}, u32[]{:S(2)}) %collective-permute-start.1) | collective-permute-done | bytes 262176 | tf_op jit(solution)/shard_map/ppermute | solution.py:240
  19.2 3.4 %collective-permute-start.11 = (bf16[256,512]{1,0:T(8,128)(2,1)}, bf16[256,512]{1,0:T(8,128)(2,1)}, u32[]{:S(2)}, u32[]{:S(2)}) collective-permute-start(bf16[256,512]{1,0:T(8,128)(2,1)} %bitcast.11.refs_0_), channel_id=1, source_target_pairs={{0,8},{4,12},{8,0},{12,4},{1,9},{5,13},{9,1},{13,5},{2,10},{6,14},... | collective-permute-start | bytes 786440 | tf_op jit(solution)/shard_map/ppermute | solution.py:240
  22.6 10.4 %collective-permute-done.2.refs_3_ = bf16[256,512]{1,0:T(8,128)(2,1)S(1)} collective-permute-done((bf16[256,512]{1,0:T(8,128)(2,1)S(1)}, bf16[256,512]{1,0:T(8,128)(2,1)S(1)}, u32[]{:S(2)}, u32[]{:S(2)}) %collective-permute-start.2) | collective-permute-done | bytes 262176 | tf_op jit(solution)/shard_map/ppermute | solution.py:240
  44.2 5.8 %collective-permute-done.12.refs_3_ = bf16[256,512]{1,0:T(8,128)(2,1)S(1)} collective-permute-done((bf16[256,512]{1,0:T(8,128)(2,1)}, bf16[256,512]{1,0:T(8,128)(2,1)S(1)}, u32[]{:S(2)}, u32[]{:S(2)}) %collective-permute-start.12) | collective-permute-done | bytes 262176 | tf_op jit(solution)/shard_map/ppermute | solution.py:240
  50.0 5.8 %copy-done.3 = bf16[2048,4096]{1,0:T(8,128)(2,1)S(1)} copy-done((bf16[2048,4096]{1,0:T(8,128)(2,1)S(1)}, bf16[2048,4096]{1,0:T(8,128)(2,1)}, u32[]{:S(2)}) %copy-start.3) | copy-done | bytes 16777240
  55.7 3.5 %in_proj.10.refs_5_ = bf16[2,256,1024]{2,1,0:T(8,128)(2,1)S(1)} custom-call(s32[2]{0:T(128)S(1)} %pad_add_fusion._.place, bf16[256,512]{1,0:T(8,128)(2,1)} %bitcast.11.refs_0_, bf16[256,512]{1,0:T(8,128)(2,1)} %collective-permute-done.10.refs_1_, bf16[256,512]{1,0:T(8,128)(2,1)} %collective-permute-done.11.refs_2_, ...), custom_call_target="tpu_custom_call" | custom-call | flops 109999996928 | bytes 1 | tf_op jit(solution)/shard_map/in_proj/pallas_call | solution.py:72
  59.4 3.7 %in_proj.11 = bf16[2,256,1024]{2,1,0:T(8,128)(2,1)S(1)} custom-call(s32[2]{0:T(128)S(1)} %pad_add_fusion._.place, bf16[256,512]{1,0:T(8,128)(2,1)} %bitcast.11.refs_0_, bf16[256,512]{1,0:T(8,128)(2,1)} %collective-permute-done.10.refs_1_, bf16[256,512]{1,0:T(8,128)(2,1)} %collective-permute-done.11.refs_2_, ...), custom_call_target="tpu_custom_call" | custom-call | flops 109999996928 | bytes 1 | tf_op jit(solution)/shard_map/in_proj/pallas_call | solution.py:72
  68.3 5.8 %load.3.refs_4_.refs_5_ = bf16[2048,4096]{1,0:T(8,128)(2,1)S(1)} custom-call(bf16[2,2048,4096]{2,1,0:T(8,128)(2,1)} %source.3, bf16[256,1024]{1,0:T(8,128)(2,1)} %fusion.23._), custom_call_target="tpu_custom_call" | custom-call | tf_op jit(solution)/shard_map/load/pallas_call | solution.py:40
  74.1 2.9 %in_proj.12.refs_5_ = bf16[2,256,1024]{2,1,0:T(8,128)(2,1)S(1)} custom-call(s32[2]{0:T(128)S(1)} %pad_add_fusion._.place, bf16[256,512]{1,0:T(8,128)(2,1)S(1)} %bitcast.60, bf16[256,512]{1,0:T(8,128)(2,1)S(1)} %collective-permute-done.refs_1_, bf16[256,512]{1,0:T(8,128)(2,1)S(1)} %copy-done.17, bf16[256,512]{1,0:T(8,128)(2,1)S(1)} %copy-done.19, ...), custom_call_target="tpu_custom_call" | custom-call | flops 109999996928 | bytes 1 | tf_op jit(solution)/shard_map/in_proj/pallas_call | solution.py:72
  77.2 2.9 %in_proj.13.refs_5_ = bf16[2,256,1024]{2,1,0:T(8,128)(2,1)S(1)} custom-call(s32[2]{0:T(128)S(1)} %pad_add_fusion._.place, bf16[256,512]{1,0:T(8,128)(2,1)S(1)} %bitcast.61, bf16[256,512]{1,0:T(8,128)(2,1)S(1)} %collective-permute-done.refs_1_, bf16[256,512]{1,0:T(8,128)(2,1)S(1)} %copy-done.17, bf16[256,512]{1,0:T(8,128)(2,1)S(1)} %copy-done.19, ...), custom_call_target="tpu_custom_call" | custom-call | flops 109999996928 | bytes 1 | tf_op jit(solution)/shard_map/in_proj/pallas_call | solution.py:72
  89.2 4.6 %collective-permute-done.24 = bf16[128,544]{1,0:T(8,128)(2,1)S(1)} collective-permute-done((bf16[128,544]{1,0:T(8,128)(2,1)S(1)}, bf16[128,544]{1,0:T(8,128)(2,1)S(1)}, u32[]{:S(2)}, u32[]{:S(2)}) %collective-permute-start.24) | collective-permute-done | bytes 139296 | tf_op jit(solution)/shard_map/ppermute | solution.py:240
  108.5 3.5 %in_proj.14.refs_5_ = bf16[2,256,1024]{2,1,0:T(8,128)(2,1)S(1)} custom-call(s32[2]{0:T(128)S(1)} %pad_add_fusion._.place, bf16[256,512]{1,0:T(8,128)(2,1)} %bitcast.11.refs_0_, bf16[256,512]{1,0:T(8,128)(2,1)} %collective-permute-done.10.refs_1_, bf16[256,512]{1,0:T(8,128)(2,1)} %collective-permute-done.11.refs_2_, ...), custom_call_target="tpu_custom_call" | custom-call | flops 109999996928 | bytes 1 | tf_op jit(solution)/shard_map/in_proj/pallas_call | solution.py:72
  112.2 3.7 %in_proj.15 = bf16[2,256,1024]{2,1,0:T(8,128)(2,1)S(1)} custom-call(s32[2]{0:T(128)S(1)} %pad_add_fusion._.place, bf16[256,512]{1,0:T(8,128)(2,1)} %bitcast.11.refs_0_, bf16[256,512]{1,0:T(8,128)(2,1)} %collective-permute-done.10.refs_1_, bf16[256,512]{1,0:T(8,128)(2,1)} %collective-permute-done.11.refs_2_, ...), custom_call_target="tpu_custom_call" | custom-call | flops 109999996928 | bytes 1 | tf_op jit(solution)/shard_map/in_proj/pallas_call | solution.py:72
  122.4 10.5 %ssm.2 = (f32[2048,1024]{1,0:T(8,128)}, f32[256,1024]{1,0:T(8,128)S(1)}) custom-call(bf16[256,512]{1,0:T(8,128)(2,1)S(1)} %fusion.27.refs_0_, f32[256,32]{1,0:T(8,128)S(1)} %fusion.33.refs_1_, bf16[256,1024]{1,0:T(8,128)(2,1)S(1)} %bitcast.55, bf16[512,1024]{1,0:T(8,128)(2,1)S(1)} %copy-done.8, f32[1,1024]{1,0:T(1,128)S(1)} %bitcast.62, ...), custom_call_target="tpu_custom_call" | custom-call | flops 1100000 | bytes 1 | tf_op jit(solution)/shard_map/ssm/pallas_call | solution.py:220
  134.8 10.2 %ssm.3 = (f32[2048,1024]{1,0:T(8,128)}, f32[256,1024]{1,0:T(8,128)S(1)}) custom-call(bf16[256,512]{1,0:T(8,128)(2,1)S(1)} %fusion.26.low, f32[256,32]{1,0:T(8,128)S(1)} %fusion.32.bc, bf16[256,1024]{1,0:T(8,128)(2,1)S(1)} %bitcast.53, bf16[512,1024]{1,0:T(8,128)(2,1)S(1)} %copy-done.8, f32[1,1024]{1,0:T(1,128)S(1)} %bitcast.63, ...), custom_call_target="tpu_custom_call", output_to_operand_aliasing={{0}: (8, {})} | custom-call | flops 1100000 | bytes 1 | tf_op jit(solution)/shard_map/ssm/pallas_call | solution.py:220
  147.5 11.5 %collective-permute-done.31.g2 = bf16[256,1024]{1,0:T(8,128)(2,1)S(1)} collective-permute-done((bf16[256,1024]{1,0:T(8,128)(2,1)S(1)}, bf16[256,1024]{1,0:T(8,128)(2,1)S(1)}, u32[]{:S(2)}, u32[]{:S(2)}) %collective-permute-start.31) | collective-permute-done | bytes 524320 | tf_op jit(solution)/shard_map/ppermute | solution.py:240
  159.0 7.9 %out_proj.2 = (bf16[256,512]{1,0:T(8,128)(2,1)S(1)}, bf16[256,512]{1,0:T(8,128)(2,1)S(1)}, bf16[256,512]{1,0:T(8,128)(2,1)S(1)}, bf16[256,512]{1,0:T(8,128)(2,1)S(1)}) custom-call(s32[2]{0:T(128)S(1)} %pad_add_fusion._.place, bf16[256,1024]{1,0:T(8,128)(2,1)S(1)} %fusion.21.g0, bf16[256,1024]{1,0:T(8,128)(2,1)S(1)} %collective-permute-done.18.g1, ...), custom_call_target="tpu_custom_call" | custom-call | flops 1100000 | bytes 1 | tf_op jit(solution)/shard_map/out_proj/pallas_call | solution.py:113
  169.3 7.9 %out_proj.3 = (bf16[256,512]{1,0:T(8,128)(2,1)S(1)}, bf16[256,512]{1,0:T(8,128)(2,1)S(1)}, bf16[256,512]{1,0:T(8,128)(2,1)S(1)}, bf16[256,512]{1,0:T(8,128)(2,1)S(1)}) custom-call(s32[2]{0:T(128)S(1)} %pad_add_fusion._.place, bf16[256,1024]{1,0:T(8,128)(2,1)S(1)} %fusion.20.g0, bf16[256,1024]{1,0:T(8,128)(2,1)S(1)} %collective-permute-done.30.g1, ...), custom_call_target="tpu_custom_call" | custom-call | flops 1100000 | bytes 1 | tf_op jit(solution)/shard_map/out_proj/pallas_call | solution.py:113
  184.4 6.8 %collective-permute-done.34 = bf16[256,512]{1,0:T(8,128)(2,1)S(1)} collective-permute-done((bf16[256,512]{1,0:T(8,128)(2,1)S(1)}, bf16[256,512]{1,0:T(8,128)(2,1)S(1)}, u32[]{:S(2)}, u32[]{:S(2)}) %collective-permute-start.34) | collective-permute-done | bytes 262176 | tf_op jit(solution)/shard_map/ppermute | solution.py:240
  192.4 5.5 %collective-permute-done.23 = bf16[256,512]{1,0:T(8,128)(2,1)S(1)} collective-permute-done((bf16[256,512]{1,0:T(8,128)(2,1)S(1)}, bf16[256,512]{1,0:T(8,128)(2,1)S(1)}, u32[]{:S(2)}, u32[]{:S(2)}) %collective-permute-start.23) | collective-permute-done | bytes 262176 | tf_op jit(solution)/shard_map/ppermute | solution.py:240
  198.1 4.2 %collective-permute-done.33 = bf16[256,512]{1,0:T(8,128)(2,1)S(1)} collective-permute-done((bf16[256,512]{1,0:T(8,128)(2,1)S(1)}, bf16[256,512]{1,0:T(8,128)(2,1)S(1)}, u32[]{:S(2)}, u32[]{:S(2)}) %collective-permute-start.33) | collective-permute-done | bytes 262176 | tf_op jit(solution)/shard_map/ppermute | solution.py:240
  202.2 5.7 %collective-permute-done.35 = bf16[256,512]{1,0:T(8,128)(2,1)S(1)} collective-permute-done((bf16[256,512]{1,0:T(8,128)(2,1)S(1)}, bf16[256,512]{1,0:T(8,128)(2,1)S(1)}, u32[]{:S(2)}, u32[]{:S(2)}) %collective-permute-start.35) | collective-permute-done | bytes 262176 | tf_op jit(solution)/shard_map/ppermute | solution.py:240
  (213 shorter events, 66.6 us)
Async XLA Ops:
  2.5 16.1 %collective-permute-start.1 = (bf16[256,512]{1,0:T(8,128)(2,1)S(1)}, bf16[256,512]{1,0:T(8,128)(2,1)S(1)}, u32[]{:S(2)}, u32[]{:S(2)}) collective-permute-start(bf16[256,512]{1,0:T(8,128)(2,1)S(1)} %bitcast.56), channel_id=1, source_target_pairs={{0,8},{4,12},{8,0},{12,4},{1,9},{5,13},{9,1},{13,5},{2,10},{6,14},... | collective-permute-start | bytes 786440 | tf_op jit(solution)/shard_map/ppermute | solution.py:240
  6.5 16.0 %collective-permute-start = (bf16[256,512]{1,0:T(8,128)(2,1)S(1)}, bf16[256,512]{1,0:T(8,128)(2,1)S(1)}, u32[]{:S(2)}, u32[]{:S(2)}) collective-permute-start(bf16[256,512]{1,0:T(8,128)(2,1)S(1)} %bitcast.57), channel_id=1, source_target_pairs={{0,4},{4,0},{8,12},{12,8},{1,5},{5,1},{9,13},{13,9},{2,6},{6,2},{1... | collective-permute-start | bytes 786440 | tf_op jit(solution)/shard_map/ppermute | solution.py:240
  18.6 14.4 %collective-permute-start.2 = (bf16[256,512]{1,0:T(8,128)(2,1)S(1)}, bf16[256,512]{1,0:T(8,128)(2,1)S(1)}, u32[]{:S(2)}, u32[]{:S(2)}) collective-permute-start(bf16[256,512]{1,0:T(8,128)(2,1)S(1)} %collective-permute-done.1.refs_2_), channel_id=1, source_target_pairs={{0,4},{4,0},{8,12},{12,8},{1,5},{5,1},{9,13},{13,9},{2,6},{6,2},{1... | collective-permute-start | bytes 786440 | tf_op jit(solution)/shard_map/ppermute | solution.py:240
  19.2 21.9 %collective-permute-start.11 = (bf16[256,512]{1,0:T(8,128)(2,1)}, bf16[256,512]{1,0:T(8,128)(2,1)}, u32[]{:S(2)}, u32[]{:S(2)}) collective-permute-start(bf16[256,512]{1,0:T(8,128)(2,1)} %bitcast.11.refs_0_), channel_id=1, source_target_pairs={{0,8},{4,12},{8,0},{12,4},{1,9},{5,13},{9,1},{13,5},{2,10},{6,14},... | collective-permute-start | bytes 786440 | tf_op jit(solution)/shard_map/ppermute | solution.py:240
  22.6 21.6 %collective-permute-start.10 = (bf16[256,512]{1,0:T(8,128)(2,1)}, bf16[256,512]{1,0:T(8,128)(2,1)}, u32[]{:S(2)}, u32[]{:S(2)}) collective-permute-start(bf16[256,512]{1,0:T(8,128)(2,1)} %bitcast.11.refs_0_), channel_id=1, source_target_pairs={{0,4},{4,0},{8,12},{12,8},{1,5},{5,1},{9,13},{13,9},{2,6},{6,2},{1... | collective-permute-start | bytes 786440 | tf_op jit(solution)/shard_map/ppermute | solution.py:240
  42.6 20.5 %collective-permute-start.4 = (bf16[256,1024]{1,0:T(8,128)(2,1)}, bf16[256,1024]{1,0:T(8,128)(2,1)}, u32[]{:S(2)}, u32[]{:S(2)}) collective-permute-start(bf16[256,1024]{1,0:T(8,128)(2,1)} %fusion.22.refs_5_), channel_id=1, source_target_pairs={{0,2},{1,3},{2,0},{3,1},{4,6},{5,7},{6,4},{7,5},{8,10},{9,11},{10,... | collective-permute-start | bytes 1572872 | tf_op jit(solution)/shard_map/ppermute | solution.py:240
  66.7 14.5 %collective-permute-start.14 = (bf16[256,1024]{1,0:T(8,128)(2,1)}, bf16[256,1024]{1,0:T(8,128)(2,1)}, u32[]{:S(2)}, u32[]{:S(2)}) collective-permute-start(bf16[256,1024]{1,0:T(8,128)(2,1)} %fusion.23._), channel_id=1, source_target_pairs={{0,2},{1,3},{2,0},{3,1},{4,6},{5,7},{6,4},{7,5},{8,10},{9,11},{10,... | collective-permute-start | bytes 1572872 | tf_op jit(solution)/shard_map/ppermute | solution.py:240
  77.1 28.8 %collective-permute-start.16 = (bf16[2,256,1024]{2,1,0:T(8,128)(2,1)S(1)}, bf16[2,256,1024]{2,1,0:T(8,128)(2,1)S(1)}, u32[]{:S(2)}, u32[]{:S(2)}) collective-permute-start(bf16[2,256,1024]{2,1,0:T(8,128)(2,1)S(1)} %in_proj.12.refs_5_), channel_id=1, source_target_pairs={{0,1},{1,0},{2,3},{3,2},{4,5},{5,4},{6,7},{7,6},{8,9},{9,8},{10,11... | collective-permute-start | bytes 3145736 | tf_op jit(solution)/shard_map/ppermute | solution.py:240
  100.7 15.2 %collective-permute-start.26 = (bf16[128,544]{1,0:T(8,128)(2,1)}, bf16[128,544]{1,0:T(8,128)(2,1)}, u32[]{:S(2)}, u32[]{:S(2)}) collective-permute-start(bf16[128,544]{1,0:T(8,128)(2,1)} %fusion.31), channel_id=1, source_target_pairs={{0,8},{4,12},{8,0},{12,4},{1,9},{5,13},{9,1},{13,5},{2,10},{6,14},... | collective-permute-start | bytes 417800 | tf_op jit(solution)/shard_map/ppermute | solution.py:240
  105.3 12.3 %collective-permute-start.8 = (bf16[128,544]{1,0:T(8,128)(2,1)}, bf16[128,544]{1,0:T(8,128)(2,1)}, u32[]{:S(2)}, u32[]{:S(2)}) collective-permute-start(bf16[128,544]{1,0:T(8,128)(2,1)} %fusion.30), channel_id=1, source_target_pairs={{0,8},{4,12},{8,0},{12,4},{1,9},{5,13},{9,1},{13,5},{2,10},{6,14},... | collective-permute-start | bytes 417800 | tf_op jit(solution)/shard_map/ppermute | solution.py:240
  107.0 14.1 %collective-permute-start.17 = (bf16[256,1024]{1,0:T(8,128)(2,1)}, bf16[256,1024]{1,0:T(8,128)(2,1)}, u32[]{:S(2)}, u32[]{:S(2)}) collective-permute-start(bf16[256,1024]{1,0:T(8,128)(2,1)} %fusion.24), channel_id=1, source_target_pairs={{0,2},{1,3},{2,0},{3,1},{4,6},{5,7},{6,4},{7,5},{8,10},{9,11},{10,... | collective-permute-start | bytes 1572872 | tf_op jit(solution)/shard_map/ppermute | solution.py:240
  120.5 24.6 %collective-permute-start.29 = (bf16[256,1024]{1,0:T(8,128)(2,1)S(1)}, bf16[256,1024]{1,0:T(8,128)(2,1)S(1)}, u32[]{:S(2)}, u32[]{:S(2)}) collective-permute-start(bf16[256,1024]{1,0:T(8,128)(2,1)S(1)} %fusion.25), channel_id=1, source_target_pairs={{0,2},{1,3},{2,0},{3,1},{4,6},{5,7},{6,4},{7,5},{8,10},{9,11},{10,... | collective-permute-start | bytes 1572872 | tf_op jit(solution)/shard_map/ppermute | solution.py:240
  133.2 13.8 %collective-permute-start.19 = (bf16[256,1024]{1,0:T(8,128)(2,1)S(1)}, bf16[256,1024]{1,0:T(8,128)(2,1)S(1)}, u32[]{:S(2)}, u32[]{:S(2)}) collective-permute-start(bf16[256,1024]{1,0:T(8,128)(2,1)S(1)} %fusion.21.g0), channel_id=1, source_target_pairs={{0,2},{1,3},{2,0},{3,1},{4,6},{5,7},{6,4},{7,5},{8,10},{9,11},{10,... | collective-permute-start | bytes 1572872 | tf_op jit(solution)/shard_map/ppermute | solution.py:240
  145.5 13.5 %collective-permute-start.31 = (bf16[256,1024]{1,0:T(8,128)(2,1)S(1)}, bf16[256,1024]{1,0:T(8,128)(2,1)S(1)}, u32[]{:S(2)}, u32[]{:S(2)}) collective-permute-start(bf16[256,1024]{1,0:T(8,128)(2,1)S(1)} %fusion.20.g0), channel_id=1, source_target_pairs={{0,2},{1,3},{2,0},{3,1},{4,6},{5,7},{6,4},{7,5},{8,10},{9,11},{10,... | collective-permute-start | bytes 1572872 | tf_op jit(solution)/shard_map/ppermute | solution.py:240
  146.2 12.8 %collective-permute-start.18 = (bf16[256,1024]{1,0:T(8,128)(2,1)S(1)}, bf16[256,1024]{1,0:T(8,128)(2,1)S(1)}, u32[]{:S(2)}, u32[]{:S(2)}) collective-permute-start(bf16[256,1024]{1,0:T(8,128)(2,1)S(1)} %fusion.21.g0), channel_id=1, source_target_pairs={{0,1},{1,0},{2,3},{3,2},{4,5},{5,4},{6,7},{7,6},{8,9},{9,8},{10,11... | collective-permute-start | bytes 1572872 | tf_op jit(solution)/shard_map/ppermute | solution.py:240
  147.0 12.0 %collective-permute-start.20 = (bf16[256,1024]{1,0:T(8,128)(2,1)S(1)}, bf16[256,1024]{1,0:T(8,128)(2,1)S(1)}, u32[]{:S(2)}, u32[]{:S(2)}) collective-permute-start(bf16[256,1024]{1,0:T(8,128)(2,1)S(1)} %collective-permute-done.19.g2), channel_id=1, source_target_pairs={{0,1},{1,0},{2,3},{3,2},{4,5},{5,4},{6,7},{7,6},{8,9},{9,8},{10,11... | collective-permute-start | bytes 1572872 | tf_op jit(solution)/shard_map/ppermute | solution.py:240
  147.0 22.3 %collective-permute-start.30 = (bf16[256,1024]{1,0:T(8,128)(2,1)S(1)}, bf16[256,1024]{1,0:T(8,128)(2,1)S(1)}, u32[]{:S(2)}, u32[]{:S(2)}) collective-permute-start(bf16[256,1024]{1,0:T(8,128)(2,1)S(1)} %fusion.20.g0), channel_id=1, source_target_pairs={{0,1},{1,0},{2,3},{3,2},{4,5},{5,4},{6,7},{7,6},{8,9},{9,8},{10,11... | collective-permute-start | bytes 1572872 | tf_op jit(solution)/shard_map/ppermute | solution.py:240
  159.0 10.3 %collective-permute-start.32 = (bf16[256,1024]{1,0:T(8,128)(2,1)S(1)}, bf16[256,1024]{1,0:T(8,128)(2,1)S(1)}, u32[]{:S(2)}, u32[]{:S(2)}) collective-permute-start(bf16[256,1024]{1,0:T(8,128)(2,1)S(1)} %collective-permute-done.31.g2), channel_id=1, source_target_pairs={{0,1},{1,0},{2,3},{3,2},{4,5},{5,4},{6,7},{7,6},{8,9},{9,8},{10,11... | collective-permute-start | bytes 1572872 | tf_op jit(solution)/shard_map/ppermute | solution.py:240
  166.9 10.3 %collective-permute-start.21 = (bf16[256,512]{1,0:T(8,128)(2,1)S(1)}, bf16[256,512]{1,0:T(8,128)(2,1)S(1)}, u32[]{:S(2)}, u32[]{:S(2)}) collective-permute-start(bf16[256,512]{1,0:T(8,128)(2,1)S(1)} %get-tuple-element.36), channel_id=1, source_target_pairs={{0,4},{4,0},{8,12},{12,8},{1,5},{5,1},{9,13},{13,9},{2,6},{6,2},{1... | collective-permute-start | bytes 786440 | tf_op jit(solution)/shard_map/ppermute | solution.py:240
  169.2 12.8 %collective-permute-start.22 = (bf16[256,512]{1,0:T(8,128)(2,1)S(1)}, bf16[256,512]{1,0:T(8,128)(2,1)S(1)}, u32[]{:S(2)}, u32[]{:S(2)}) collective-permute-start(bf16[256,512]{1,0:T(8,128)(2,1)S(1)} %get-tuple-element.38), channel_id=1, source_target_pairs={{0,4},{4,0},{8,12},{12,8},{1,5},{5,1},{9,13},{13,9},{2,6},{6,2},{1... | collective-permute-start | bytes 786440 | tf_op jit(solution)/shard_map/ppermute | solution.py:240
  177.3 13.9 %collective-permute-start.34 = (bf16[256,512]{1,0:T(8,128)(2,1)S(1)}, bf16[256,512]{1,0:T(8,128)(2,1)S(1)}, u32[]{:S(2)}, u32[]{:S(2)}) collective-permute-start(bf16[256,512]{1,0:T(8,128)(2,1)S(1)} %get-tuple-element.47), channel_id=1, source_target_pairs={{0,4},{4,0},{8,12},{12,8},{1,5},{5,1},{9,13},{13,9},{2,6},{6,2},{1... | collective-permute-start | bytes 786440 | tf_op jit(solution)/shard_map/ppermute | solution.py:240
  182.1 15.9 %collective-permute-start.23 = (bf16[256,512]{1,0:T(8,128)(2,1)S(1)}, bf16[256,512]{1,0:T(8,128)(2,1)S(1)}, u32[]{:S(2)}, u32[]{:S(2)}) collective-permute-start(bf16[256,512]{1,0:T(8,128)(2,1)S(1)} %add_convert_fusion.7), channel_id=1, source_target_pairs={{0,8},{4,12},{8,0},{12,4},{1,9},{5,13},{9,1},{13,5},{2,10},{6,14},... | collective-permute-start | bytes 786440 | tf_op jit(solution)/shard_map/ppermute | solution.py:240
  184.3 17.9 %collective-permute-start.33 = (bf16[256,512]{1,0:T(8,128)(2,1)S(1)}, bf16[256,512]{1,0:T(8,128)(2,1)S(1)}, u32[]{:S(2)}, u32[]{:S(2)}) collective-permute-start(bf16[256,512]{1,0:T(8,128)(2,1)S(1)} %get-tuple-element.44), channel_id=1, source_target_pairs={{0,4},{4,0},{8,12},{12,8},{1,5},{5,1},{9,13},{13,9},{2,6},{6,2},{1... | collective-permute-start | bytes 786440 | tf_op jit(solution)/shard_map/ppermute | solution.py:240
  191.2 16.7 %collective-permute-start.35 = (bf16[256,512]{1,0:T(8,128)(2,1)S(1)}, bf16[256,512]{1,0:T(8,128)(2,1)S(1)}, u32[]{:S(2)}, u32[]{:S(2)}) collective-permute-start(bf16[256,512]{1,0:T(8,128)(2,1)S(1)} %add_convert_fusion.5), channel_id=1, source_target_pairs={{0,8},{4,12},{8,0},{12,4},{1,9},{5,13},{9,1},{13,5},{2,10},{6,14},... | collective-permute-start | bytes 786440 | tf_op jit(solution)/shard_map/ppermute | solution.py:240
  (67 other events, 449.4 us)

commit v4 on v3

--- a/solution.py
+++ b/solution.py
@@ -30,52 +30,51 @@
     return pltpu.CompilerParams(vmem_limit_bytes=mib * 1024 * 1024)
 
 
-def _load_kernel(half, source, _, target, sem):
-    copy = pltpu.make_async_copy(source if half is None else source.at[half], target, sem)
-    copy.start()
-    copy.wait()
-
-
-def load(weight, half, after):
-    return pl.pallas_call(
-        functools.partial(_load_kernel, half),
-        out_shape=jax.ShapeDtypeStruct(weight.shape[-2:], weight.dtype),
-        in_specs=[ANYWHERE] * 2,
-        out_specs=IN_VMEM,
-        scratch_shapes=[pltpu.SemaphoreType.DMA],
-        compiler_params=_params(8),
-        name="load",
-    )(weight, after)
-
-
-def _held_kernel(sibling, place, *refs):
-    *pieces, weight, _, out = refs
+def _in_kernel(half, cores, place, *refs):
+    *refs, held, sems = refs
+    outs = refs[-len(cores) :]
+    *pieces, weight, _ = refs[: -len(cores)]
     depth = pieces[0].shape[1]
-    channels = out.shape[2]
-    core = jnp.bitwise_xor(jnp.bitwise_and(place[1], 1), sibling)
-    for i in range(2):
-        chip = jnp.bitwise_xor(jnp.right_shift(place[1], 1), 1 - i)
-        columns = pl.ds(pl.multiple_of((chip * 2 + core) * channels, channels), channels)
+    channels = outs[0].shape[2]
+    width = held.shape[2]
+    tiles = []
+    for out, sibling in zip(outs, cores):
+        core = jnp.bitwise_xor(jnp.bitwise_and(place[1], 1), sibling)
+        for i in range(2):
+            chip = jnp.bitwise_xor(jnp.right_shift(place[1], 1), 1 - i)
+            for column in range(0, channels, width):
+                first = pl.multiple_of((chip * 2 + core) * channels + column, width)
+                slot = len(tiles)
+                copy = pltpu.make_async_copy(
+                    weight.at[half, :, pl.ds(first, width)], held.at[slot], sems.at[slot]
+                )
+                copy.start()
+                tiles.append((copy, out, i, column))
+    for slot, (copy, out, i, column) in enumerate(tiles):
+        copy.wait()
         total = None
         for k, piece in enumerate(pieces):
-            start = pl.multiple_of(jnp.bitwise_xor(place[0], k) * depth, depth)
-            part = jnp.dot(
-                piece[...], weight[pl.ds(start, depth), columns], preferred_element_type=F32
-            )
+            rows = pl.ds(pl.multiple_of(jnp.bitwise_xor(place[0], k) * depth, depth), depth)
+            part = jnp.dot(piece[...], held[slot, rows, :], preferred_element_type=F32)
             total = part if total is None else total + part
-        out[i] = total.astype(out.dtype)
-
-
-def held_proj(place, pieces, weight, sibling, after):
+        out[i, :, column : column + width] = total.astype(out.dtype)
+
+
+def in_proj(place, pieces, weight, half, cores, after, width=512):
     rows = pieces[0].shape[0]
-    channels = weight.shape[1] // 4
+    channels = weight.shape[2] // 4
+    count = len(cores) * 2 * channels // width
     return pl.pallas_call(
-        functools.partial(_held_kernel, sibling),
-        out_shape=jax.ShapeDtypeStruct((2, rows, channels), BF),
-        in_specs=[SCALARS] + [IN_VMEM] * (len(pieces) + 1) + [ANYWHERE],
-        out_specs=IN_VMEM,
+        functools.partial(_in_kernel, half, cores),
+        out_shape=[jax.ShapeDtypeStruct((2, rows, channels), BF)] * len(cores),
+        in_specs=[SCALARS] + [IN_VMEM] * len(pieces) + [IN_HBM, ANYWHERE],
+        out_specs=[IN_VMEM] * len(cores),
+        scratch_shapes=[
+            pltpu.VMEM((count, weight.shape[1], width), BF),
+            pltpu.SemaphoreType.DMA((count,)),
+        ],
         cost_estimate=_cost(100),
-        compiler_params=_params(8),
+        compiler_params=_params(44),
         name="in_proj",
     )(place, *pieces, weight, after)
 
@@ -280,9 +279,13 @@
     kept, near = {}, {}
 
     def multiply(half, c, pieces, after):
-        away = held_proj(place, pieces, weights[half], 1, after)
-        near[half, c] = _core(away)
-        kept[half, c] = held_proj(place, pieces, weights[half], 0, away)
+        if half in (0,):
+            (away,) = in_proj(place, pieces, in_weight, half, (1,), after)
+            near[half, c] = _core(away)
+            (kept[half, c],) = in_proj(place, pieces, in_weight, half, (0,), away)
+        else:
+            away, kept[half, c] = in_proj(place, pieces, in_weight, half, (1, 0), after)
+            near[half, c] = _core(away)
         return away
 
     def cross(c, half):
@@ -320,11 +323,10 @@
         return mine, both[:, :DT], both[:, DT:].astype(F32)
 
     owns = [normed[:, cut[c], :].reshape(rows, depth) for c in chunks]
-    weights = [load(in_weight, 0, place)]
-    held0 = weights[0]
+    held0 = place
     two = _gx(owns[0], 2)
     one = _gx(owns[0], 1)
-    relay = _order(two, held0)
+    relay = two
     pieces0 = (owns[0], one, two, _gx(relay, 1))
     second = _order(owns[1], relay)
     two = _gx(second, 2)
@@ -338,8 +340,7 @@
     multiply(0, 1, (_order(second, summed0), *pieces1[1:]), summed0)
     summed1, parts = cross(1, 0)
     fin0, low0, b_c0 = reduce(mine, far0)
-    weights.append(load(in_weight, 1, summed1))
-    ag0 = multiply(1, 0, (_order(owns[0], summed1), *pieces0[1:]), weights[1])
+    ag0 = multiply(1, 0, (_order(owns[0], summed1), *pieces0[1:]), summed1)
     kg0 = kept[1, 0]
     left, right, over = parts
     conv1, next1 = convolve(1, (left, right, _order(over, kg0)))

time: 209 us -> 208 us (level)
  waiting for transfers between devices: 72.6 us -> 83.4 us
  other arithmetic: 16.9 us -> 9.62 us
  local copies, waits for them, and re-layouts: 10.9 us -> 5.83 us
    ppermute x36, waiting for transfers between devices: 72.6 us -> 83.4 us  [_swap(): return lax.ppermute(array, axis, [(i, i ^ bits) for i in range(size)])]
    unnamed x110 -> x48, local copies, waits for them, and re-layouts: 7.41 us -> 2.29 us
    convert_element_type x4, other arithmetic: 3.58 us -> 0.38 us  [reduce(): mine = _add(mine, two_away(mine.astype(BF))).astype(BF)]
    convert_element_type x2, other arithmetic: 3.77 us -> 1.61 us  [convolve(): values = _add(*parts).astype(BF).reshape(steps, piece, channels)]
    pallas_call x10 -> x6, Pallas kernels: 37.7 us -> 37.7 us  [in_proj(): pl.pallas_call(functools.partial(_in_kernel, half, cores), out_shape=[jax...]
  transfers between devices with their start and end apart: 36 -> 36, of which waited for: 17 -> 18; matrix products, arithmetic and copies ran while one was open for 8% -> 5% of each run, Pallas kernels for 36% -> 36%
where the time goes in v4:
time: 208 us; the launch traced here: 207 us
  waiting for transfers between devices  83.4 us (40%)
  Pallas kernels  74.3 us (36%)
  starting transfers between devices  31.6 us (15%)
  other arithmetic  9.62 us (5%)
  local copies, waits for them, and re-layouts  5.83 us (3%)
    ppermute x36, waiting for transfers between devices, _swap(): return lax.ppermute(array, axis, [(i, i ^ bits) for i in range(size)])  83.4 us
    pallas_call x6, Pallas kernels, in_proj(): pl.pallas_call(functools.partial(_in_kernel, half, cores), out_shape=[jax...  37.7 us
    ppermute x36, starting transfers between devices, _swap(): return lax.ppermute(array, axis, [(i, i ^ bits) for i in range(size)])  31.6 us
    pallas_call x2, Pallas kernels, ssm(): pl.pallas_call(kernel_fn, out_shape=[jax.ShapeDtypeStruct(state.shape, F3...  20.7 us
    pallas_call x2, Pallas kernels, out_proj(): pl.pallas_call(_out_kernel, out_shape=[jax.ShapeDtypeStruct((rows, width)...  15.9 us
  transfers between devices with their start and end apart: 36, of which 18 were waited for; matrix products, arithmetic and copies ran while one was open for 5% of the time, Pallas kernels for 36%

profile of v4, /device:TPU:0, one launch (start us, length us, event | category | flops | bytes accessed | tf_op | source)
XLA Modules:
  0.0 207.3 jit_solution(13754116250245860913)
XLA Ops:
  2.5 4.0 %collective-permute-start.1 = (bf16[256,512]{1,0:T(8,128)(2,1)S(1)}, bf16[256,512]{1,0:T(8,128)(2,1)S(1)}, u32[]{:S(2)}, u32[]{:S(2)}) collective-permute-start(bf16[256,512]{1,0:T(8,128)(2,1)S(1)} %bitcast.58), channel_id=1, source_target_pairs={{0,8},{4,12},{8,0},{12,4},{1,9},{5,13},{9,1},{13,5},{2,10},{6,14},... | collective-permute-start | bytes 786440 | tf_op jit(solution)/shard_map/ppermute | solution.py:239
  8.1 10.5 %collective-permute-done.1.refs_2_ = bf16[256,512]{1,0:T(8,128)(2,1)S(1)} collective-permute-done((bf16[256,512]{1,0:T(8,128)(2,1)S(1)}, bf16[256,512]{1,0:T(8,128)(2,1)S(1)}, u32[]{:S(2)}, u32[]{:S(2)}) %collective-permute-start.1) | collective-permute-done | bytes 262176 | tf_op jit(solution)/shard_map/ppermute | solution.py:239
  19.3 3.4 %collective-permute-start.11 = (bf16[256,512]{1,0:T(8,128)(2,1)}, bf16[256,512]{1,0:T(8,128)(2,1)}, u32[]{:S(2)}, u32[]{:S(2)}) collective-permute-start(bf16[256,512]{1,0:T(8,128)(2,1)} %bitcast.11.refs_0_), channel_id=1, source_target_pairs={{0,8},{4,12},{8,0},{12,4},{1,9},{5,13},{9,1},{13,5},{2,10},{6,14},... | collective-permute-start | bytes 786440 | tf_op jit(solution)/shard_map/ppermute | solution.py:239
  22.7 10.3 %collective-permute-done.2.refs_3_ = bf16[256,512]{1,0:T(8,128)(2,1)S(1)} collective-permute-done((bf16[256,512]{1,0:T(8,128)(2,1)S(1)}, bf16[256,512]{1,0:T(8,128)(2,1)S(1)}, u32[]{:S(2)}, u32[]{:S(2)}) %collective-permute-start.2) | collective-permute-done | bytes 262176 | tf_op jit(solution)/shard_map/ppermute | solution.py:239
  32.9 5.0 %in_proj.6.refs_5_ = bf16[2,256,1024]{2,1,0:T(8,128)(2,1)S(1)} custom-call(s32[2]{0:T(128)S(1)} %pad_add_fusion.place.refs_5_, bf16[256,512]{1,0:T(8,128)(2,1)S(1)} %bitcast.60, bf16[256,512]{1,0:T(8,128)(2,1)S(1)} %collective-permute-done.refs_1_, bf16[256,512]{1,0:T(8,128)(2,1)S(1)} %collective-permute-done.1.refs_2_, ...), custom_call_target="tpu_custom_call" | custom-call | flops 109999996928 | bytes 1 | tf_op jit(solution)/shard_map/in_proj/pallas_call | solution.py:67
  38.1 5.0 %in_proj.7 = bf16[2,256,1024]{2,1,0:T(8,128)(2,1)S(1)} custom-call(s32[2]{0:T(128)S(1)} %pad_add_fusion.place.refs_5_, bf16[256,512]{1,0:T(8,128)(2,1)S(1)} %bitcast.61, bf16[256,512]{1,0:T(8,128)(2,1)S(1)} %collective-permute-done.refs_1_, bf16[256,512]{1,0:T(8,128)(2,1)S(1)} %collective-permute-done.1.refs_2_, ...), custom_call_target="tpu_custom_call" | custom-call | flops 109999996928 | bytes 1 | tf_op jit(solution)/shard_map/in_proj/pallas_call | solution.py:67
  48.4 5.8 %collective-permute-done.12.refs_3_ = bf16[256,512]{1,0:T(8,128)(2,1)S(1)} collective-permute-done((bf16[256,512]{1,0:T(8,128)(2,1)}, bf16[256,512]{1,0:T(8,128)(2,1)S(1)}, u32[]{:S(2)}, u32[]{:S(2)}) %collective-permute-start.12) | collective-permute-done | bytes 262176 | tf_op jit(solution)/shard_map/ppermute | solution.py:239
  54.1 5.6 %in_proj.8.refs_5_ = bf16[2,256,1024]{2,1,0:T(8,128)(2,1)S(1)} custom-call(s32[2]{0:T(128)S(1)} %pad_add_fusion.place.refs_5_, bf16[256,512]{1,0:T(8,128)(2,1)} %bitcast.11.refs_0_, bf16[256,512]{1,0:T(8,128)(2,1)} %collective-permute-done.10.refs_1_, bf16[256,512]{1,0:T(8,128)(2,1)} %collective-permute-done.11.refs_2_, ...), custom_call_target="tpu_custom_call" | custom-call | flops 109999996928 | bytes 1 | tf_op jit(solution)/shard_map/in_proj/pallas_call | solution.py:67
  59.8 5.7 %in_proj.9 = bf16[2,256,1024]{2,1,0:T(8,128)(2,1)S(1)} custom-call(s32[2]{0:T(128)S(1)} %pad_add_fusion.place.refs_5_, bf16[256,512]{1,0:T(8,128)(2,1)} %bitcast.11.refs_0_, bf16[256,512]{1,0:T(8,128)(2,1)} %collective-permute-done.10.refs_1_, bf16[256,512]{1,0:T(8,128)(2,1)} %collective-permute-done.11.refs_2_, ...), custom_call_target="tpu_custom_call" | custom-call | flops 109999996928 | bytes 1 | tf_op jit(solution)/shard_map/in_proj/pallas_call | solution.py:67
  68.8 7.9 %in_proj.10 = (bf16[2,256,1024]{2,1,0:T(8,128)(2,1)S(1)}, bf16[2,256,1024]{2,1,0:T(8,128)(2,1)S(1)}) custom-call(s32[2]{0:T(128)S(1)} %pad_add_fusion.place.refs_5_, bf16[256,512]{1,0:T(8,128)(2,1)S(1)} %bitcast.62, bf16[256,512]{1,0:T(8,128)(2,1)S(1)} %collective-permute-done.refs_1_, bf16[256,512]{1,0:T(8,128)(2,1)S(1)} %copy-done.8, ...), custom_call_target="tpu_custom_call" | custom-call | flops 109999996928 | bytes 1 | tf_op jit(solution)/shard_map/in_proj/pallas_call | solution.py:67
  76.8 4.6 %collective-permute-done.14 = bf16[256,1024]{1,0:T(8,128)(2,1)S(1)} collective-permute-done((bf16[256,1024]{1,0:T(8,128)(2,1)S(1)}, bf16[256,1024]{1,0:T(8,128)(2,1)S(1)}, u32[]{:S(2)}, u32[]{:S(2)}) %collective-permute-start.14) | collective-permute-done | bytes 524320 | tf_op jit(solution)/shard_map/ppermute | solution.py:239
  88.2 4.6 %collective-permute-done.24 = bf16[128,544]{1,0:T(8,128)(2,1)S(1)} collective-permute-done((bf16[128,544]{1,0:T(8,128)(2,1)S(1)}, bf16[128,544]{1,0:T(8,128)(2,1)S(1)}, u32[]{:S(2)}, u32[]{:S(2)}) %collective-permute-start.24) | collective-permute-done | bytes 139296 | tf_op jit(solution)/shard_map/ppermute | solution.py:239
  96.0 3.0 %collective-permute-done.25 = bf16[128,544]{1,0:T(8,128)(2,1)S(1)} collective-permute-done((bf16[128,544]{1,0:T(8,128)(2,1)S(1)}, bf16[128,544]{1,0:T(8,128)(2,1)S(1)}, u32[]{:S(2)}, u32[]{:S(2)}) %collective-permute-start.25) | collective-permute-done | bytes 139296 | tf_op jit(solution)/shard_map/ppermute | solution.py:239
  100.3 3.2 %collective-permute-done.7 = bf16[128,544]{1,0:T(8,128)(2,1)S(1)} collective-permute-done((bf16[128,544]{1,0:T(8,128)(2,1)S(1)}, bf16[128,544]{1,0:T(8,128)(2,1)S(1)}, u32[]{:S(2)}, u32[]{:S(2)}) %collective-permute-start.7) | collective-permute-done | bytes 139296 | tf_op jit(solution)/shard_map/ppermute | solution.py:239
  106.6 8.5 %in_proj.11 = (bf16[2,256,1024]{2,1,0:T(8,128)(2,1)S(1)}, bf16[2,256,1024]{2,1,0:T(8,128)(2,1)S(1)}) custom-call(s32[2]{0:T(128)S(1)} %pad_add_fusion.place.refs_5_, bf16[256,512]{1,0:T(8,128)(2,1)} %bitcast.11.refs_0_, bf16[256,512]{1,0:T(8,128)(2,1)} %collective-permute-done.10.refs_1_, bf16[256,512]{1,0:T(8,128)(2,1)} %collective-permute-done.11.refs_2_, ...), custom_call_target="tpu_custom_call" | custom-call | flops 109999996928 | bytes 1 | tf_op jit(solution)/shard_map/in_proj/pallas_call | solution.py:67
  120.9 10.5 %ssm.2 = (f32[2048,1024]{1,0:T(8,128)}, f32[256,1024]{1,0:T(8,128)S(1)}) custom-call(bf16[256,512]{1,0:T(8,128)(2,1)S(1)} %fusion.27.refs_0_, f32[256,32]{1,0:T(8,128)S(1)} %fusion.33.refs_1_, bf16[256,1024]{1,0:T(8,128)(2,1)S(1)} %bitcast.57, bf16[512,1024]{1,0:T(8,128)(2,1)S(1)} %copy-done.1, f32[1,1024]{1,0:T(1,128)S(1)} %bitcast.63, ...), custom_call_target="tpu_custom_call" | custom-call | flops 1100000 | bytes 1 | tf_op jit(solution)/shard_map/ssm/pallas_call | solution.py:219
  133.0 10.3 %ssm.3 = (f32[2048,1024]{1,0:T(8,128)}, f32[256,1024]{1,0:T(8,128)S(1)}) custom-call(bf16[256,512]{1,0:T(8,128)(2,1)S(1)} %fusion.26.low, f32[256,32]{1,0:T(8,128)S(1)} %fusion.32.bc, bf16[256,1024]{1,0:T(8,128)(2,1)S(1)} %bitcast.55, bf16[512,1024]{1,0:T(8,128)(2,1)S(1)} %copy-done.1, f32[1,1024]{1,0:T(1,128)S(1)} %bitcast.64, ...), custom_call_target="tpu_custom_call", output_to_operand_aliasing={{0}: (8, {})} | custom-call | flops 1100000 | bytes 1 | tf_op jit(solution)/shard_map/ssm/pallas_call | solution.py:219
  146.1 11.1 %collective-permute-done.31.g2 = bf16[256,1024]{1,0:T(8,128)(2,1)S(1)} collective-permute-done((bf16[256,1024]{1,0:T(8,128)(2,1)S(1)}, bf16[256,1024]{1,0:T(8,128)(2,1)S(1)}, u32[]{:S(2)}, u32[]{:S(2)}) %collective-permute-start.31) | collective-permute-done | bytes 524320 | tf_op jit(solution)/shard_map/ppermute | solution.py:239
  157.2 7.9 %out_proj.2 = (bf16[256,512]{1,0:T(8,128)(2,1)S(1)}, bf16[256,512]{1,0:T(8,128)(2,1)S(1)}, bf16[256,512]{1,0:T(8,128)(2,1)S(1)}, bf16[256,512]{1,0:T(8,128)(2,1)S(1)}) custom-call(s32[2]{0:T(128)S(1)} %pad_add_fusion.place.refs_5_, bf16[256,1024]{1,0:T(8,128)(2,1)S(1)} %fusion.21.g0, bf16[256,1024]{1,0:T(8,128)(2,1)S(1)} %collective-permute-done.18.g1, ...), custom_call_target="tpu_custom_call" | custom-call | flops 1100000 | bytes 1 | tf_op jit(solution)/shard_map/out_proj/pallas_call | solution.py:112
  167.7 7.9 %out_proj.3 = (bf16[256,512]{1,0:T(8,128)(2,1)S(1)}, bf16[256,512]{1,0:T(8,128)(2,1)S(1)}, bf16[256,512]{1,0:T(8,128)(2,1)S(1)}, bf16[256,512]{1,0:T(8,128)(2,1)S(1)}) custom-call(s32[2]{0:T(128)S(1)} %pad_add_fusion.place.refs_5_, bf16[256,1024]{1,0:T(8,128)(2,1)S(1)} %fusion.20.g0, bf16[256,1024]{1,0:T(8,128)(2,1)S(1)} %collective-permute-done.30.g1, ...), custom_call_target="tpu_custom_call" | custom-call | flops 1100000 | bytes 1 | tf_op jit(solution)/shard_map/out_proj/pallas_call | solution.py:112
  182.7 6.8 %collective-permute-done.34 = bf16[256,512]{1,0:T(8,128)(2,1)S(1)} collective-permute-done((bf16[256,512]{1,0:T(8,128)(2,1)S(1)}, bf16[256,512]{1,0:T(8,128)(2,1)S(1)}, u32[]{:S(2)}, u32[]{:S(2)}) %collective-permute-start.34) | collective-permute-done | bytes 262176 | tf_op jit(solution)/shard_map/ppermute | solution.py:239
  190.9 5.5 %collective-permute-done.23 = bf16[256,512]{1,0:T(8,128)(2,1)S(1)} collective-permute-done((bf16[256,512]{1,0:T(8,128)(2,1)S(1)}, bf16[256,512]{1,0:T(8,128)(2,1)S(1)}, u32[]{:S(2)}, u32[]{:S(2)}) %collective-permute-start.23) | collective-permute-done | bytes 262176 | tf_op jit(solution)/shard_map/ppermute | solution.py:239
  196.5 4.0 %collective-permute-done.33 = bf16[256,512]{1,0:T(8,128)(2,1)S(1)} collective-permute-done((bf16[256,512]{1,0:T(8,128)(2,1)S(1)}, bf16[256,512]{1,0:T(8,128)(2,1)S(1)}, u32[]{:S(2)}, u32[]{:S(2)}) %collective-permute-start.33) | collective-permute-done | bytes 262176 | tf_op jit(solution)/shard_map/ppermute | solution.py:239
  200.5 5.8 %collective-permute-done.35 = bf16[256,512]{1,0:T(8,128)(2,1)S(1)} collective-permute-done((bf16[256,512]{1,0:T(8,128)(2,1)S(1)}, bf16[256,512]{1,0:T(8,128)(2,1)S(1)}, u32[]{:S(2)}, u32[]{:S(2)}) %collective-permute-start.35) | collective-permute-done | bytes 262176 | tf_op jit(solution)/shard_map/ppermute | solution.py:239
  (148 shorter events, 49.1 us)
Async XLA Ops:
  2.5 16.1 %collective-permute-start.1 = (bf16[256,512]{1,0:T(8,128)(2,1)S(1)}, bf16[256,512]{1,0:T(8,128)(2,1)S(1)}, u32[]{:S(2)}, u32[]{:S(2)}) collective-permute-start(bf16[256,512]{1,0:T(8,128)(2,1)S(1)} %bitcast.58), channel_id=1, source_target_pairs={{0,8},{4,12},{8,0},{12,4},{1,9},{5,13},{9,1},{13,5},{2,10},{6,14},... | collective-permute-start | bytes 786440 | tf_op jit(solution)/shard_map/ppermute | solution.py:239
  6.6 16.1 %collective-permute-start = (bf16[256,512]{1,0:T(8,128)(2,1)S(1)}, bf16[256,512]{1,0:T(8,128)(2,1)S(1)}, u32[]{:S(2)}, u32[]{:S(2)}) collective-permute-start(bf16[256,512]{1,0:T(8,128)(2,1)S(1)} %bitcast.59), channel_id=1, source_target_pairs={{0,4},{4,0},{8,12},{12,8},{1,5},{5,1},{9,13},{13,9},{2,6},{6,2},{1... | collective-permute-start | bytes 786440 | tf_op jit(solution)/shard_map/ppermute | solution.py:239
  18.6 14.3 %collective-permute-start.2 = (bf16[256,512]{1,0:T(8,128)(2,1)S(1)}, bf16[256,512]{1,0:T(8,128)(2,1)S(1)}, u32[]{:S(2)}, u32[]{:S(2)}) collective-permute-start(bf16[256,512]{1,0:T(8,128)(2,1)S(1)} %collective-permute-done.1.refs_2_), channel_id=1, source_target_pairs={{0,4},{4,0},{8,12},{12,8},{1,5},{5,1},{9,13},{13,9},{2,6},{6,2},{1... | collective-permute-start | bytes 786440 | tf_op jit(solution)/shard_map/ppermute | solution.py:239
  19.3 26.0 %collective-permute-start.11 = (bf16[256,512]{1,0:T(8,128)(2,1)}, bf16[256,512]{1,0:T(8,128)(2,1)}, u32[]{:S(2)}, u32[]{:S(2)}) collective-permute-start(bf16[256,512]{1,0:T(8,128)(2,1)} %bitcast.11.refs_0_), channel_id=1, source_target_pairs={{0,8},{4,12},{8,0},{12,4},{1,9},{5,13},{9,1},{13,5},{2,10},{6,14},... | collective-permute-start | bytes 786440 | tf_op jit(solution)/shard_map/ppermute | solution.py:239
  22.7 25.7 %collective-permute-start.10 = (bf16[256,512]{1,0:T(8,128)(2,1)}, bf16[256,512]{1,0:T(8,128)(2,1)}, u32[]{:S(2)}, u32[]{:S(2)}) collective-permute-start(bf16[256,512]{1,0:T(8,128)(2,1)} %bitcast.11.refs_0_), channel_id=1, source_target_pairs={{0,4},{4,0},{8,12},{12,8},{1,5},{5,1},{9,13},{13,9},{2,6},{6,2},{1... | collective-permute-start | bytes 786440 | tf_op jit(solution)/shard_map/ppermute | solution.py:239
  46.8 18.8 %collective-permute-start.4 = (bf16[256,1024]{1,0:T(8,128)(2,1)}, bf16[256,1024]{1,0:T(8,128)(2,1)}, u32[]{:S(2)}, u32[]{:S(2)}) collective-permute-start(bf16[256,1024]{1,0:T(8,128)(2,1)} %fusion.22.refs_5_), channel_id=1, source_target_pairs={{0,2},{1,3},{2,0},{3,1},{4,6},{5,7},{6,4},{7,5},{8,10},{9,11},{10,... | collective-permute-start | bytes 1572872 | tf_op jit(solution)/shard_map/ppermute | solution.py:239
  67.2 14.3 %collective-permute-start.14 = (bf16[256,1024]{1,0:T(8,128)(2,1)S(1)}, bf16[256,1024]{1,0:T(8,128)(2,1)S(1)}, u32[]{:S(2)}, u32[]{:S(2)}) collective-permute-start(bf16[256,1024]{1,0:T(8,128)(2,1)S(1)} %fusion.23.refs_5_), channel_id=1, source_target_pairs={{0,2},{1,3},{2,0},{3,1},{4,6},{5,7},{6,4},{7,5},{8,10},{9,11},{10,... | collective-permute-start | bytes 1572872 | tf_op jit(solution)/shard_map/ppermute | solution.py:239
  76.7 27.5 %collective-permute-start.16 = (bf16[2,256,1024]{2,1,0:T(8,128)(2,1)S(1)}, bf16[2,256,1024]{2,1,0:T(8,128)(2,1)S(1)}, u32[]{:S(2)}, u32[]{:S(2)}) collective-permute-start(bf16[2,256,1024]{2,1,0:T(8,128)(2,1)S(1)} %get-tuple-element.36), channel_id=1, source_target_pairs={{0,1},{1,0},{2,3},{3,2},{4,5},{5,4},{6,7},{7,6},{8,9},{9,8},{10,11... | collective-permute-start | bytes 3145736 | tf_op jit(solution)/shard_map/ppermute | solution.py:239
  99.1 16.1 %collective-permute-start.26 = (bf16[128,544]{1,0:T(8,128)(2,1)S(1)}, bf16[128,544]{1,0:T(8,128)(2,1)S(1)}, u32[]{:S(2)}, u32[]{:S(2)}) collective-permute-start(bf16[128,544]{1,0:T(8,128)(2,1)S(1)} %fusion.31), channel_id=1, source_target_pairs={{0,8},{4,12},{8,0},{12,4},{1,9},{5,13},{9,1},{13,5},{2,10},{6,14},... | collective-permute-start | bytes 417800 | tf_op jit(solution)/shard_map/ppermute | solution.py:239
  103.7 12.2 %collective-permute-start.8 = (bf16[128,544]{1,0:T(8,128)(2,1)S(1)}, bf16[128,544]{1,0:T(8,128)(2,1)S(1)}, u32[]{:S(2)}, u32[]{:S(2)}) collective-permute-start(bf16[128,544]{1,0:T(8,128)(2,1)S(1)} %fusion.30), channel_id=1, source_target_pairs={{0,8},{4,12},{8,0},{12,4},{1,9},{5,13},{9,1},{13,5},{2,10},{6,14},... | collective-permute-start | bytes 417800 | tf_op jit(solution)/shard_map/ppermute | solution.py:239
  105.1 14.4 %collective-permute-start.17 = (bf16[256,1024]{1,0:T(8,128)(2,1)S(1)}, bf16[256,1024]{1,0:T(8,128)(2,1)}, u32[]{:S(2)}, u32[]{:S(2)}) collective-permute-start(bf16[256,1024]{1,0:T(8,128)(2,1)S(1)} %fusion.24), channel_id=1, source_target_pairs={{0,2},{1,3},{2,0},{3,1},{4,6},{5,7},{6,4},{7,5},{8,10},{9,11},{10,... | collective-permute-start | bytes 1572872 | tf_op jit(solution)/shard_map/ppermute | solution.py:239
  118.7 24.6 %collective-permute-start.29 = (bf16[256,1024]{1,0:T(8,128)(2,1)S(1)}, bf16[256,1024]{1,0:T(8,128)(2,1)S(1)}, u32[]{:S(2)}, u32[]{:S(2)}) collective-permute-start(bf16[256,1024]{1,0:T(8,128)(2,1)S(1)} %fusion.25), channel_id=1, source_target_pairs={{0,2},{1,3},{2,0},{3,1},{4,6},{5,7},{6,4},{7,5},{8,10},{9,11},{10,... | collective-permute-start | bytes 1572872 | tf_op jit(solution)/shard_map/ppermute | solution.py:239
  131.7 13.8 %collective-permute-start.19 = (bf16[256,1024]{1,0:T(8,128)(2,1)S(1)}, bf16[256,1024]{1,0:T(8,128)(2,1)S(1)}, u32[]{:S(2)}, u32[]{:S(2)}) collective-permute-start(bf16[256,1024]{1,0:T(8,128)(2,1)S(1)} %fusion.21.g0), channel_id=1, source_target_pairs={{0,2},{1,3},{2,0},{3,1},{4,6},{5,7},{6,4},{7,5},{8,10},{9,11},{10,... | collective-permute-start | bytes 1572872 | tf_op jit(solution)/shard_map/ppermute | solution.py:239
  143.8 13.5 %collective-permute-start.31 = (bf16[256,1024]{1,0:T(8,128)(2,1)S(1)}, bf16[256,1024]{1,0:T(8,128)(2,1)S(1)}, u32[]{:S(2)}, u32[]{:S(2)}) collective-permute-start(bf16[256,1024]{1,0:T(8,128)(2,1)S(1)} %fusion.20.g0), channel_id=1, source_target_pairs={{0,2},{1,3},{2,0},{3,1},{4,6},{5,7},{6,4},{7,5},{8,10},{9,11},{10,... | collective-permute-start | bytes 1572872 | tf_op jit(solution)/shard_map/ppermute | solution.py:239
  144.6 12.6 %collective-permute-start.18 = (bf16[256,1024]{1,0:T(8,128)(2,1)S(1)}, bf16[256,1024]{1,0:T(8,128)(2,1)S(1)}, u32[]{:S(2)}, u32[]{:S(2)}) collective-permute-start(bf16[256,1024]{1,0:T(8,128)(2,1)S(1)} %fusion.21.g0), channel_id=1, source_target_pairs={{0,1},{1,0},{2,3},{3,2},{4,5},{5,4},{6,7},{7,6},{8,9},{9,8},{10,11... | collective-permute-start | bytes 1572872 | tf_op jit(solution)/shard_map/ppermute | solution.py:239
  145.6 11.7 %collective-permute-start.20 = (bf16[256,1024]{1,0:T(8,128)(2,1)S(1)}, bf16[256,1024]{1,0:T(8,128)(2,1)S(1)}, u32[]{:S(2)}, u32[]{:S(2)}) collective-permute-start(bf16[256,1024]{1,0:T(8,128)(2,1)S(1)} %collective-permute-done.19.g2), channel_id=1, source_target_pairs={{0,1},{1,0},{2,3},{3,2},{4,5},{5,4},{6,7},{7,6},{8,9},{9,8},{10,11... | collective-permute-start | bytes 1572872 | tf_op jit(solution)/shard_map/ppermute | solution.py:239
  145.6 22.2 %collective-permute-start.30 = (bf16[256,1024]{1,0:T(8,128)(2,1)S(1)}, bf16[256,1024]{1,0:T(8,128)(2,1)S(1)}, u32[]{:S(2)}, u32[]{:S(2)}) collective-permute-start(bf16[256,1024]{1,0:T(8,128)(2,1)S(1)} %fusion.20.g0), channel_id=1, source_target_pairs={{0,1},{1,0},{2,3},{3,2},{4,5},{5,4},{6,7},{7,6},{8,9},{9,8},{10,11... | collective-permute-start | bytes 1572872 | tf_op jit(solution)/shard_map/ppermute | solution.py:239
  157.2 10.5 %collective-permute-start.32 = (bf16[256,1024]{1,0:T(8,128)(2,1)S(1)}, bf16[256,1024]{1,0:T(8,128)(2,1)S(1)}, u32[]{:S(2)}, u32[]{:S(2)}) collective-permute-start(bf16[256,1024]{1,0:T(8,128)(2,1)S(1)} %collective-permute-done.31.g2), channel_id=1, source_target_pairs={{0,1},{1,0},{2,3},{3,2},{4,5},{5,4},{6,7},{7,6},{8,9},{9,8},{10,11... | collective-permute-start | bytes 1572872 | tf_op jit(solution)/shard_map/ppermute | solution.py:239
  165.2 10.5 %collective-permute-start.21 = (bf16[256,512]{1,0:T(8,128)(2,1)S(1)}, bf16[256,512]{1,0:T(8,128)(2,1)S(1)}, u32[]{:S(2)}, u32[]{:S(2)}) collective-permute-start(bf16[256,512]{1,0:T(8,128)(2,1)S(1)} %get-tuple-element.40), channel_id=1, source_target_pairs={{0,4},{4,0},{8,12},{12,8},{1,5},{5,1},{9,13},{13,9},{2,6},{6,2},{1... | collective-permute-start | bytes 786440 | tf_op jit(solution)/shard_map/ppermute | solution.py:239
  167.7 12.8 %collective-permute-start.22 = (bf16[256,512]{1,0:T(8,128)(2,1)S(1)}, bf16[256,512]{1,0:T(8,128)(2,1)S(1)}, u32[]{:S(2)}, u32[]{:S(2)}) collective-permute-start(bf16[256,512]{1,0:T(8,128)(2,1)S(1)} %get-tuple-element.42), channel_id=1, source_target_pairs={{0,4},{4,0},{8,12},{12,8},{1,5},{5,1},{9,13},{13,9},{2,6},{6,2},{1... | collective-permute-start | bytes 786440 | tf_op jit(solution)/shard_map/ppermute | solution.py:239
  175.7 13.8 %collective-permute-start.34 = (bf16[256,512]{1,0:T(8,128)(2,1)S(1)}, bf16[256,512]{1,0:T(8,128)(2,1)S(1)}, u32[]{:S(2)}, u32[]{:S(2)}) collective-permute-start(bf16[256,512]{1,0:T(8,128)(2,1)S(1)} %get-tuple-element.53), channel_id=1, source_target_pairs={{0,4},{4,0},{8,12},{12,8},{1,5},{5,1},{9,13},{13,9},{2,6},{6,2},{1... | collective-permute-start | bytes 786440 | tf_op jit(solution)/shard_map/ppermute | solution.py:239
  180.5 15.9 %collective-permute-start.23 = (bf16[256,512]{1,0:T(8,128)(2,1)S(1)}, bf16[256,512]{1,0:T(8,128)(2,1)S(1)}, u32[]{:S(2)}, u32[]{:S(2)}) collective-permute-start(bf16[256,512]{1,0:T(8,128)(2,1)S(1)} %add_convert_fusion.7), channel_id=1, source_target_pairs={{0,8},{4,12},{8,0},{12,4},{1,9},{5,13},{9,1},{13,5},{2,10},{6,14},... | collective-permute-start | bytes 786440 | tf_op jit(solution)/shard_map/ppermute | solution.py:239
  182.6 17.9 %collective-permute-start.33 = (bf16[256,512]{1,0:T(8,128)(2,1)S(1)}, bf16[256,512]{1,0:T(8,128)(2,1)S(1)}, u32[]{:S(2)}, u32[]{:S(2)}) collective-permute-start(bf16[256,512]{1,0:T(8,128)(2,1)S(1)} %get-tuple-element.50), channel_id=1, source_target_pairs={{0,4},{4,0},{8,12},{12,8},{1,5},{5,1},{9,13},{13,9},{2,6},{6,2},{1... | collective-permute-start | bytes 786440 | tf_op jit(solution)/shard_map/ppermute | solution.py:239
  189.5 16.8 %collective-permute-start.35 = (bf16[256,512]{1,0:T(8,128)(2,1)S(1)}, bf16[256,512]{1,0:T(8,128)(2,1)S(1)}, u32[]{:S(2)}, u32[]{:S(2)}) collective-permute-start(bf16[256,512]{1,0:T(8,128)(2,1)S(1)} %add_convert_fusion.5), channel_id=1, source_target_pairs={{0,8},{4,12},{8,0},{12,4},{1,9},{5,13},{9,1},{13,5},{2,10},{6,14},... | collective-permute-start | bytes 786440 | tf_op jit(solution)/shard_map/ppermute | solution.py:239
  (36 other events, 261.9 us)

commit v5 on v4

--- a/solution.py
+++ b/solution.py
@@ -334,7 +334,7 @@
     away0 = multiply(0, 0, pieces0, held0)
     kept0 = kept[0, 0]
     summed0, parts = cross(0, 0)
-    pieces1 = (second, one, two, _gx(_order(two, summed0), 1))
+    pieces1 = (second, one, two, _gx(_order(two, kept0), 1))
     conv0, next0 = convolve(0, parts)
     theirs0, mine, far0 = project(conv0)
     multiply(0, 1, (_order(second, summed0), *pieces1[1:]), summed0)
@@ -382,7 +382,7 @@
     three1, two1, one1, own1 = out_proj(
         place, (gated1, _core(gated1), across1, near1), out_weight
     )
-    three1 = _gx(_order(three1, one0), 1)
+    three1 = _gx(three1, 1)
     one1 = _gx(one1, 1)
     two1 = _gx(_add(two1, three1).astype(BF), 2)
     return (

time: 208 us -> 203 us (0.976)
  waiting for transfers between devices: 83.4 us -> 79.5 us
  starting transfers between devices: 31.6 us -> 29 us
    ppermute x36, waiting for transfers between devices: 83.4 us -> 79.5 us  [_swap(): return lax.ppermute(array, axis, [(i, i ^ bits) for i in range(size)])]
    ppermute x36, starting transfers between devices: 31.6 us -> 29 us  [_swap(): return lax.ppermute(array, axis, [(i, i ^ bits) for i in range(size)])]
  transfers between devices with their start and end apart: 36 -> 36, of which waited for: 18 -> 17; matrix products, arithmetic and copies ran while one was open for 5% -> 7% of each run, Pallas kernels for 36% -> 37%
where the time goes in v5:
time: 203 us
  waiting for transfers between devices  79.5 us (39%)
  Pallas kernels  74.3 us (37%)
  starting transfers between devices  29 us (14%)
  other arithmetic  9.63 us (5%)
  local copies, waits for them, and re-layouts  7.79 us (4%)
    ppermute x36, waiting for transfers between devices, _swap(): return lax.ppermute(array, axis, [(i, i ^ bits) for i in range(size)])  79.5 us
    pallas_call x6, Pallas kernels, in_proj(): pl.pallas_call(functools.partial(_in_kernel, half, cores), out_shape=[jax...  37.7 us
    ppermute x36, starting transfers between devices, _swap(): return lax.ppermute(array, axis, [(i, i ^ bits) for i in range(size)])  29 us
    pallas_call x2, Pallas kernels, ssm(): pl.pallas_call(kernel_fn, out_shape=[jax.ShapeDtypeStruct(state.shape, F3...  20.7 us
    pallas_call x2, Pallas kernels, out_proj(): pl.pallas_call(_out_kernel, out_shape=[jax.ShapeDtypeStruct((rows, width)...  15.9 us
  transfers between devices with their start and end apart: 36, of which 17 were waited for; matrix products, arithmetic and copies ran while one was open for 7% of the time, Pallas kernels for 37%

profile of v5, /device:TPU:0, one launch (start us, length us, event | category | flops | bytes accessed | tf_op | source)
XLA Modules:
  0.0 202.7 jit_solution(457421976683129927)
XLA Ops:
  2.5 4.0 %collective-permute-start.1 = (bf16[256,512]{1,0:T(8,128)(2,1)S(1)}, bf16[256,512]{1,0:T(8,128)(2,1)S(1)}, u32[]{:S(2)}, u32[]{:S(2)}) collective-permute-start(bf16[256,512]{1,0:T(8,128)(2,1)S(1)} %bitcast.58), channel_id=1, source_target_pairs={{0,8},{4,12},{8,0},{12,4},{1,9},{5,13},{9,1},{13,5},{2,10},{6,14},... | collective-permute-start | bytes 786440 | tf_op jit(solution)/shard_map/ppermute | solution.py:239
  9.6 9.0 %collective-permute-done.1.refs_2_ = bf16[256,512]{1,0:T(8,128)(2,1)S(1)} collective-permute-done((bf16[256,512]{1,0:T(8,128)(2,1)S(1)}, bf16[256,512]{1,0:T(8,128)(2,1)S(1)}, u32[]{:S(2)}, u32[]{:S(2)}) %collective-permute-start.1) | collective-permute-done | bytes 262176 | tf_op jit(solution)/shard_map/ppermute | solution.py:239
  21.4 3.4 %collective-permute-start.11 = (bf16[256,512]{1,0:T(8,128)(2,1)}, bf16[256,512]{1,0:T(8,128)(2,1)}, u32[]{:S(2)}, u32[]{:S(2)}) collective-permute-start(bf16[256,512]{1,0:T(8,128)(2,1)} %bitcast.11.refs_0_), channel_id=1, source_target_pairs={{0,8},{4,12},{8,0},{12,4},{1,9},{5,13},{9,1},{13,5},{2,10},{6,14},... | collective-permute-start | bytes 786440 | tf_op jit(solution)/shard_map/ppermute | solution.py:239
  24.8 4.5 %collective-permute-done.2.refs_3_ = bf16[256,512]{1,0:T(8,128)(2,1)S(1)} collective-permute-done((bf16[256,512]{1,0:T(8,128)(2,1)S(1)}, bf16[256,512]{1,0:T(8,128)(2,1)S(1)}, u32[]{:S(2)}, u32[]{:S(2)}) %collective-permute-start.2) | collective-permute-done | bytes 262176 | tf_op jit(solution)/shard_map/ppermute | solution.py:239
  29.3 5.0 %in_proj.6.refs_5_ = bf16[2,256,1024]{2,1,0:T(8,128)(2,1)S(1)} custom-call(s32[2]{0:T(128)S(1)} %pad_add_fusion.place.refs_5_, bf16[256,512]{1,0:T(8,128)(2,1)S(1)} %bitcast.60, bf16[256,512]{1,0:T(8,128)(2,1)S(1)} %collective-permute-done.refs_1_, bf16[256,512]{1,0:T(8,128)(2,1)S(1)} %collective-permute-done.1.refs_2_, ...), custom_call_target="tpu_custom_call" | custom-call | flops 109999996928 | bytes 1 | tf_op jit(solution)/shard_map/in_proj/pallas_call | solution.py:67
  34.4 5.0 %in_proj.7 = bf16[2,256,1024]{2,1,0:T(8,128)(2,1)S(1)} custom-call(s32[2]{0:T(128)S(1)} %pad_add_fusion.place.refs_5_, bf16[256,512]{1,0:T(8,128)(2,1)S(1)} %bitcast.61, bf16[256,512]{1,0:T(8,128)(2,1)S(1)} %collective-permute-done.refs_1_, bf16[256,512]{1,0:T(8,128)(2,1)S(1)} %collective-permute-done.1.refs_2_, ...), custom_call_target="tpu_custom_call" | custom-call | flops 109999996928 | bytes 1 | tf_op jit(solution)/shard_map/in_proj/pallas_call | solution.py:67
  42.1 6.3 %collective-permute-done.12.refs_3_ = bf16[256,512]{1,0:T(8,128)(2,1)S(1)} collective-permute-done((bf16[256,512]{1,0:T(8,128)(2,1)}, bf16[256,512]{1,0:T(8,128)(2,1)S(1)}, u32[]{:S(2)}, u32[]{:S(2)}) %collective-permute-start.12) | collective-permute-done | bytes 262176 | tf_op jit(solution)/shard_map/ppermute | solution.py:239
  48.5 5.6 %in_proj.8.refs_5_ = bf16[2,256,1024]{2,1,0:T(8,128)(2,1)S(1)} custom-call(s32[2]{0:T(128)S(1)} %pad_add_fusion.place.refs_5_, bf16[256,512]{1,0:T(8,128)(2,1)} %bitcast.11.refs_0_, bf16[256,512]{1,0:T(8,128)(2,1)} %collective-permute-done.10.refs_1_, bf16[256,512]{1,0:T(8,128)(2,1)} %collective-permute-done.11.refs_2_, ...), custom_call_target="tpu_custom_call" | custom-call | flops 109999996928 | bytes 1 | tf_op jit(solution)/shard_map/in_proj/pallas_call | solution.py:67
  54.2 5.7 %in_proj.9 = bf16[2,256,1024]{2,1,0:T(8,128)(2,1)S(1)} custom-call(s32[2]{0:T(128)S(1)} %pad_add_fusion.place.refs_5_, bf16[256,512]{1,0:T(8,128)(2,1)} %bitcast.11.refs_0_, bf16[256,512]{1,0:T(8,128)(2,1)} %collective-permute-done.10.refs_1_, bf16[256,512]{1,0:T(8,128)(2,1)} %collective-permute-done.11.refs_2_, ...), custom_call_target="tpu_custom_call" | custom-call | flops 109999996928 | bytes 1 | tf_op jit(solution)/shard_map/in_proj/pallas_call | solution.py:67
  62.1 7.9 %in_proj.10 = (bf16[2,256,1024]{2,1,0:T(8,128)(2,1)S(1)}, bf16[2,256,1024]{2,1,0:T(8,128)(2,1)S(1)}) custom-call(s32[2]{0:T(128)S(1)} %pad_add_fusion.place.refs_5_, bf16[256,512]{1,0:T(8,128)(2,1)S(1)} %bitcast.62, bf16[256,512]{1,0:T(8,128)(2,1)S(1)} %collective-permute-done.refs_1_, bf16[256,512]{1,0:T(8,128)(2,1)S(1)} %copy-done.8, ...), custom_call_target="tpu_custom_call" | custom-call | flops 109999996928 | bytes 1 | tf_op jit(solution)/shard_map/in_proj/pallas_call | solution.py:67
  70.1 5.6 %collective-permute-done.14 = bf16[256,1024]{1,0:T(8,128)(2,1)S(1)} collective-permute-done((bf16[256,1024]{1,0:T(8,128)(2,1)S(1)}, bf16[256,1024]{1,0:T(8,128)(2,1)S(1)}, u32[]{:S(2)}, u32[]{:S(2)}) %collective-permute-start.14) | collective-permute-done | bytes 524320 | tf_op jit(solution)/shard_map/ppermute | solution.py:239
  82.3 4.9 %collective-permute-done.24 = bf16[128,544]{1,0:T(8,128)(2,1)S(1)} collective-permute-done((bf16[128,544]{1,0:T(8,128)(2,1)S(1)}, bf16[128,544]{1,0:T(8,128)(2,1)S(1)}, u32[]{:S(2)}, u32[]{:S(2)}) %collective-permute-start.24) | collective-permute-done | bytes 139296 | tf_op jit(solution)/shard_map/ppermute | solution.py:239
  90.4 3.0 %collective-permute-done.25 = bf16[128,544]{1,0:T(8,128)(2,1)S(1)} collective-permute-done((bf16[128,544]{1,0:T(8,128)(2,1)S(1)}, bf16[128,544]{1,0:T(8,128)(2,1)S(1)}, u32[]{:S(2)}, u32[]{:S(2)}) %collective-permute-start.25) | collective-permute-done | bytes 139296 | tf_op jit(solution)/shard_map/ppermute | solution.py:239
  95.6 2.3 %collective-permute-done.7 = bf16[128,544]{1,0:T(8,128)(2,1)S(1)} collective-permute-done((bf16[128,544]{1,0:T(8,128)(2,1)S(1)}, bf16[128,544]{1,0:T(8,128)(2,1)S(1)}, u32[]{:S(2)}, u32[]{:S(2)}) %collective-permute-start.7) | collective-permute-done | bytes 139296 | tf_op jit(solution)/shard_map/ppermute | solution.py:239
  101.8 8.5 %in_proj.11 = (bf16[2,256,1024]{2,1,0:T(8,128)(2,1)S(1)}, bf16[2,256,1024]{2,1,0:T(8,128)(2,1)S(1)}) custom-call(s32[2]{0:T(128)S(1)} %pad_add_fusion.place.refs_5_, bf16[256,512]{1,0:T(8,128)(2,1)} %bitcast.11.refs_0_, bf16[256,512]{1,0:T(8,128)(2,1)} %collective-permute-done.10.refs_1_, bf16[256,512]{1,0:T(8,128)(2,1)} %collective-permute-done.11.refs_2_, ...), custom_call_target="tpu_custom_call" | custom-call | flops 109999996928 | bytes 1 | tf_op jit(solution)/shard_map/in_proj/pallas_call | solution.py:67
  116.1 10.5 %ssm.2 = (f32[2048,1024]{1,0:T(8,128)}, f32[256,1024]{1,0:T(8,128)S(1)}) custom-call(bf16[256,512]{1,0:T(8,128)(2,1)S(1)} %fusion.27.refs_0_, f32[256,32]{1,0:T(8,128)S(1)} %fusion.33.refs_1_, bf16[256,1024]{1,0:T(8,128)(2,1)S(1)} %bitcast.57, bf16[512,1024]{1,0:T(8,128)(2,1)S(1)} %copy-done.1, f32[1,1024]{1,0:T(1,128)S(1)} %bitcast.63, ...), custom_call_target="tpu_custom_call" | custom-call | flops 1100000 | bytes 1 | tf_op jit(solution)/shard_map/ssm/pallas_call | solution.py:219
  128.2 10.3 %ssm.3 = (f32[2048,1024]{1,0:T(8,128)}, f32[256,1024]{1,0:T(8,128)S(1)}) custom-call(bf16[256,512]{1,0:T(8,128)(2,1)S(1)} %fusion.26.low, f32[256,32]{1,0:T(8,128)S(1)} %fusion.32.bc, bf16[256,1024]{1,0:T(8,128)(2,1)S(1)} %bitcast.55, bf16[512,1024]{1,0:T(8,128)(2,1)S(1)} %copy-done.1, f32[1,1024]{1,0:T(1,128)S(1)} %bitcast.64, ...), custom_call_target="tpu_custom_call", output_to_operand_aliasing={{0}: (8, {})} | custom-call | flops 1100000 | bytes 1 | tf_op jit(solution)/shard_map/ssm/pallas_call | solution.py:219
  141.3 11.1 %collective-permute-done.31.g2 = bf16[256,1024]{1,0:T(8,128)(2,1)S(1)} collective-permute-done((bf16[256,1024]{1,0:T(8,128)(2,1)S(1)}, bf16[256,1024]{1,0:T(8,128)(2,1)S(1)}, u32[]{:S(2)}, u32[]{:S(2)}) %collective-permute-start.31) | collective-permute-done | bytes 524320 | tf_op jit(solution)/shard_map/ppermute | solution.py:239
  152.4 7.9 %out_proj.2 = (bf16[256,512]{1,0:T(8,128)(2,1)S(1)}, bf16[256,512]{1,0:T(8,128)(2,1)S(1)}, bf16[256,512]{1,0:T(8,128)(2,1)S(1)}, bf16[256,512]{1,0:T(8,128)(2,1)S(1)}) custom-call(s32[2]{0:T(128)S(1)} %pad_add_fusion.place.refs_5_, bf16[256,1024]{1,0:T(8,128)(2,1)S(1)} %fusion.21.g0, bf16[256,1024]{1,0:T(8,128)(2,1)S(1)} %collective-permute-done.18.g1, ...), custom_call_target="tpu_custom_call" | custom-call | flops 1100000 | bytes 1 | tf_op jit(solution)/shard_map/out_proj/pallas_call | solution.py:112
  160.4 2.5 %collective-permute-start.22 = (bf16[256,512]{1,0:T(8,128)(2,1)S(1)}, bf16[256,512]{1,0:T(8,128)(2,1)S(1)}, u32[]{:S(2)}, u32[]{:S(2)}) collective-permute-start(bf16[256,512]{1,0:T(8,128)(2,1)S(1)} %get-tuple-element.41), channel_id=1, source_target_pairs={{0,4},{4,0},{8,12},{12,8},{1,5},{5,1},{9,13},{13,9},{2,6},{6,2},{1... | collective-permute-start | bytes 786440 | tf_op jit(solution)/shard_map/ppermute | solution.py:239
  162.9 7.9 %out_proj.3 = (bf16[256,512]{1,0:T(8,128)(2,1)S(1)}, bf16[256,512]{1,0:T(8,128)(2,1)S(1)}, bf16[256,512]{1,0:T(8,128)(2,1)S(1)}, bf16[256,512]{1,0:T(8,128)(2,1)S(1)}) custom-call(s32[2]{0:T(128)S(1)} %pad_add_fusion.place.refs_5_, bf16[256,1024]{1,0:T(8,128)(2,1)S(1)} %fusion.20.g0, bf16[256,1024]{1,0:T(8,128)(2,1)S(1)} %collective-permute-done.30.g1, ...), custom_call_target="tpu_custom_call" | custom-call | flops 1100000 | bytes 1 | tf_op jit(solution)/shard_map/out_proj/pallas_call | solution.py:112
  173.8 11.9 %collective-permute-done.34 = bf16[256,512]{1,0:T(8,128)(2,1)S(1)} collective-permute-done((bf16[256,512]{1,0:T(8,128)(2,1)S(1)}, bf16[256,512]{1,0:T(8,128)(2,1)S(1)}, u32[]{:S(2)}, u32[]{:S(2)}) %collective-permute-start.34) | collective-permute-done | bytes 262176 | tf_op jit(solution)/shard_map/ppermute | solution.py:239
  186.7 10.2 %collective-permute-done.21 = bf16[256,512]{1,0:T(8,128)(2,1)S(1)} collective-permute-done((bf16[256,512]{1,0:T(8,128)(2,1)S(1)}, bf16[256,512]{1,0:T(8,128)(2,1)S(1)}, u32[]{:S(2)}, u32[]{:S(2)}) %collective-permute-start.21) | collective-permute-done | bytes 262176 | tf_op jit(solution)/shard_map/ppermute | solution.py:239
  197.0 4.8 %collective-permute-done.33 = bf16[256,512]{1,0:T(8,128)(2,1)S(1)} collective-permute-done((bf16[256,512]{1,0:T(8,128)(2,1)S(1)}, bf16[256,512]{1,0:T(8,128)(2,1)S(1)}, u32[]{:S(2)}, u32[]{:S(2)}) %collective-permute-start.33) | collective-permute-done | bytes 262176 | tf_op jit(solution)/shard_map/ppermute | solution.py:239
  (144 shorter events, 43.6 us)
Async XLA Ops:
  2.5 16.1 %collective-permute-start.1 = (bf16[256,512]{1,0:T(8,128)(2,1)S(1)}, bf16[256,512]{1,0:T(8,128)(2,1)S(1)}, u32[]{:S(2)}, u32[]{:S(2)}) collective-permute-start(bf16[256,512]{1,0:T(8,128)(2,1)S(1)} %bitcast.58), channel_id=1, source_target_pairs={{0,8},{4,12},{8,0},{12,4},{1,9},{5,13},{9,1},{13,5},{2,10},{6,14},... | collective-permute-start | bytes 786440 | tf_op jit(solution)/shard_map/ppermute | solution.py:239
  6.6 18.2 %collective-permute-start = (bf16[256,512]{1,0:T(8,128)(2,1)S(1)}, bf16[256,512]{1,0:T(8,128)(2,1)S(1)}, u32[]{:S(2)}, u32[]{:S(2)}) collective-permute-start(bf16[256,512]{1,0:T(8,128)(2,1)S(1)} %bitcast.59), channel_id=1, source_target_pairs={{0,4},{4,0},{8,12},{12,8},{1,5},{5,1},{9,13},{13,9},{2,6},{6,2},{1... | collective-permute-start | bytes 786440 | tf_op jit(solution)/shard_map/ppermute | solution.py:239
  18.6 10.7 %collective-permute-start.2 = (bf16[256,512]{1,0:T(8,128)(2,1)S(1)}, bf16[256,512]{1,0:T(8,128)(2,1)S(1)}, u32[]{:S(2)}, u32[]{:S(2)}) collective-permute-start(bf16[256,512]{1,0:T(8,128)(2,1)S(1)} %collective-permute-done.1.refs_2_), channel_id=1, source_target_pairs={{0,4},{4,0},{8,12},{12,8},{1,5},{5,1},{9,13},{13,9},{2,6},{6,2},{1... | collective-permute-start | bytes 786440 | tf_op jit(solution)/shard_map/ppermute | solution.py:239
  21.4 18.1 %collective-permute-start.11 = (bf16[256,512]{1,0:T(8,128)(2,1)}, bf16[256,512]{1,0:T(8,128)(2,1)}, u32[]{:S(2)}, u32[]{:S(2)}) collective-permute-start(bf16[256,512]{1,0:T(8,128)(2,1)} %bitcast.11.refs_0_), channel_id=1, source_target_pairs={{0,8},{4,12},{8,0},{12,4},{1,9},{5,13},{9,1},{13,5},{2,10},{6,14},... | collective-permute-start | bytes 786440 | tf_op jit(solution)/shard_map/ppermute | solution.py:239
  24.8 17.4 %collective-permute-start.10 = (bf16[256,512]{1,0:T(8,128)(2,1)}, bf16[256,512]{1,0:T(8,128)(2,1)}, u32[]{:S(2)}, u32[]{:S(2)}) collective-permute-start(bf16[256,512]{1,0:T(8,128)(2,1)} %bitcast.11.refs_0_), channel_id=1, source_target_pairs={{0,4},{4,0},{8,12},{12,8},{1,5},{5,1},{9,13},{13,9},{2,6},{6,2},{1... | collective-permute-start | bytes 786440 | tf_op jit(solution)/shard_map/ppermute | solution.py:239
  41.6 18.3 %collective-permute-start.4 = (bf16[256,1024]{1,0:T(8,128)(2,1)}, bf16[256,1024]{1,0:T(8,128)(2,1)}, u32[]{:S(2)}, u32[]{:S(2)}) collective-permute-start(bf16[256,1024]{1,0:T(8,128)(2,1)} %fusion.22.refs_5_), channel_id=1, source_target_pairs={{0,2},{1,3},{2,0},{3,1},{4,6},{5,7},{6,4},{7,5},{8,10},{9,11},{10,... | collective-permute-start | bytes 1572872 | tf_op jit(solution)/shard_map/ppermute | solution.py:239
  61.5 14.3 %collective-permute-start.14 = (bf16[256,1024]{1,0:T(8,128)(2,1)S(1)}, bf16[256,1024]{1,0:T(8,128)(2,1)S(1)}, u32[]{:S(2)}, u32[]{:S(2)}) collective-permute-start(bf16[256,1024]{1,0:T(8,128)(2,1)S(1)} %fusion.23.refs_5_), channel_id=1, source_target_pairs={{0,2},{1,3},{2,0},{3,1},{4,6},{5,7},{6,4},{7,5},{8,10},{9,11},{10,... | collective-permute-start | bytes 1572872 | tf_op jit(solution)/shard_map/ppermute | solution.py:239
  70.0 29.4 %collective-permute-start.16 = (bf16[2,256,1024]{2,1,0:T(8,128)(2,1)S(1)}, bf16[2,256,1024]{2,1,0:T(8,128)(2,1)S(1)}, u32[]{:S(2)}, u32[]{:S(2)}) collective-permute-start(bf16[2,256,1024]{2,1,0:T(8,128)(2,1)S(1)} %get-tuple-element.35), channel_id=1, source_target_pairs={{0,1},{1,0},{2,3},{3,2},{4,5},{5,4},{6,7},{7,6},{8,9},{9,8},{10,11... | collective-permute-start | bytes 3145736 | tf_op jit(solution)/shard_map/ppermute | solution.py:239
  93.4 17.0 %collective-permute-start.26 = (bf16[128,544]{1,0:T(8,128)(2,1)S(1)}, bf16[128,544]{1,0:T(8,128)(2,1)S(1)}, u32[]{:S(2)}, u32[]{:S(2)}) collective-permute-start(bf16[128,544]{1,0:T(8,128)(2,1)S(1)} %fusion.31), channel_id=1, source_target_pairs={{0,8},{4,12},{8,0},{12,4},{1,9},{5,13},{9,1},{13,5},{2,10},{6,14},... | collective-permute-start | bytes 417800 | tf_op jit(solution)/shard_map/ppermute | solution.py:239
  98.0 13.1 %collective-permute-start.8 = (bf16[128,544]{1,0:T(8,128)(2,1)S(1)}, bf16[128,544]{1,0:T(8,128)(2,1)S(1)}, u32[]{:S(2)}, u32[]{:S(2)}) collective-permute-start(bf16[128,544]{1,0:T(8,128)(2,1)S(1)} %fusion.30), channel_id=1, source_target_pairs={{0,8},{4,12},{8,0},{12,4},{1,9},{5,13},{9,1},{13,5},{2,10},{6,14},... | collective-permute-start | bytes 417800 | tf_op jit(solution)/shard_map/ppermute | solution.py:239
  100.4 14.4 %collective-permute-start.17 = (bf16[256,1024]{1,0:T(8,128)(2,1)S(1)}, bf16[256,1024]{1,0:T(8,128)(2,1)}, u32[]{:S(2)}, u32[]{:S(2)}) collective-permute-start(bf16[256,1024]{1,0:T(8,128)(2,1)S(1)} %fusion.24), channel_id=1, source_target_pairs={{0,2},{1,3},{2,0},{3,1},{4,6},{5,7},{6,4},{7,5},{8,10},{9,11},{10,... | collective-permute-start | bytes 1572872 | tf_op jit(solution)/shard_map/ppermute | solution.py:239
  113.9 24.6 %collective-permute-start.29 = (bf16[256,1024]{1,0:T(8,128)(2,1)S(1)}, bf16[256,1024]{1,0:T(8,128)(2,1)S(1)}, u32[]{:S(2)}, u32[]{:S(2)}) collective-permute-start(bf16[256,1024]{1,0:T(8,128)(2,1)S(1)} %fusion.25), channel_id=1, source_target_pairs={{0,2},{1,3},{2,0},{3,1},{4,6},{5,7},{6,4},{7,5},{8,10},{9,11},{10,... | collective-permute-start | bytes 1572872 | tf_op jit(solution)/shard_map/ppermute | solution.py:239
  126.9 13.8 %collective-permute-start.19 = (bf16[256,1024]{1,0:T(8,128)(2,1)S(1)}, bf16[256,1024]{1,0:T(8,128)(2,1)S(1)}, u32[]{:S(2)}, u32[]{:S(2)}) collective-permute-start(bf16[256,1024]{1,0:T(8,128)(2,1)S(1)} %fusion.21.g0), channel_id=1, source_target_pairs={{0,2},{1,3},{2,0},{3,1},{4,6},{5,7},{6,4},{7,5},{8,10},{9,11},{10,... | collective-permute-start | bytes 1572872 | tf_op jit(solution)/shard_map/ppermute | solution.py:239
  139.0 13.5 %collective-permute-start.31 = (bf16[256,1024]{1,0:T(8,128)(2,1)S(1)}, bf16[256,1024]{1,0:T(8,128)(2,1)S(1)}, u32[]{:S(2)}, u32[]{:S(2)}) collective-permute-start(bf16[256,1024]{1,0:T(8,128)(2,1)S(1)} %fusion.20.g0), channel_id=1, source_target_pairs={{0,2},{1,3},{2,0},{3,1},{4,6},{5,7},{6,4},{7,5},{8,10},{9,11},{10,... | collective-permute-start | bytes 1572872 | tf_op jit(solution)/shard_map/ppermute | solution.py:239
  139.8 12.6 %collective-permute-start.18 = (bf16[256,1024]{1,0:T(8,128)(2,1)S(1)}, bf16[256,1024]{1,0:T(8,128)(2,1)S(1)}, u32[]{:S(2)}, u32[]{:S(2)}) collective-permute-start(bf16[256,1024]{1,0:T(8,128)(2,1)S(1)} %fusion.21.g0), channel_id=1, source_target_pairs={{0,1},{1,0},{2,3},{3,2},{4,5},{5,4},{6,7},{7,6},{8,9},{9,8},{10,11... | collective-permute-start | bytes 1572872 | tf_op jit(solution)/shard_map/ppermute | solution.py:239
  140.8 11.7 %collective-permute-start.20 = (bf16[256,1024]{1,0:T(8,128)(2,1)S(1)}, bf16[256,1024]{1,0:T(8,128)(2,1)S(1)}, u32[]{:S(2)}, u32[]{:S(2)}) collective-permute-start(bf16[256,1024]{1,0:T(8,128)(2,1)S(1)} %collective-permute-done.19.g2), channel_id=1, source_target_pairs={{0,1},{1,0},{2,3},{3,2},{4,5},{5,4},{6,7},{7,6},{8,9},{9,8},{10,11... | collective-permute-start | bytes 1572872 | tf_op jit(solution)/shard_map/ppermute | solution.py:239
  140.8 22.1 %collective-permute-start.30 = (bf16[256,1024]{1,0:T(8,128)(2,1)S(1)}, bf16[256,1024]{1,0:T(8,128)(2,1)S(1)}, u32[]{:S(2)}, u32[]{:S(2)}) collective-permute-start(bf16[256,1024]{1,0:T(8,128)(2,1)S(1)} %fusion.20.g0), channel_id=1, source_target_pairs={{0,1},{1,0},{2,3},{3,2},{4,5},{5,4},{6,7},{7,6},{8,9},{9,8},{10,11... | collective-permute-start | bytes 1572872 | tf_op jit(solution)/shard_map/ppermute | solution.py:239
  152.4 10.4 %collective-permute-start.32 = (bf16[256,1024]{1,0:T(8,128)(2,1)S(1)}, bf16[256,1024]{1,0:T(8,128)(2,1)S(1)}, u32[]{:S(2)}, u32[]{:S(2)}) collective-permute-start(bf16[256,1024]{1,0:T(8,128)(2,1)S(1)} %collective-permute-done.31.g2), channel_id=1, source_target_pairs={{0,1},{1,0},{2,3},{3,2},{4,5},{5,4},{6,7},{7,6},{8,9},{9,8},{10,11... | collective-permute-start | bytes 1572872 | tf_op jit(solution)/shard_map/ppermute | solution.py:239
  160.4 12.7 %collective-permute-start.22 = (bf16[256,512]{1,0:T(8,128)(2,1)S(1)}, bf16[256,512]{1,0:T(8,128)(2,1)S(1)}, u32[]{:S(2)}, u32[]{:S(2)}) collective-permute-start(bf16[256,512]{1,0:T(8,128)(2,1)S(1)} %get-tuple-element.41), channel_id=1, source_target_pairs={{0,4},{4,0},{8,12},{12,8},{1,5},{5,1},{9,13},{13,9},{2,6},{6,2},{1... | collective-permute-start | bytes 786440 | tf_op jit(solution)/shard_map/ppermute | solution.py:239
  170.8 14.8 %collective-permute-start.34 = (bf16[256,512]{1,0:T(8,128)(2,1)S(1)}, bf16[256,512]{1,0:T(8,128)(2,1)S(1)}, u32[]{:S(2)}, u32[]{:S(2)}) collective-permute-start(bf16[256,512]{1,0:T(8,128)(2,1)S(1)} %get-tuple-element.51), channel_id=1, source_target_pairs={{0,4},{4,0},{8,12},{12,8},{1,5},{5,1},{9,13},{13,9},{2,6},{6,2},{1... | collective-permute-start | bytes 786440 | tf_op jit(solution)/shard_map/ppermute | solution.py:239
  171.0 25.9 %collective-permute-start.21 = (bf16[256,512]{1,0:T(8,128)(2,1)S(1)}, bf16[256,512]{1,0:T(8,128)(2,1)S(1)}, u32[]{:S(2)}, u32[]{:S(2)}) collective-permute-start(bf16[256,512]{1,0:T(8,128)(2,1)S(1)} %get-tuple-element.39), channel_id=1, source_target_pairs={{0,4},{4,0},{8,12},{12,8},{1,5},{5,1},{9,13},{13,9},{2,6},{6,2},{1... | collective-permute-start | bytes 786440 | tf_op jit(solution)/shard_map/ppermute | solution.py:239
  173.1 23.8 %collective-permute-start.23 = (bf16[256,512]{1,0:T(8,128)(2,1)S(1)}, bf16[256,512]{1,0:T(8,128)(2,1)S(1)}, u32[]{:S(2)}, u32[]{:S(2)}) collective-permute-start(bf16[256,512]{1,0:T(8,128)(2,1)S(1)} %add_convert_fusion.7), channel_id=1, source_target_pairs={{0,8},{4,12},{8,0},{12,4},{1,9},{5,13},{9,1},{13,5},{2,10},{6,14},... | collective-permute-start | bytes 786440 | tf_op jit(solution)/shard_map/ppermute | solution.py:239
  173.2 28.6 %collective-permute-start.33 = (bf16[256,512]{1,0:T(8,128)(2,1)S(1)}, bf16[256,512]{1,0:T(8,128)(2,1)S(1)}, u32[]{:S(2)}, u32[]{:S(2)}) collective-permute-start(bf16[256,512]{1,0:T(8,128)(2,1)S(1)} %get-tuple-element.49), channel_id=1, source_target_pairs={{0,4},{4,0},{8,12},{12,8},{1,5},{5,1},{9,13},{13,9},{2,6},{6,2},{1... | collective-permute-start | bytes 786440 | tf_op jit(solution)/shard_map/ppermute | solution.py:239
  185.7 16.1 %collective-permute-start.35 = (bf16[256,512]{1,0:T(8,128)(2,1)S(1)}, bf16[256,512]{1,0:T(8,128)(2,1)S(1)}, u32[]{:S(2)}, u32[]{:S(2)}) collective-permute-start(bf16[256,512]{1,0:T(8,128)(2,1)S(1)} %add_convert_fusion.5), channel_id=1, source_target_pairs={{0,8},{4,12},{8,0},{12,4},{1,9},{5,13},{9,1},{13,5},{2,10},{6,14},... | collective-permute-start | bytes 786440 | tf_op jit(solution)/shard_map/ppermute | solution.py:239
  (34 other events, 245.1 us)
